TPU v7x, 32 devices: a whole 2x2x4 slice. The times are simulated.
32 devices in a mesh: seq: 8 (over y, x, core), tp: 4 (over z).
Axes of the slice: x: 2, y: 2, z: 4, core: 2. Of those that a mesh axis runs over, the one named last changes fastest.
Arguments:
- tokens: bfloat16 [4, 1024, 768], P(None, 'seq'), may hold values from -6 to 6
- norm_gain: float32 [768], replicated, may hold values from 0.5 to 1.5
- norm_bias: float32 [768], replicated, may hold values from -1.75 to 1.75
- in_right: bfloat16 [4, 192, 192], replicated, may hold values from -0.4375 to 0.4375
- in_left: bfloat16 [4, 192, 576], replicated, may hold values from -0.4375 to 0.4375
- short_kernel: bfloat16 [3, 768, 3], replicated, may hold values from -3.5 to 3.5
- filter_first: bfloat16 [5, 128], replicated, may hold values from -12 to 12
- filter_second: bfloat16 [128, 128], replicated, may hold values from -2.5 to 2.5
- filter_third: bfloat16 [128, 768], replicated, may hold values from -0.75 to 0.75
- conv_bias: float32 [768], replicated, may hold values from -6 to 6
- out_right: bfloat16 [4, 192, 192], replicated, may hold values from -0.4375 to 0.4375
- out_left: bfloat16 [4, 192, 192], replicated, may hold values from -0.4375 to 0.4375
- ffn_gain: float32 [768], replicated, may hold values from 0.5 to 1.5
- ffn_bias: float32 [768], replicated, may hold values from -1.75 to 1.75
- gate_weight: bfloat16 [768, 3072], P(None, 'tp'), may hold values from -0.21875 to 0.21875
- up_weight: bfloat16 [768, 3072], P(None, 'tp'), may hold values from -0.21875 to 0.21875
- down_weight: bfloat16 [3072, 768], P('tp'), may hold values from -0.21875 to 0.21875
- cotangent: bfloat16 [4, 1024, 768], P(None, ('seq', 'tp')), may hold values from -6 to 6
Outputs:
- output: bfloat16 [4, 1024, 768], P(None, ('seq', 'tp'))
- grad_tokens: float32 [4, 1024, 768], P(None, 'seq')
- grad_norm_gain: float32 [768], replicated
- grad_norm_bias: float32 [768], replicated
- grad_in_right: float32 [4, 192, 192], replicated
- grad_in_left: float32 [4, 192, 576], replicated
- grad_short_kernel: float32 [3, 768, 3], replicated
- grad_filter_first: float32 [5, 128], replicated
- grad_filter_second: float32 [128, 128], replicated
- grad_filter_third: float32 [128, 768], replicated
- grad_conv_bias: float32 [768], replicated
- grad_out_right: float32 [4, 192, 192], replicated
- grad_out_left: float32 [4, 192, 192], replicated
- grad_ffn_gain: float32 [768], replicated
- grad_ffn_bias: float32 [768], replicated
- grad_gate_weight: float32 [768, 3072], P(None, 'tp')
- grad_up_weight: float32 [768, 3072], P(None, 'tp')
- grad_down_weight: float32 [3072, 768], P('tp')
All inputs are finite; a program needn't handle non-finite values.
Results may differ from a plain program's by a relative error of at most 0.022.
Values may be sent and summed in bfloat16 or wider, within the bound.
A program may use at most 128 MiB of HBM per device.

v0:
```python
import math

import jax
import jax.numpy as jnp
from jax import lax
from jax.sharding import PartitionSpec as P

highest = lax.Precision.HIGHEST


def norm_forward(values, gain, bias):
    centre = jnp.mean(values, axis=-1, keepdims=True)
    shifted = values - centre
    inverse = lax.rsqrt(jnp.mean(shifted * shifted, axis=-1, keepdims=True) + 1e-05)
    scaled = shifted * inverse
    return (scaled * gain + bias, scaled, inverse)


def norm_backward(upstream, scaled, inverse, gain):
    weighted = upstream * gain
    first_mean = jnp.mean(weighted, axis=-1, keepdims=True)
    second_mean = jnp.mean(weighted * scaled, axis=-1, keepdims=True)
    grad_input = inverse * (weighted - first_mean - scaled * second_mean)
    breadth = upstream.shape[-1]
    grad_gain = jnp.sum((upstream * scaled).reshape(-1, breadth), axis=0)
    grad_bias = jnp.sum(upstream.reshape(-1, breadth), axis=0)
    return (grad_input, grad_gain, grad_bias)


def shuffle(blocked):
    row_count, groups, breadth = blocked.shape
    return (
        blocked.reshape(row_count, groups, groups, breadth // groups)
        .transpose(0, 2, 1, 3)
        .reshape(row_count, groups, breadth)
    )


def monarch_forward(operand, right_factor, left_factor):
    row_count = operand.shape[0]
    groups = right_factor.shape[0]
    blocked = operand.reshape(row_count, groups, -1)
    middle = jnp.einsum(
        "tbi,bij->tbj", blocked, right_factor, preferred_element_type=jnp.float32
    ).astype(jnp.bfloat16)
    shuffled = shuffle(middle)
    result = jnp.einsum("tbi,bij->tbj", shuffled, left_factor, preferred_element_type=jnp.float32)
    return (shuffled, result.reshape(row_count, -1))


def monarch_backward(grad_result, operand, shuffled, right_factor, left_factor):
    row_count = operand.shape[0]
    groups = right_factor.shape[0]
    grad_blocked = grad_result.reshape(row_count, groups, -1)
    grad_left = jnp.einsum(
        "tbi,tbj->bij", shuffled, grad_blocked, preferred_element_type=jnp.float32
    )
    grad_shuffled = jnp.einsum(
        "tbj,bij->tbi", grad_blocked, left_factor, preferred_element_type=jnp.float32
    )
    grad_middle = shuffle(grad_shuffled).astype(jnp.bfloat16)
    blocked = operand.reshape(row_count, groups, -1)
    grad_right = jnp.einsum(
        "tbi,tbj->bij", blocked, grad_middle, preferred_element_type=jnp.float32
    )
    grad_operand = jnp.einsum(
        "tbj,bij->tbi", grad_middle, right_factor, preferred_element_type=jnp.float32
    )
    return (grad_operand.reshape(row_count, -1), grad_right, grad_left)


def roots(row_count, col_count, period):
    product = jnp.arange(row_count)[:, None] * jnp.arange(col_count)[None, :] % period
    angle = product.astype(jnp.float32) * (2.0 * math.pi / period)
    return (jnp.cos(angle), jnp.sin(angle))


def complex_step(real_part, imag_part, cos_table, sin_table, sign, form):
    real_out = jnp.einsum(form, real_part, cos_table, precision=highest) - sign * jnp.einsum(
        form, imag_part, sin_table, precision=highest
    )
    imag_out = jnp.einsum(form, imag_part, cos_table, precision=highest) + sign * jnp.einsum(
        form, real_part, sin_table, precision=highest
    )
    return (real_out, imag_out)


def real_step(real_part, cos_table, sin_table, sign, form):
    real_out = jnp.einsum(form, real_part, cos_table, precision=highest)
    imag_out = sign * jnp.einsum(form, real_part, sin_table, precision=highest)
    return (real_out, imag_out)


def twiddle(real_part, imag_part, cos_table, sin_table, sign):
    real_out = real_part * cos_table - sign * imag_part * sin_table
    imag_out = imag_part * cos_table + sign * real_part * sin_table
    return (real_out, imag_out)


def spectrum_of(real_part):
    total = real_part.shape[-1]
    first = math.gcd(total, 128)
    second = total // first
    leading = real_part.shape[:-1]
    real_part = real_part.reshape(leading + (first, second))
    cos_first, sin_first = roots(first, first, first)
    real_part, imag_part = real_step(real_part, cos_first, sin_first, -1.0, "...ab,ak->...kb")
    cos_twist, sin_twist = roots(first, second, total)
    real_part, imag_part = twiddle(real_part, imag_part, cos_twist, sin_twist, -1.0)
    cos_second, sin_second = roots(second, second, second)
    return complex_step(real_part, imag_part, cos_second, sin_second, -1.0, "...kb,bm->...km")


def signal_of(real_part, imag_part):
    first = real_part.shape[-2]
    second = real_part.shape[-1]
    total = first * second
    leading = real_part.shape[:-2]
    cos_second, sin_second = roots(second, second, second)
    real_part, imag_part = complex_step(
        real_part, imag_part, cos_second, sin_second, 1.0, "...kb,bm->...km"
    )
    cos_twist, sin_twist = roots(first, second, total)
    real_part, imag_part = twiddle(real_part, imag_part, cos_twist, sin_twist, 1.0)
    cos_first, sin_first = roots(first, first, first)
    real_part, imag_part = complex_step(
        real_part, imag_part, cos_first, sin_first, 1.0, "...ab,ak->...kb"
    )
    return real_part.reshape(leading + (total,)) / total


def filter_parts(filter_first, filter_second, third_cols, seq_length):
    total = 2 * seq_length
    index = jnp.arange(total)
    offset = jnp.where(index < seq_length, index, index - total).astype(jnp.float32)
    scaled = offset / seq_length
    features = jnp.stack(
        [
            scaled,
            jnp.sin(math.pi * scaled),
            jnp.cos(math.pi * scaled),
            jnp.sin(7.0 * math.pi * scaled),
            jnp.cos(7.0 * math.pi * scaled),
        ],
        axis=1,
    )
    pre_one = jnp.dot(features, filter_first, precision=highest)
    act_one = jnp.sin(pre_one)
    pre_two = jnp.dot(act_one, filter_second, precision=highest)
    act_two = jnp.sin(pre_two)
    tap_mask = (index != seq_length).astype(jnp.float32)[:, None] * seq_length ** (-0.5)
    taps = jnp.dot(act_two, third_cols, precision=highest) * tap_mask
    filt_real, filt_imag = spectrum_of(taps.T)
    return (features, pre_one, act_one, pre_two, act_two, tap_mask, filt_real, filt_imag)


def body(
    tokens,
    norm_gain,
    norm_bias,
    in_right,
    in_left,
    short_kernel,
    filter_first,
    filter_second,
    filter_third,
    conv_bias,
    out_right,
    out_left,
    ffn_gain,
    ffn_bias,
    gate_weight,
    up_weight,
    down_weight,
    cotangent,
):
    seq_count, pos_count, model_width = tokens.shape
    row_count = seq_count * pos_count
    axis_count = lax.axis_size("seq")
    my_index = lax.axis_index("seq")
    chan_count = model_width // axis_count
    seq_length = pos_count * axis_count
    part_rows = cotangent.shape[1]
    tp_index = lax.axis_index("tp")
    tp_count = lax.axis_size("tp")
    chan_start = my_index * chan_count
    mix_count = seq_count // tp_count
    mix_tokens = lax.dynamic_slice_in_dim(tokens, tp_index * mix_count, mix_count, 0)
    mix_rows = mix_count * pos_count
    flat = mix_tokens.reshape(mix_rows, model_width).astype(jnp.float32)
    normed, scaled_one, inverse_one = norm_forward(flat, norm_gain, norm_bias)
    normed_low = normed.astype(jnp.bfloat16)
    shuffled_in, projected = monarch_forward(normed_low, in_right, in_left)
    projected_low = (
        projected.astype(jnp.bfloat16)
        .reshape(mix_count, pos_count, 3, model_width)
        .transpose(2, 3, 0, 1)
    )
    channels = lax.all_to_all(projected_low, "seq", split_axis=1, concat_axis=3, tiled=True)
    signals = channels.astype(jnp.float32)
    kernel = lax.dynamic_slice_in_dim(short_kernel, chan_start, chan_count, 1).astype(jnp.float32)
    tap_zero = kernel[:, :, 0][:, :, None, None]
    tap_one = kernel[:, :, 1][:, :, None, None]
    tap_two = kernel[:, :, 2][:, :, None, None]
    padded = jnp.pad(signals, ((0, 0), (0, 0), (0, 0), (1, 1)))
    shorted = padded[..., :-2] * tap_zero + padded[..., 1:-1] * tap_one + padded[..., 2:] * tap_two
    first_f = filter_first.astype(jnp.float32)
    second_f = filter_second.astype(jnp.float32)
    third_cols = lax.dynamic_slice_in_dim(filter_third, chan_start, chan_count, 1).astype(
        jnp.float32
    )
    kept = filter_parts(first_f, second_f, third_cols, seq_length)
    filt_real = kept[6][:, None]
    filt_imag = kept[7][:, None]
    bias_cols = lax.dynamic_slice_in_dim(conv_bias, chan_start, chan_count, 0)[:, None, None]
    product = shorted[0] * shorted[2]
    product_pad = jnp.pad(product, ((0, 0), (0, 0), (0, seq_length)))
    spec_real, spec_imag = spectrum_of(product_pad)
    conv_real = spec_real * filt_real - spec_imag * filt_imag
    conv_imag = spec_real * filt_imag + spec_imag * filt_real
    convolved = signal_of(conv_real, conv_imag)[..., :seq_length] + bias_cols * product
    mixed_low = (shorted[1] * convolved).astype(jnp.bfloat16)
    back_rows = lax.all_to_all(mixed_low, "seq", split_axis=2, concat_axis=0, tiled=True)
    mixed_rows = back_rows.transpose(1, 2, 0).reshape(mix_rows, model_width)
    shuffled_out, branch = monarch_forward(mixed_rows, out_right, out_left)
    residual_mine = (flat + branch).reshape(mix_count, pos_count, model_width)
    residual = lax.all_gather(residual_mine, "tp", axis=0, tiled=True)
    part_resid = lax.dynamic_slice_in_dim(residual, tp_index * part_rows, part_rows, 1)
    normed_two, scaled_two, inverse_two = norm_forward(part_resid, ffn_gain, ffn_bias)
    normed_rows = lax.all_gather(normed_two.astype(jnp.bfloat16), "tp", axis=1, tiled=True).reshape(
        row_count, model_width
    )
    gate = jnp.dot(normed_rows, gate_weight, preferred_element_type=jnp.float32)
    upward = jnp.dot(normed_rows, up_weight, preferred_element_type=jnp.float32)
    sigma = jax.nn.sigmoid(gate)
    hidden_low = (gate * sigma * upward).astype(jnp.bfloat16)
    partial_down = jnp.dot(hidden_low, down_weight, preferred_element_type=jnp.float32).reshape(
        seq_count, pos_count, model_width
    )
    glu_part = lax.psum_scatter(
        partial_down.astype(jnp.bfloat16), "tp", scatter_dimension=1, tiled=True
    ).astype(jnp.float32)
    output = (part_resid + glu_part).astype(jnp.bfloat16)
    grad_out_rows = lax.all_gather(cotangent, "tp", axis=1, tiled=True).reshape(
        row_count, model_width
    )
    grad_hidden = jnp.dot(grad_out_rows, down_weight.T, preferred_element_type=jnp.float32)
    grad_gate = (grad_hidden * upward * (sigma + gate * sigma * (1.0 - sigma))).astype(jnp.bfloat16)
    grad_up = (grad_hidden * gate * sigma).astype(jnp.bfloat16)
    grad_down_w = jnp.dot(hidden_low.T, grad_out_rows, preferred_element_type=jnp.float32)
    grad_gate_w = jnp.dot(normed_rows.T, grad_gate, preferred_element_type=jnp.float32)
    grad_up_w = jnp.dot(normed_rows.T, grad_up, preferred_element_type=jnp.float32)
    grad_normed = jnp.dot(grad_gate, gate_weight.T, preferred_element_type=jnp.float32) + jnp.dot(
        grad_up, up_weight.T, preferred_element_type=jnp.float32
    )
    grad_normed_part = lax.psum_scatter(
        grad_normed.reshape(seq_count, pos_count, model_width),
        "tp",
        scatter_dimension=1,
        tiled=True,
    )
    grad_in_two, grad_gain_two, grad_bias_two = norm_backward(
        grad_normed_part, scaled_two, inverse_two, ffn_gain
    )
    gain_total = lax.psum((grad_gain_two, grad_bias_two), ("seq", "tp"))
    grad_resid_part = cotangent.astype(jnp.float32) + grad_in_two
    grad_resid = lax.all_gather(
        grad_resid_part.astype(jnp.bfloat16), "tp", axis=1, tiled=True
    ).astype(grad_resid_part.dtype)
    grad_resid_mix = lax.dynamic_slice_in_dim(
        grad_resid, tp_index * mix_count, mix_count, 0
    ).reshape(mix_rows, model_width)
    grad_mixed_rows, grad_out_right, grad_out_left = monarch_backward(
        grad_resid_mix.astype(jnp.bfloat16), mixed_rows, shuffled_out, out_right, out_left
    )
    grad_mixed_low = (
        grad_mixed_rows.astype(jnp.bfloat16)
        .reshape(mix_count, pos_count, model_width)
        .transpose(2, 0, 1)
    )
    grad_mixed = lax.all_to_all(
        grad_mixed_low, "seq", split_axis=0, concat_axis=2, tiled=True
    ).astype(jnp.float32)
    grad_conv = grad_mixed * shorted[1]
    grad_key = grad_mixed * convolved
    again = lax.optimization_barrier((first_f, second_f, third_cols))
    kept = filter_parts(again[0], again[1], again[2], seq_length)
    filt_real = kept[6][:, None]
    filt_imag = kept[7][:, None]
    features, pre_one, act_one, pre_two, act_two, tap_mask = (
        kept[0],
        kept[1],
        kept[2],
        kept[3],
        kept[4],
        kept[5],
    )
    grad_pad = jnp.pad(grad_conv, ((0, 0), (0, 0), (0, seq_length)))
    grad_spec_real, grad_spec_imag = spectrum_of(grad_pad)
    back_real = grad_spec_real * filt_real + grad_spec_imag * filt_imag
    back_imag = grad_spec_imag * filt_real - grad_spec_real * filt_imag
    grad_product = signal_of(back_real, back_imag)[..., :seq_length] + bias_cols * grad_conv
    grad_bias_cols = jnp.sum(grad_conv * product, axis=(1, 2))
    taps_real = jnp.sum(grad_spec_real * spec_real + grad_spec_imag * spec_imag, axis=1)
    taps_imag = jnp.sum(grad_spec_imag * spec_real - grad_spec_real * spec_imag, axis=1)
    grad_taps = signal_of(taps_real, taps_imag)
    grad_pre = grad_taps.T * tap_mask
    grad_third_cols = jnp.dot(act_two.T, grad_pre, precision=highest)
    grad_pre_two = jnp.dot(grad_pre, third_cols.T, precision=highest) * jnp.cos(pre_two)
    grad_second = jnp.dot(act_one.T, grad_pre_two, precision=highest)
    grad_pre_one = jnp.dot(grad_pre_two, second_f.T, precision=highest) * jnp.cos(pre_one)
    grad_first = jnp.dot(features.T, grad_pre_one, precision=highest)
    grad_shorted = jnp.stack([grad_product * shorted[2], grad_key, grad_product * shorted[0]])
    grad_short_pad = jnp.pad(grad_shorted, ((0, 0), (0, 0), (0, 0), (1, 1)))
    grad_signals = (
        grad_short_pad[..., 2:] * tap_zero
        + grad_short_pad[..., 1:-1] * tap_one
        + grad_short_pad[..., :-2] * tap_two
    )
    grad_kernel = jnp.stack(
        [
            jnp.sum(grad_shorted * padded[..., :-2], axis=(2, 3)),
            jnp.sum(grad_shorted * padded[..., 1:-1], axis=(2, 3)),
            jnp.sum(grad_shorted * padded[..., 2:], axis=(2, 3)),
        ],
        axis=-1,
    )
    grad_proj = lax.all_to_all(
        grad_signals.astype(jnp.bfloat16), "seq", split_axis=3, concat_axis=1, tiled=True
    )
    grad_proj_rows = grad_proj.transpose(2, 3, 0, 1).reshape(mix_rows, 3 * model_width)
    grad_normed_one, grad_in_right, grad_in_left = monarch_backward(
        grad_proj_rows, normed_low, shuffled_in, in_right, in_left
    )
    grad_in_one, grad_gain_one, grad_bias_one = norm_backward(
        grad_normed_one, scaled_one, inverse_one, norm_gain
    )
    grad_mine = (grad_resid_mix + grad_in_one).reshape(mix_count, pos_count, model_width)
    short_full = lax.dynamic_update_slice_in_dim(
        jnp.zeros(short_kernel.shape, jnp.float32), grad_kernel, chan_start, 1
    )
    third_full = lax.dynamic_update_slice_in_dim(
        jnp.zeros(filter_third.shape, jnp.float32), grad_third_cols, chan_start, 1
    )
    bias_full = lax.dynamic_update_slice_in_dim(
        jnp.zeros(conv_bias.shape, jnp.float32), grad_bias_cols, chan_start, 0
    )
    mixer_grads = (
        grad_gain_one,
        grad_bias_one,
        grad_in_right,
        grad_in_left,
        short_full,
        grad_first,
        grad_second,
        third_full,
        bias_full,
        grad_out_right,
        grad_out_left,
    )
    grad_tokens = lax.all_gather(grad_mine.astype(jnp.bfloat16), "tp", axis=0, tiled=True).astype(
        grad_mine.dtype
    )
    mixer_grads = (
        lax.psum(mixer_grads[0].astype(jnp.bfloat16), "tp").astype(jnp.float32),
        lax.psum(mixer_grads[1].astype(jnp.bfloat16), "tp").astype(jnp.float32),
        lax.psum(mixer_grads[2].astype(jnp.bfloat16), "tp").astype(jnp.float32),
        lax.psum(mixer_grads[3].astype(jnp.bfloat16), "tp").astype(jnp.float32),
        lax.psum(mixer_grads[4].astype(jnp.bfloat16), "tp").astype(jnp.float32),
        lax.psum(mixer_grads[5].astype(jnp.bfloat16), "tp").astype(jnp.float32),
        lax.psum(mixer_grads[6].astype(jnp.bfloat16), "tp").astype(jnp.float32),
        lax.psum(mixer_grads[7].astype(jnp.bfloat16), "tp").astype(jnp.float32),
        lax.psum(mixer_grads[8].astype(jnp.bfloat16), "tp").astype(jnp.float32),
        lax.psum(mixer_grads[9].astype(jnp.bfloat16), "tp").astype(jnp.float32),
        lax.psum(mixer_grads[10].astype(jnp.bfloat16), "tp").astype(jnp.float32),
    )
    all_total = lax.psum(
        (
            mixer_grads[0],
            mixer_grads[1],
            mixer_grads[2],
            mixer_grads[3],
            mixer_grads[4],
            mixer_grads[5],
            mixer_grads[6],
            mixer_grads[7],
            mixer_grads[8],
            mixer_grads[9],
            mixer_grads[10],
            grad_gate_w,
            grad_up_w,
            grad_down_w,
        ),
        "seq",
    )
    return (
        output,
        grad_tokens,
        all_total[0],
        all_total[1],
        all_total[2],
        all_total[3],
        all_total[4],
        all_total[5],
        all_total[6],
        all_total[7],
        all_total[8],
        all_total[9],
        all_total[10],
        gain_total[0],
        gain_total[1],
        all_total[11],
        all_total[12],
        all_total[13],
    )


def solution(mesh):
    return jax.shard_map(
        body,
        mesh=mesh,
        in_specs=(
            P(None, "seq", None),
            P(),
            P(),
            P(),
            P(),
            P(),
            P(),
            P(),
            P(),
            P(),
            P(),
            P(),
            P(),
            P(),
            P(None, "tp"),
            P(None, "tp"),
            P("tp", None),
            P(None, ("seq", "tp"), None),
        ),
        out_specs=(
            P(None, ("seq", "tp"), None),
            P(None, "seq", None),
            P(),
            P(),
            P(),
            P(),
            P(),
            P(),
            P(),
            P(),
            P(),
            P(),
            P(),
            P(),
            P(),
            P(None, "tp"),
            P(None, "tp"),
            P("tp", None),
        ),
        check_vma=False,
    )
```

profile of v0, /device:TPU:0, one launch (start us, length us, event | category | flops | bytes accessed | tf_op | source)
XLA Modules:
  0.0 679.4 jit_solution(11072885682833746554)
XLA Ops:
  13.5 5.3 all-to-all-start
  20.2 5.0 convolution_sine_fusion.1
  26.2 6.1 fusion.341
  32.3 5.3 fusion.342
  45.1 4.4 convolution_sine_fusion
  65.9 8.0 %multiply_add_fusion = f32[3,96,1,1024]{3,2,1,0:T(1,128)S(1)} fusion(f32[3,96,1,1024]{3,2,1,0:T(1,128)S(1)} %bitcast.379, f32[3,96]{1,0:T(4,128)S(1)} %get-tuple-element.109, f32[3,96]{1,0:T(4,128)S(1)} %get-tuple-element.110, f32[3,96]{1,0:T(4,128)S(1)} %bitcast.432), kind=kLoop, calls=%fused_computation.59 | loop fusion | flops 1474560 | bytes 2362752 | tf_op jit(solution)/shard_map/add | solution.py:206
  97.3 2.7 multiply_convert_fusion.3
  100.0 2.7 copy.283
  106.0 10.2 %all_to_all.54 = bf16[8,2,6144]{2,1,0:T(2,128)(2,1)S(1)} all-to-all(bf16[8,2,6144]{2,1,0:T(2,128)(2,1)S(1)} %reshape.858), channel_id=1, replica_groups=mesh['seq'=8,'tp'=4] {'seq'}, dimensions={0} | all-to-all | bytes 393216 | tf_op jit(solution)/shard_map/all_to_all | solution.py:223
  124.2 27.8 %all_gather.17 = bf16[4,128,768]{2,1,0:T(8,128)(2,1)} all-gather(bf16[4,32,768]{2,1,0:T(8,128)(2,1)} %param.35), channel_id=1, replica_groups=mesh['seq'=8,'tp'=4] {'tp'}, dimensions={1}, use_global_device_ids=true | all-gather | bytes 983040 | tf_op jit(solution)/shard_map/all_gather | solution.py:244
  152.0 16.8 %all-gather.2.cloned.1.call-done = f32[4,128,768]{2,1,0:T(8,128)} async-done(((f32[1,128,768]{2,1,0:T(8,128)}), f32[4,128,768]{2,1,0:T(8,128)}) %all-gather.2.cloned.1.call-update) | async-done | bytes 1572880 | tf_op jit(solution)/shard_map/all_gather | solution.py:227
  172.9 18.0 %all_gather.16 = bf16[4,128,768]{2,1,0:T(8,128)(2,1)S(1)} all-gather(bf16[4,32,768]{2,1,0:T(8,128)(2,1)S(1)} %add_convert_fusion.3), channel_id=1, replica_groups=mesh['seq'=8,'tp'=4] {'tp'}, dimensions={1}, use_global_device_ids=true | all-gather | bytes 983040 | tf_op jit(solution)/shard_map/all_gather | solution.py:230
  199.0 2.8 convolution_convert_fusion.1
  209.8 22.5 %reduce-scatter.5.cloned.1.call-done = f32[4,32,768]{2,1,0:T(8,128)} async-done(((f32[4,128,768]{2,1,0:T(8,128)}), f32[4,32,768]{2,1,0:T(8,128)}) %reduce-scatter.5.cloned.1.call-update) | async-done | bytes 393232 | tf_op jit(solution)/shard_map/reduce_scatter | solution.py:256
  234.3 23.2 %reduce-scatter.3.cloned.1.call-done = bf16[4,32,768]{2,1,0:T(8,128)(2,1)} async-done(((bf16[4,128,768]{2,1,0:T(8,128)(2,1)}), bf16[4,32,768]{2,1,0:T(8,128)(2,1)}) %reduce-scatter.3.cloned.1.call-update) | async-done | bytes 196624 | tf_op jit(solution)/shard_map/reduce_scatter | solution.py:240
  259.4 18.0 %all_gather.18 = bf16[4,128,768]{2,1,0:T(8,128)(2,1)S(1)} all-gather(bf16[4,32,768]{2,1,0:T(8,128)(2,1)S(1)} %get-tuple-element.89), channel_id=1, replica_groups=mesh['seq'=8,'tp'=4] {'tp'}, dimensions={1}, use_global_device_ids=true | all-gather | bytes 983040 | tf_op jit(solution)/shard_map/all_gather | solution.py:267
  284.0 3.7 all-to-all-start.2
  288.7 5.2 all-to-all-done.2
  326.2 13.6 %multiply_reduce_fusion.1 = (bf16[3,96]{1,0:T(4,128)(2,1)}, bf16[3,96]{1,0:T(4,128)(2,1)}, f32[3,96,1,1024]{3,2,1,0:T(1,128)S(1)}) fusion(f32[3,96,1,1024]{3,2,1,0:T(1,128)S(1)} %bitcast.380, f32[1,96,1,1024]{3,2,1,0:T(1,128)S(1)} %bitcast.396, f32[1,96,1,1024]{3,2,1,0:T(1,128)S(1)} %bitcast.398, f32[1,96,1,1024]{3,2,1,0:T(1,128)S(1)} %bitcast.394), kind=kLoop, calls=%fused_computation.57 | loop fusion | flops 1768896 | bytes 3540096 | tf_op jit(solution)/shard_map/reduce_sum | solution.py:322
  339.8 7.3 %add_convert_fusion = bf16[3,96,1,1024]{3,2,1,0:T(2,128)(2,1)S(1)} fusion(f32[3,96,1,1024]{3,2,1,0:T(1,128)S(1)} %get-tuple-element.63, f32[3,96]{1,0:T(4,128)S(1)} %copy-done.85, f32[3,96]{1,0:T(4,128)S(1)} %copy-done.87, f32[3,96]{1,0:T(4,128)S(1)} %bitcast.433), kind=kLoop, calls=%fused_computation.58 | loop fusion | flops 1769472 | bytes 1772928 | tf_op jit(solution)/shard_map/convert_element_type | solution.py:329
  347.2 3.9 copy.313
  351.0 4.4 all-to-all-start.3
  363.0 7.8 %all-to-all-done.3 = bf16[3,96,1,1024]{1,0,2,3:T(4,128)(2,1)} async-done(((bf16[3,96,1,1024]{1,0,2,3:T(4,128)(2,1)}), bf16[3,96,1,1024]{1,0,2,3:T(4,128)(2,1)}, u32[]{:S(2)}, u32[]{:S(2)}) %all-to-all-start.3) | async-done | bytes 589856 | tf_op jit(solution)/shard_map/all_to_all | solution.py:328
  376.9 3.4 fusion.353
  385.4 42.0 %all-reduce.4 = (f32[768]{0:T(1024)}, f32[768]{0:T(1024)}) all-reduce(f32[768]{0:T(1024)S(1)} %copy-done.90, f32[768]{0:T(1024)S(1)} %copy-done.91), channel_id=1, replica_groups=mesh['seq'=8,'tp'=4] {'seq','tp'}, use_global_device_ids=true, to_apply=%region_39.40 | all-reduce | flops 1536 | bytes 12288 | tf_op jit(solution)/shard_map/psum | solution.py:265
  429.2 5.0 convolution_multiply_fusion
  434.2 4.0 convolution_multiply_fusion.1
  443.3 30.3 %all_gather.19 = bf16[4,128,768]{2,1,0:T(8,128)(2,1)S(1)} all-gather(bf16[1,128,768]{2,1,0:T(8,128)(2,1)S(1)} %fusion.36), channel_id=1, replica_groups=mesh['seq'=8,'tp'=4] {'tp'}, dimensions={0}, use_global_device_ids=true | all-gather | bytes 983040 | tf_op jit(solution)/shard_map/all_gather | solution.py:361
  475.0 19.8 %all-reduce.7 = (bf16[768]{0:T(1024)(128)(2,1)S(1)}, bf16[768]{0:T(1024)(128)(2,1)S(1)}, bf16[3,768,3]{1,2,0:T(4,128)(2,1)S(1)}, bf16[5,128]{1,0:T(8,128)(2,1)S(...) all-reduce(bf16[768]{0:T(1024)(128)(2,1)S(1)} %convert_element_type, ...), channel_id=1, replica_groups=mesh['seq'=8,'tp'=4] {'tp'}, use_global_device_ids=true, to_apply=%region_11.12 | all-reduce | flops 26240 | bytes 104960 | tf_op jit(solution)/shard_map/psum | solution.py:365
  494.8 159.0 %all-reduce.16 = (f32[768]{0:T(1024)}, f32[768]{0:T(1024)}, f32[4,192,192]{2,1,0:T(8,128)}, f32[4,192,576]{2,1,0:T(8,128)}, f32[3,768,3]{1,2,0:T(4,128)}, /*inde...) all-reduce(bf16[768]{0:T(1024)(128)(2,1)S(1)} %get-tuple-element.50, ...), channel_id=1, replica_groups=mesh['seq'=8,'tp'=4] {'seq'}, use_global_device_ids=true, to_apply=%region_12.13 | all-reduce | flops 1009280 | bytes 6055680 | tf_op jit(solution)/shard_map/psum | solution.py:377
  653.8 10.8 %all-reduce.13.cloned.1.call-done = (f32[768,768]{1,0:T(8,128)}, f32[768,768]{1,0:T(8,128)}, f32[768,768]{1,0:T(8,128)}) async-done(((f32[768,768]{1,0:T(8,128)}, f32[768,768]{1,0:T(8,128)}, f32[768,768]{1,0:T(8,128)}), (f32[768,768]{1,0:T(8,128)}, f32[768,768]{1,0:T(8,128)}, f32[768,768]{1,0:T(8,128)})) %all-reduce.13.cloned.1.call-update) | async-done | bytes 7077904 | tf_op jit(solution)/shard_map/psum | solution.py:377
  664.7 3.4 copy.430
  (392 shorter events, 161.1 us)
Async XLA Ops:
  7.2 185.9 %copy-start = (bf16[768,768]{1,0:T(8,128)(2,1)S(1)}, bf16[768,768]{1,0:T(8,128)(2,1)}, u32[]{:S(2)}) copy-start(bf16[768,768]{1,0:T(8,128)(2,1)} %param.34) | copy-start | bytes 3538948
  13.5 11.7 %copy-start.62 = (bf16[128,128]{1,0:T(8,128)(2,1)S(1)}, bf16[128,128]{1,0:T(8,128)(2,1)}, u32[]{:S(2)}) copy-start(bf16[128,128]{1,0:T(8,128)(2,1)} %param.25) | copy-start | bytes 98308
  13.5 50.2 %all-to-all-start = ((bf16[3,768,1,128]{3,0,2,1:T(4,128)(2,1)}), bf16[3,768,1,128]{3,0,2,1:T(4,128)(2,1)}, u32[]{:S(2)}, u32[]{:S(2)}) async-start(bf16[3,768,1,128]{3,0,2,1:T(4,128)(2,1)} %bitcast.372), calls=%async_computation | async-start | bytes 1572864 | tf_op jit(solution)/shard_map/all_to_all | solution.py:199
  18.8 149.9 %all-gather.2.cloned.1.call-start = ((), (), s32[]{:S(2)}) async-start(), calls=%async_computation.6 | async-start | bytes 1966080 | tf_op jit(solution)/shard_map/all_gather | solution.py:227
  20.0 29.6 %copy-start.64 = (f32[2048]{0:T(1024)}, f32[2048]{0:T(1024)S(1)}, u32[]{:S(2)}) copy-start(f32[2048]{0:T(1024)S(1)} %fusion.136) | copy-start | bytes 24580
  20.1 32.9 %copy-start.66 = (f32[128,16]{0,1:T(8,128)}, f32[128,16]{0,1:T(8,128)S(1)}, u32[]{:S(2)}) copy-start(f32[128,16]{0,1:T(8,128)S(1)} %get-tuple-element.115) | copy-start | bytes 24580
  20.1 32.9 %copy-start.69 = (f32[128,16]{0,1:T(8,128)}, f32[128,16]{0,1:T(8,128)S(1)}, u32[]{:S(2)}) copy-start(f32[128,16]{0,1:T(8,128)S(1)} %get-tuple-element.116) | copy-start | bytes 24580
  20.2 12.1 %copy-start.53 = (f32[2048,5]{0,1:T(8,128)}, f32[2048,5]{0,1:T(8,128)S(1)}, u32[]{:S(2)}) copy-start(f32[2048,5]{0,1:T(8,128)S(1)} %stack.46) | copy-start | bytes 122884
  65.8 8.1 %copy-start.2 = (f32[3,96,1,8,128]{4,3,2,1,0:T(8,128)}, f32[3,96,1,8,128]{4,3,2,1,0:T(8,128)S(1)}, u32[]{:S(2)}) copy-start(f32[3,96,1,8,128]{4,3,2,1,0:T(8,128)S(1)} %copy.264) | copy-start | bytes 3538948
  124.1 47.7 %copy-start.74 = (f32[768]{0:T(1024)S(1)}, f32[768]{0:T(1024)}, u32[]{:S(2)}) copy-start(f32[768]{0:T(1024)} %param.30) | copy-start | bytes 9220
  124.1 47.7 %copy-start.98 = (f32[768]{0:T(1024)S(1)}, f32[768]{0:T(1024)}, u32[]{:S(2)}) copy-start(f32[768]{0:T(1024)} %param.31) | copy-start | bytes 9220
  124.1 108.2 %reduce-scatter.5.cloned.1.call-start = ((), (), s32[]{:S(2)}) async-start(), calls=%async_computation.8 | async-start | bytes 1966080 | tf_op jit(solution)/shard_map/reduce_scatter | solution.py:256
  168.8 22.2 %copy-start.105 = (bf16[768,768]{1,0:T(8,128)(2,1)S(1)}, bf16[768,768]{1,0:T(8,128)(2,1)}, u32[]{:S(2)}) copy-start(bf16[768,768]{1,0:T(8,128)(2,1)} %param.32) | copy-start | bytes 3538948
  198.7 58.7 %reduce-scatter.3.cloned.1.call-start = ((), (), s32[]{:S(2)}) async-start(), calls=%async_computation.7 | async-start | bytes 983040 | tf_op jit(solution)/shard_map/reduce_scatter | solution.py:240
  207.6 24.7 %copy-start.73 = (f32[4,32]{1,0:T(4,128)S(1)}, f32[4,32]{1,0:T(4,128)}, u32[]{:S(2)}) copy-start(f32[4,32]{1,0:T(4,128)} %copy-done.72) | copy-start | bytes 1540
  207.6 24.7 %copy-start.75 = (f32[768]{0:T(1024)S(1)}, f32[768]{0:T(1024)}, u32[]{:S(2)}) copy-start(f32[768]{0:T(1024)} %param.30) | copy-start | bytes 9220
  207.6 24.7 %copy-start.81 = (f32[4,32]{1,0:T(4,128)S(1)}, f32[4,32]{1,0:T(4,128)}, u32[]{:S(2)}) copy-start(f32[4,32]{1,0:T(4,128)} %copy-done.80) | copy-start | bytes 1540
  207.6 49.9 %copy-start.59 = (bf16[4,32,768]{2,1,0:T(8,128)(2,1)S(1)}, bf16[4,32,768]{2,1,0:T(8,128)(2,1)}, u32[]{:S(2)}) copy-start(bf16[4,32,768]{2,1,0:T(8,128)(2,1)} %param.35) | copy-start | bytes 589828
  284.0 9.9 %all-to-all-start.2 = ((bf16[8,2,6144]{2,1,0:T(2,128)(2,1)}), bf16[8,2,6144]{2,1,0:T(2,128)(2,1)S(1)}, u32[]{:S(2)}, u32[]{:S(2)}) async-start(bf16[8,2,6144]{2,1,0:T(2,128)(2,1)} %reshape.860), calls=%async_computation.4 | async-start | bytes 393216 | tf_op jit(solution)/shard_map/all_to_all | solution.py:281
  296.2 29.9 %copy-start.22 = (f32[96,1,1024]{2,1,0:T(1,128)}, f32[96,1,1024]{2,1,0:T(1,128)S(1)}, u32[]{:S(2)}) copy-start(f32[96,1,1024]{2,1,0:T(1,128)S(1)} %get-tuple-element.95) | copy-start | bytes 1179652
  325.7 14.2 %copy-start.18 = (f32[96,1,1024]{2,1,0:T(1,128)}, f32[96,1,1024]{2,1,0:T(1,128)S(1)}, u32[]{:S(2)}) copy-start(f32[96,1,1024]{2,1,0:T(1,128)S(1)} %get-tuple-element.64) | copy-start | bytes 1179652
  326.1 13.7 %copy-start.20 = (f32[96,1,1024]{2,1,0:T(1,128)}, f32[96,1,1024]{2,1,0:T(1,128)S(1)}, u32[]{:S(2)}) copy-start(f32[96,1,1024]{2,1,0:T(1,128)S(1)} %fusion.44) | copy-start | bytes 1179652
  326.2 13.6 %copy-start.83 = (f32[3,96,1]{1,0,2:T(4,128)S(1)}, f32[3,96,1]{1,0,2:T(4,128)}, u32[]{:S(2)}) copy-start(f32[3,96,1]{1,0,2:T(4,128)} %copy-done.82) | copy-start | bytes 3460
  326.2 13.6 %copy-start.85 = (f32[3,96]{1,0:T(4,128)S(1)}, f32[3,96]{1,0:T(4,128)}, u32[]{:S(2)}) copy-start(f32[3,96]{1,0:T(4,128)} %copy-done.84) | copy-start | bytes 3460
  326.2 13.6 %copy-start.87 = (f32[3,96]{1,0:T(4,128)S(1)}, f32[3,96]{1,0:T(4,128)}, u32[]{:S(2)}) copy-start(f32[3,96]{1,0:T(4,128)} %copy-done.86) | copy-start | bytes 3460
  351.0 19.8 %all-to-all-start.3 = ((bf16[3,96,1,1024]{1,0,2,3:T(4,128)(2,1)}), bf16[3,96,1,1024]{1,0,2,3:T(4,128)(2,1)}, u32[]{:S(2)}, u32[]{:S(2)}) async-start(bf16[3,96,1,1024]{1,0,2,3:T(4,128)(2,1)} %copy.313), calls=%async_computation.5 | async-start | bytes 2097152 | tf_op jit(solution)/shard_map/all_to_all | solution.py:328
  355.4 139.4 %all-reduce.15.cloned.1.call-start = ((), (), s32[]{:S(2)}) async-start(), calls=%async_computation.10 | async-start | bytes 4718592 | tf_op jit(solution)/shard_map/psum | solution.py:367
  363.0 11.1 %copy-start.55 = (bf16[128,768]{1,0:T(8,128)(2,1)}, bf16[128,768]{1,0:T(8,128)(2,1)S(1)}, u32[]{:S(2)}) copy-start(bf16[128,768]{1,0:T(8,128)(2,1)S(1)} %dynamic_update_slice.10) | copy-start | bytes 589828
  376.8 287.9 %all-reduce.13.cloned.1.call-start = ((), (), s32[]{:S(2)}) async-start(), calls=%async_computation.9 | async-start | bytes 14155776 | tf_op jit(solution)/shard_map/psum | solution.py:377
  384.7 42.7 %copy-start.21 = (f32[96,1,1024]{2,1,0:T(1,128)S(1)}, f32[96,1,1024]{2,1,0:T(1,128)}, u32[]{:S(2)}) copy-start(f32[96,1,1024]{2,1,0:T(1,128)} %copy-done.20) | copy-start | bytes 1179652
  384.7 42.8 %copy-start.23 = (f32[96,1,1024]{2,1,0:T(1,128)S(1)}, f32[96,1,1024]{2,1,0:T(1,128)}, u32[]{:S(2)}) copy-start(f32[96,1,1024]{2,1,0:T(1,128)} %copy-done.22) | copy-start | bytes 1179652
  384.7 42.8 %copy-start.19 = (f32[96,1,1024]{2,1,0:T(1,128)S(1)}, f32[96,1,1024]{2,1,0:T(1,128)}, u32[]{:S(2)}) copy-start(f32[96,1,1024]{2,1,0:T(1,128)} %copy-done.18) | copy-start | bytes 1179652
  (82 other events, 181.8 us)
Sparse Core Ops, SparseCore 0:
  124.2 44.5 all-gather.1
  198.9 33.3 reduce-scatter.4
  235.2 22.2 reduce-scatter.2
  376.9 109.1 all-reduce.14
  490.7 173.9 all-reduce.12
where the time goes:
time: 684 us; the launch traced here: 679 us
  blocking collectives  325 us (48%)
  matrix products  122 us (18%)
  waiting for transfers between devices  86.5 us (13%)
  local copies, waits for them, and re-layouts  58 us (8%)
  other arithmetic  57.5 us (8%)
  between operations  15.8 us (2%)
  starting transfers between devices  14.4 us (2%)
    psum x1, blocking collectives, body(): lax.psum((mixer_grads[0], mixer_grads[1], mixer_grads[2], mixer_grads[3],...  159 us
    psum x1, blocking collectives, body(): gain_total = lax.psum((grad_gain_two, grad_bias_two), ('seq', 'tp'))  42 us
    all_gather x1, blocking collectives, body(): lax.all_gather(grad_mine.astype(jnp.bfloat16), 'tp', axis=0, tiled=True)  30.3 us
    all_gather x1, blocking collectives, body(): lax.all_gather(cotangent, 'tp', axis=1, tiled=True)  27.8 us
    unnamed x227, local copies, waits for them, and re-layouts  24.1 us
    reduce_scatter x1, waiting for transfers between devices, body(): lax.psum_scatter(partial_down.astype(jnp.bfloat16), 'tp', scatter_dimensi...  23.2 us
    reduce_scatter x1, waiting for transfers between devices, body(): lax.psum_scatter(grad_normed.reshape(seq_count, pos_count, model_width),...  22.5 us
    psum x1, blocking collectives, body(): lax.psum(mixer_grads[0].astype(jnp.bfloat16), 'tp').astype(jnp.float32)  19.8 us
  transfers between devices with their start and end apart: 8, of which 6 were waited for; matrix products, arithmetic and copies ran while one was open for 13% of the time, Pallas kernels for 0%

commit v1 on v0

--- a/solution.py
+++ b/solution.py
@@ -1,9 +1,403 @@
+import functools
 import math
 
+import numpy as np
 import jax
 import jax.numpy as jnp
 from jax import lax
+from jax.experimental import pallas as pl
+from jax.experimental.pallas import tpu as pltpu
 from jax.sharding import PartitionSpec as P
+
+BF = jnp.bfloat16
+F32 = jnp.float32
+MESH = pl.DeviceIdType.MESH
+NN = ((1,), (0,))
+NT = ((1,), (1,))
+TN = ((0,), (0,))
+LIMIT = 56 * 1024 * 1024
+
+
+def dot(first, second, form=NN):
+    return lax.dot_general(first, second, (form, ((), ())), preferred_element_type=F32)
+
+
+def any_spec():
+    return pl.BlockSpec(memory_space=pl.ANY)
+
+
+def vmem_spec():
+    return pl.BlockSpec(memory_space=pltpu.VMEM)
+
+
+def sin_cos(value):
+    turns = jnp.floor(value * (1.0 / math.pi) + 0.5)
+    rest = value - turns * 3.140625
+    rest = rest - turns * 9.67502593994140625e-4
+    rest = rest - turns * 1.509957990978376432e-7
+    half = turns * 0.5
+    sign = 1.0 - 4.0 * (half - jnp.floor(half))
+    square = rest * rest
+    sine = 1.0 / 362880 - square * (1.0 / 39916800)
+    sine = -1.0 / 5040 + square * sine
+    sine = 1.0 / 120 + square * sine
+    sine = -1.0 / 6 + square * sine
+    sine = rest + rest * square * sine
+    cosine = 1.0 / 40320 - square * (1.0 / 3628800 - square * (1.0 / 479001600))
+    cosine = -1.0 / 720 + square * cosine
+    cosine = 1.0 / 24 + square * cosine
+    cosine = -0.5 + square * cosine
+    cosine = 1.0 + square * cosine
+    return sign * sine, sign * cosine
+
+
+def flip(index, bits):
+    result = 0
+    for place in range(3):
+        digit = lax.rem(index // (1 << place), 2)
+        if (bits >> place) & 1:
+            digit = 1 - digit
+        result = result + digit * (1 << place)
+    return result
+
+
+def greet(n_seq, n_tp):
+    me, plane = lax.axis_index("seq"), lax.axis_index("tp")
+    barrier = pltpu.get_barrier_semaphore()
+    for k in range(1, n_seq):
+        pl.semaphore_signal(barrier, inc=1, device_id={"seq": flip(me, k)}, device_id_type=MESH)
+    for k in range(1, n_tp):
+        pl.semaphore_signal(barrier, inc=1, device_id={"tp": flip(plane, k)}, device_id_type=MESH)
+    return lambda: pl.semaphore_wait(barrier, n_seq + n_tp - 2)
+
+
+def sign_rows(count, width):
+    row = lax.broadcasted_iota(jnp.int32, (count, width), 0)
+    return (1 - 2 * lax.rem(row, 2)).astype(F32)
+
+
+def sign_lanes(count, width):
+    lane = lax.broadcasted_iota(jnp.int32, (count, width), 1)
+    return (1 - 2 * lax.rem(lane, 2)).astype(F32)
+
+
+def previous(values):
+    lane = lax.broadcasted_iota(jnp.int32, values.shape, 1)
+    return jnp.where(lane == 0, 0.0, pltpu.roll(values, 1, 1))
+
+
+def following(values):
+    last = values.shape[1] - 1
+    lane = lax.broadcasted_iota(jnp.int32, values.shape, 1)
+    return jnp.where(lane == last, 0.0, pltpu.roll(values, last, 1))
+
+
+def monarch_forward(load, right, left, shuffled, store):
+    groups, width, _ = right.shape
+    part = width // groups
+    for b in range(groups):
+        middle = dot(right[b], load(b), TN).astype(BF)
+        for g in range(groups):
+            shuffled[pl.ds(g * width + b * part, part), :] = middle[g * part : (g + 1) * part]
+    for g in range(groups):
+        store(g, dot(left[g], shuffled[pl.ds(g * width, width), :], TN))
+
+
+SEQ_ORDER = (6, 7, 2, 3, 4, 5, 1)
+
+
+def front_kernel(n_seq, n_tp, dims, *refs):
+    (tokens, cotangent, table, vectors, right, left, columns, features, first, second, third) = refs[:11]
+    (mixed_out, signals_out, conv_out, wave_out, taps_out, nyquist_out, acts_out, normed_out, shuffled_out, cot_out) = refs[11:21]
+    (token_v, table_v, normed, shuffled, projected, signals, acts, spread, taps_v, padded, product, keyed, wave, spectrum, conv,
+     mixed, mixed_rows, nyquist, totals, local_sems, seq_send, seq_recv, back_send, back_recv, tp_send, tp_recv) = refs[21:]
+    width, chans, length, rows = dims
+    me, plane = lax.axis_index("seq"), lax.axis_index("tp")
+    entered = greet(n_seq, n_tp)
+    token_load = pltpu.make_async_copy(tokens.at[plane], token_v, local_sems.at[0])
+    token_load.start()
+    table_load = pltpu.make_async_copy(table, table_v, local_sems.at[1])
+    table_load.start()
+    token_load.wait()
+    value = token_v[...].astype(F32)
+    shifted = value - jnp.mean(value, axis=-1, keepdims=True)
+    inverse = lax.rsqrt(jnp.mean(shifted * shifted, axis=-1, keepdims=True) + 1e-05)
+    value = shifted * inverse * vectors[0:1, :] + vectors[1:2, :]
+    normed[...] = value.T.astype(BF)
+    groups = right.shape[0]
+    block = width // groups
+    fan = left.shape[2]
+
+    def keep(g, result):
+        projected[pl.ds(g * fan, fan), :] = result.astype(BF)
+
+    monarch_forward(lambda b: normed[pl.ds(b * block, block), :], right, left, shuffled, keep)
+    entered()
+    sends = []
+    mine = pl.ds(pl.multiple_of(me * rows, rows), rows)
+    for k in SEQ_ORDER:
+        other = flip(me, k)
+        for s in range(3):
+            copy = pltpu.make_async_remote_copy(
+                src_ref=projected.at[pl.ds(pl.multiple_of(s * width + other * chans, 16), chans), :],
+                dst_ref=signals.at[s, :, mine],
+                send_sem=seq_send.at[k, s],
+                recv_sem=seq_recv.at[k, s],
+                device_id={"seq": other},
+                device_id_type=MESH,
+            )
+            copy.start()
+            sends.append(copy)
+    for s in range(3):
+        signals[s, :, mine] = projected[pl.ds(pl.multiple_of(s * width + me * chans, 16), chans), :]
+    part = rows // n_tp
+    spot = pl.ds(pl.multiple_of(plane * part, part), part)
+    cot_copies = []
+    for k in range(1, n_tp):
+        copy = pltpu.make_async_remote_copy(
+            src_ref=cotangent,
+            dst_ref=cot_out.at[:, spot, :],
+            send_sem=tp_send.at[k],
+            recv_sem=tp_recv.at[k],
+            device_id={"tp": flip(plane, k)},
+            device_id_type=MESH,
+        )
+        copy.start()
+        cot_copies.append(copy)
+    own_cot = pltpu.make_async_copy(cotangent, cot_out.at[:, spot, :], local_sems.at[2])
+    own_cot.start()
+    out_copies = [
+        pltpu.make_async_copy(normed, normed_out, local_sems.at[3]),
+        pltpu.make_async_copy(shuffled, shuffled_out, local_sems.at[4]),
+    ]
+    for copy in out_copies:
+        copy.start()
+
+    chunk = 256
+    per = length // chunk
+    totals[...] = jnp.zeros_like(totals)
+    for half in range(2):
+
+        def tap_step(at, carry, half=half):
+            row = pl.multiple_of(half * length + at * chunk, chunk)
+            here = pl.ds(row, chunk)
+            sine, cosine = sin_cos(dot(features[here, :], first[...]))
+            high = sine.astype(BF)
+            acts[0, here, :] = high
+            acts[1, here, :] = cosine.astype(BF)
+            low = (sine - high.astype(F32)).astype(BF)
+            sine, cosine = sin_cos(dot(high, second[...]) + dot(low, second[...]))
+            high = sine.astype(BF)
+            acts[2, here, :] = high
+            acts[3, here, :] = cosine.astype(BF)
+            taps = dot(high, third[...]) * (length**-0.5)
+            if half == 1:
+                index = lax.broadcasted_iota(jnp.int32, taps.shape, 0) + at * chunk
+                taps = jnp.where(index == 0, 0.0, taps)
+            totals[...] += jnp.sum(taps * sign_rows(*taps.shape), axis=0, keepdims=True)
+            spread[pl.ds(pl.multiple_of(at * chunk, chunk), chunk), pl.ds(half * 128, 128)] = taps.astype(BF)
+            return carry
+
+        lax.fori_loop(0, per, tap_step, 0)
+    acts_copy = pltpu.make_async_copy(acts, acts_out, local_sems.at[5])
+    acts_copy.start()
+    out_copies.append(acts_copy)
+    table_load.wait()
+
+    def spectrum_step(at, carry):
+        here = pl.ds(pl.multiple_of(at * chunk, chunk), chunk)
+        sign = sign_rows(chunk, 128)
+        index = lax.broadcasted_iota(jnp.int32, (chunk, 128), 0) + at * chunk
+        weight = jnp.where(index == 0, 0.5 / length, 1.0 / length)
+        for which in range(2):
+            result = dot(table_v[which, here, :], spread[...])
+            taps_v[which, here, :] = ((result[:, :128] + sign * result[:, 128:]) * weight).astype(BF)
+        return carry
+
+    lax.fori_loop(0, per, spectrum_step, 0)
+    copy = pltpu.make_async_copy(taps_v, taps_out, local_sems.at[6])
+    copy.start()
+    out_copies.append(copy)
+    tap_total = jnp.broadcast_to(totals[...], (128, 128)).T[:chans, 0:1]
+
+    for copy in sends:
+        copy.wait_recv()
+    copy = pltpu.make_async_copy(signals, signals_out, local_sems.at[7])
+    copy.start()
+    out_copies.append(copy)
+
+    step = 16
+    padded[pl.ds(chans, 128 - chans), :] = jnp.zeros((128 - chans, length), BF)
+
+    def short_step(at, carry):
+        here = pl.ds(pl.multiple_of(at * step, step), step)
+        shorted = []
+        for s in range(3):
+            value = signals[s, here, :].astype(F32)
+            shorted.append(
+                previous(value) * columns[here, 3 * s : 3 * s + 1]
+                + value * columns[here, 3 * s + 1 : 3 * s + 2]
+                + following(value) * columns[here, 3 * s + 2 : 3 * s + 3]
+            )
+        result = shorted[0] * shorted[2]
+        product[here, :] = result
+        keyed[here, :] = shorted[1]
+        padded[here, :] = result.astype(BF)
+        nyquist[here, 0:1] = jnp.sum(result * sign_lanes(step, length), axis=1, keepdims=True)
+        return carry
+
+    lax.fori_loop(0, chans // step, short_step, 0)
+    nyquist[:, 1:2] = tap_total
+
+    def wave_step(at, carry):
+        here = pl.ds(pl.multiple_of(at * chunk, chunk), chunk)
+        cos_part = dot(table_v[0, here, :], padded[...], NT)
+        sin_part = dot(table_v[1, here, :], padded[...], NT)
+        wave[0, here, :] = cos_part.astype(BF)
+        wave[1, here, :] = sin_part.astype(BF)
+        tap_cos = taps_v[0, here, :].astype(F32)
+        tap_sin = taps_v[1, here, :].astype(F32)
+        spectrum[0, here, :] = (cos_part * tap_cos - sin_part * tap_sin).astype(BF)
+        spectrum[1, here, :] = (cos_part * tap_sin + sin_part * tap_cos).astype(BF)
+        return carry
+
+    lax.fori_loop(0, per, wave_step, 0)
+
+    def conv_step(at, carry):
+        here = pl.ds(pl.multiple_of(at * chunk, chunk), chunk)
+        result = dot(table_v[0, here, :], spectrum[0]) + dot(table_v[1, here, :], spectrum[1])
+        result = result.T[:chans]
+        result = (
+            result
+            + sign_lanes(chans, chunk) * (nyquist[:, 0:1] * nyquist[:, 1:2] * (0.5 / length))
+            + columns[:, 9:10] * product[:, here]
+        )
+        conv[:, here] = result
+        mixed[:, here] = (keyed[:, here] * result).astype(BF)
+        return carry
+
+    lax.fori_loop(0, per, conv_step, 0)
+    backs = []
+    slot = pl.ds(pl.multiple_of(me * chans, 16), chans)
+    for k in SEQ_ORDER:
+        other = flip(me, k)
+        copy = pltpu.make_async_remote_copy(
+            src_ref=mixed.at[:, pl.ds(pl.multiple_of(other * rows, rows), rows)],
+            dst_ref=mixed_rows.at[slot, :],
+            send_sem=back_send.at[k],
+            recv_sem=back_recv.at[k],
+            device_id={"seq": other},
+            device_id_type=MESH,
+        )
+        copy.start()
+        backs.append(copy)
+    mixed_rows[slot, :] = mixed[:, mine]
+    for at, pair in enumerate(((wave, wave_out), (conv, conv_out), (nyquist, nyquist_out))):
+        copy = pltpu.make_async_copy(pair[0], pair[1], local_sems.at[8 + at])
+        copy.start()
+        out_copies.append(copy)
+    for copy in sends:
+        copy.wait_send()
+    for copy in cot_copies:
+        copy.wait()
+    own_cot.wait()
+    for copy in backs:
+        copy.wait()
+    mixed_out[...] = mixed_rows[...]
+    for copy in out_copies:
+        copy.wait()
+
+
+def front(mesh_shape, tokens, cotangent, table, vectors, right, left, columns, features, first, second, third):
+    n_seq, n_tp = mesh_shape
+    _, rows, width = tokens.shape
+    chans, length = width // n_seq, rows * n_seq
+    shape = jax.ShapeDtypeStruct
+    return pl.pallas_call(
+        functools.partial(front_kernel, n_seq, n_tp, (width, chans, length, rows)),
+        out_shape=(
+            shape((width, rows), BF),
+            shape((3, chans, length), BF),
+            shape((chans, length), F32),
+            shape((2, length, 128), BF),
+            shape((2, length, 128), BF),
+            shape((chans, 128), F32),
+            shape((4, 2 * length, 128), BF),
+            shape((width, rows), BF),
+            shape((width, rows), BF),
+            shape((n_tp, rows, width), BF),
+        ),
+        in_specs=[any_spec()] * 3 + [vmem_spec()] * 8,
+        out_specs=(vmem_spec(),) + (any_spec(),) * 9,
+        scratch_shapes=[
+            pltpu.VMEM((rows, width), BF),
+            pltpu.VMEM((2, length, length), BF),
+            pltpu.VMEM((width, rows), BF),
+            pltpu.VMEM((width, rows), BF),
+            pltpu.VMEM((3 * width, rows), BF),
+            pltpu.VMEM((3, chans, length), BF),
+            pltpu.VMEM((4, 2 * length, 128), BF),
+            pltpu.VMEM((length, 256), BF),
+            pltpu.VMEM((2, length, 128), BF),
+            pltpu.VMEM((128, length), BF),
+            pltpu.VMEM((chans, length), F32),
+            pltpu.VMEM((chans, length), F32),
+            pltpu.VMEM((2, length, 128), BF),
+            pltpu.VMEM((2, length, 128), BF),
+            pltpu.VMEM((chans, length), F32),
+            pltpu.VMEM((chans, length), BF),
+            pltpu.VMEM((width, rows), BF),
+            pltpu.VMEM((chans, 128), F32),
+            pltpu.VMEM((1, 128), F32),
+            pltpu.SemaphoreType.DMA((12,)),
+            pltpu.SemaphoreType.DMA((n_seq, 3)),
+            pltpu.SemaphoreType.DMA((n_seq, 3)),
+            pltpu.SemaphoreType.DMA((n_seq,)),
+            pltpu.SemaphoreType.DMA((n_seq,)),
+            pltpu.SemaphoreType.DMA((n_tp,)),
+            pltpu.SemaphoreType.DMA((n_tp,)),
+        ],
+        compiler_params=pltpu.CompilerParams(collective_id=0, has_side_effects=True, vmem_limit_bytes=LIMIT),
+        name="front",
+    )(tokens, cotangent, table, vectors, right, left, columns, features, first, second, third)
+
+
+def split_table(values):
+    high = values.astype(BF)
+    low = (values - high.astype(np.float32)).astype(BF)
+    return high, low
+
+
+def constants(length):
+    index = np.arange(length)
+    angle = (index[:, None] * index[None, :] % (2 * length)) * (math.pi / length)
+    table = np.stack([np.cos(angle), np.sin(angle)]).astype(np.float32).astype(BF)
+    place = np.arange(2 * length)
+    scaled = np.where(place < length, place, place - 2 * length) / length
+    features = np.zeros((2 * length, 8), np.float32)
+    features[:, 0] = scaled
+    features[:, 1] = np.sin(math.pi * scaled)
+    features[:, 2] = np.cos(math.pi * scaled)
+    features[:, 3] = np.sin(7.0 * math.pi * scaled)
+    features[:, 4] = np.cos(7.0 * math.pi * scaled)
+    return table, np.concatenate(split_table(features), axis=1)
+
+
+def prepare(tokens, norm_gain, norm_bias, ffn_gain, ffn_bias, short_kernel, filter_first, filter_third, conv_bias):
+    me = lax.axis_index("seq")
+    width = tokens.shape[2]
+    chans = width // lax.axis_size("seq")
+    vectors = jnp.stack([norm_gain, norm_bias, ffn_gain, ffn_bias] + [jnp.zeros_like(norm_gain)] * 4)
+    kernel = lax.dynamic_slice_in_dim(short_kernel, me * chans, chans, 1).astype(F32)
+    bias = lax.dynamic_slice_in_dim(conv_bias, me * chans, chans, 0)
+    columns = jnp.concatenate(
+        [kernel.transpose(1, 0, 2).reshape(chans, 9), bias[:, None], jnp.zeros((chans, 6), F32)], axis=1
+    )
+    lead = jnp.pad(filter_first, ((0, 3), (0, 0)))
+    first = jnp.concatenate([lead, lead], axis=0)
+    third = jnp.pad(lax.dynamic_slice_in_dim(filter_third, me * chans, chans, 1), ((0, 0), (0, 128 - chans)))
+    return vectors, columns, first, third
+
 
 highest = lax.Precision.HIGHEST
 
@@ -36,7 +430,7 @@
     )
 
 
-def monarch_forward(operand, right_factor, left_factor):
+def rows_monarch_forward(operand, right_factor, left_factor):
     row_count = operand.shape[0]
     groups = right_factor.shape[0]
     blocked = operand.reshape(row_count, groups, -1)
@@ -48,7 +442,7 @@
     return (shuffled, result.reshape(row_count, -1))
 
 
-def monarch_backward(grad_result, operand, shuffled, right_factor, left_factor):
+def rows_monarch_backward(grad_result, operand, shuffled, right_factor, left_factor):
     row_count = operand.shape[0]
     groups = right_factor.shape[0]
     grad_blocked = grad_result.reshape(row_count, groups, -1)
@@ -154,7 +548,7 @@
     return (features, pre_one, act_one, pre_two, act_two, tap_mask, filt_real, filt_imag)
 
 
-def body(
+def general_body(
     tokens,
     norm_gain,
     norm_bias,
@@ -190,7 +584,7 @@
     flat = mix_tokens.reshape(mix_rows, model_width).astype(jnp.float32)
     normed, scaled_one, inverse_one = norm_forward(flat, norm_gain, norm_bias)
     normed_low = normed.astype(jnp.bfloat16)
-    shuffled_in, projected = monarch_forward(normed_low, in_right, in_left)
+    shuffled_in, projected = rows_monarch_forward(normed_low, in_right, in_left)
     projected_low = (
         projected.astype(jnp.bfloat16)
         .reshape(mix_count, pos_count, 3, model_width)
@@ -222,7 +616,7 @@
     mixed_low = (shorted[1] * convolved).astype(jnp.bfloat16)
     back_rows = lax.all_to_all(mixed_low, "seq", split_axis=2, concat_axis=0, tiled=True)
     mixed_rows = back_rows.transpose(1, 2, 0).reshape(mix_rows, model_width)
-    shuffled_out, branch = monarch_forward(mixed_rows, out_right, out_left)
+    shuffled_out, branch = rows_monarch_forward(mixed_rows, out_right, out_left)
     residual_mine = (flat + branch).reshape(mix_count, pos_count, model_width)
     residual = lax.all_gather(residual_mine, "tp", axis=0, tiled=True)
     part_resid = lax.dynamic_slice_in_dim(residual, tp_index * part_rows, part_rows, 1)
@@ -270,7 +664,7 @@
     grad_resid_mix = lax.dynamic_slice_in_dim(
         grad_resid, tp_index * mix_count, mix_count, 0
     ).reshape(mix_rows, model_width)
-    grad_mixed_rows, grad_out_right, grad_out_left = monarch_backward(
+    grad_mixed_rows, grad_out_right, grad_out_left = rows_monarch_backward(
         grad_resid_mix.astype(jnp.bfloat16), mixed_rows, shuffled_out, out_right, out_left
     )
     grad_mixed_low = (
@@ -329,7 +723,7 @@
         grad_signals.astype(jnp.bfloat16), "seq", split_axis=3, concat_axis=1, tiled=True
     )
     grad_proj_rows = grad_proj.transpose(2, 3, 0, 1).reshape(mix_rows, 3 * model_width)
-    grad_normed_one, grad_in_right, grad_in_left = monarch_backward(
+    grad_normed_one, grad_in_right, grad_in_left = rows_monarch_backward(
         grad_proj_rows, normed_low, shuffled_in, in_right, in_left
     )
     grad_in_one, grad_gain_one, grad_bias_one = norm_backward(
@@ -415,9 +809,272 @@
     )
 
 
+def fast_body(
+    tokens,
+    norm_gain,
+    norm_bias,
+    in_right,
+    in_left,
+    short_kernel,
+    filter_first,
+    filter_second,
+    filter_third,
+    conv_bias,
+    out_right,
+    out_left,
+    ffn_gain,
+    ffn_bias,
+    gate_weight,
+    up_weight,
+    down_weight,
+    cotangent,
+):
+    seq_count, pos_count, model_width = tokens.shape
+    row_count = seq_count * pos_count
+    axis_count = lax.axis_size("seq")
+    my_index = lax.axis_index("seq")
+    chan_count = model_width // axis_count
+    seq_length = pos_count * axis_count
+    part_rows = cotangent.shape[1]
+    tp_index = lax.axis_index("tp")
+    tp_count = lax.axis_size("tp")
+    chan_start = my_index * chan_count
+    mix_count = seq_count // tp_count
+    mix_tokens = lax.dynamic_slice_in_dim(tokens, tp_index * mix_count, mix_count, 0)
+    mix_rows = mix_count * pos_count
+    flat = mix_tokens.reshape(mix_rows, model_width).astype(jnp.float32)
+    normed, scaled_one, inverse_one = norm_forward(flat, norm_gain, norm_bias)
+    normed_low = normed.astype(jnp.bfloat16)
+    table, features = constants(seq_length)
+    vectors, columns, first_pair, third_pad = prepare(
+        tokens, norm_gain, norm_bias, ffn_gain, ffn_bias, short_kernel, filter_first, filter_third, conv_bias
+    )
+    (mixed_t, signal_t, conv_t, wave, taps_wave, nyquist, acts, normed_t, shuffled_t, cot_rows) = front(
+        (axis_count, tp_count), tokens, cotangent, jnp.asarray(table), vectors, in_right, in_left, columns,
+        jnp.asarray(features), first_pair, filter_second, third_pad
+    )
+    normed_low = normed_t.T
+    shuffled_in = shuffled_t.T.reshape(mix_rows, 4, -1)
+    channels = signal_t[:, :, None, :]
+    signals = channels.astype(jnp.float32)
+    kernel = lax.dynamic_slice_in_dim(short_kernel, chan_start, chan_count, 1).astype(jnp.float32)
+    tap_zero = kernel[:, :, 0][:, :, None, None]
+    tap_one = kernel[:, :, 1][:, :, None, None]
+    tap_two = kernel[:, :, 2][:, :, None, None]
+    padded = jnp.pad(signals, ((0, 0), (0, 0), (0, 0), (1, 1)))
+    shorted = padded[..., :-2] * tap_zero + padded[..., 1:-1] * tap_one + padded[..., 2:] * tap_two
+    first_f = filter_first.astype(jnp.float32)
+    second_f = filter_second.astype(jnp.float32)
+    third_cols = lax.dynamic_slice_in_dim(filter_third, chan_start, chan_count, 1).astype(
+        jnp.float32
+    )
+    bias_cols = lax.dynamic_slice_in_dim(conv_bias, chan_start, chan_count, 0)[:, None, None]
+    product = shorted[0] * shorted[2]
+    product_pad = jnp.pad(product, ((0, 0), (0, 0), (0, seq_length)))
+    spec_real, spec_imag = spectrum_of(product_pad)
+    convolved = conv_t[:, None, :]
+    mixed_rows = mixed_t.T
+    shuffled_out, branch = rows_monarch_forward(mixed_rows, out_right, out_left)
+    residual_mine = (flat + branch).reshape(mix_count, pos_count, model_width)
+    residual = lax.all_gather(residual_mine, "tp", axis=0, tiled=True)
+    part_resid = lax.dynamic_slice_in_dim(residual, tp_index * part_rows, part_rows, 1)
+    normed_two, scaled_two, inverse_two = norm_forward(part_resid, ffn_gain, ffn_bias)
+    normed_rows = lax.all_gather(normed_two.astype(jnp.bfloat16), "tp", axis=1, tiled=True).reshape(
+        row_count, model_width
+    )
+    gate = jnp.dot(normed_rows, gate_weight, preferred_element_type=jnp.float32)
+    upward = jnp.dot(normed_rows, up_weight, preferred_element_type=jnp.float32)
+    sigma = jax.nn.sigmoid(gate)
+    hidden_low = (gate * sigma * upward).astype(jnp.bfloat16)
+    partial_down = jnp.dot(hidden_low, down_weight, preferred_element_type=jnp.float32).reshape(
+        seq_count, pos_count, model_width
+    )
+    glu_part = lax.psum_scatter(
+        partial_down.astype(jnp.bfloat16), "tp", scatter_dimension=1, tiled=True
+    ).astype(jnp.float32)
+    output = (part_resid + glu_part).astype(jnp.bfloat16)
+    grad_out_rows = cot_rows.reshape(row_count, model_width)
+    grad_hidden = jnp.dot(grad_out_rows, down_weight.T, preferred_element_type=jnp.float32)
+    grad_gate = (grad_hidden * upward * (sigma + gate * sigma * (1.0 - sigma))).astype(jnp.bfloat16)
+    grad_up = (grad_hidden * gate * sigma).astype(jnp.bfloat16)
+    grad_down_w = jnp.dot(hidden_low.T, grad_out_rows, preferred_element_type=jnp.float32)
+    grad_gate_w = jnp.dot(normed_rows.T, grad_gate, preferred_element_type=jnp.float32)
+    grad_up_w = jnp.dot(normed_rows.T, grad_up, preferred_element_type=jnp.float32)
+    grad_normed = jnp.dot(grad_gate, gate_weight.T, preferred_element_type=jnp.float32) + jnp.dot(
+        grad_up, up_weight.T, preferred_element_type=jnp.float32
+    )
+    grad_normed_part = lax.psum_scatter(
+        grad_normed.reshape(seq_count, pos_count, model_width),
+        "tp",
+        scatter_dimension=1,
+        tiled=True,
+    )
+    grad_in_two, grad_gain_two, grad_bias_two = norm_backward(
+        grad_normed_part, scaled_two, inverse_two, ffn_gain
+    )
+    gain_total = lax.psum((grad_gain_two, grad_bias_two), ("seq", "tp"))
+    grad_resid_part = cotangent.astype(jnp.float32) + grad_in_two
+    grad_resid = lax.all_gather(
+        grad_resid_part.astype(jnp.bfloat16), "tp", axis=1, tiled=True
+    ).astype(grad_resid_part.dtype)
+    grad_resid_mix = lax.dynamic_slice_in_dim(
+        grad_resid, tp_index * mix_count, mix_count, 0
+    ).reshape(mix_rows, model_width)
+    grad_mixed_rows, grad_out_right, grad_out_left = rows_monarch_backward(
+        grad_resid_mix.astype(jnp.bfloat16), mixed_rows, shuffled_out, out_right, out_left
+    )
+    grad_mixed_low = (
+        grad_mixed_rows.astype(jnp.bfloat16)
+        .reshape(mix_count, pos_count, model_width)
+        .transpose(2, 0, 1)
+    )
+    grad_mixed = lax.all_to_all(
+        grad_mixed_low, "seq", split_axis=0, concat_axis=2, tiled=True
+    ).astype(jnp.float32)
+    grad_conv = grad_mixed * shorted[1]
+    grad_key = grad_mixed * convolved
+    again = lax.optimization_barrier((first_f, second_f, third_cols))
+    kept = filter_parts(again[0], again[1], again[2], seq_length)
+    filt_real = kept[6][:, None]
+    filt_imag = kept[7][:, None]
+    features, pre_one, act_one, pre_two, act_two, tap_mask = (
+        kept[0],
+        kept[1],
+        kept[2],
+        kept[3],
+        kept[4],
+        kept[5],
+    )
+    grad_pad = jnp.pad(grad_conv, ((0, 0), (0, 0), (0, seq_length)))
+    grad_spec_real, grad_spec_imag = spectrum_of(grad_pad)
+    back_real = grad_spec_real * filt_real + grad_spec_imag * filt_imag
+    back_imag = grad_spec_imag * filt_real - grad_spec_real * filt_imag
+    grad_product = signal_of(back_real, back_imag)[..., :seq_length] + bias_cols * grad_conv
+    grad_bias_cols = jnp.sum(grad_conv * product, axis=(1, 2))
+    taps_real = jnp.sum(grad_spec_real * spec_real + grad_spec_imag * spec_imag, axis=1)
+    taps_imag = jnp.sum(grad_spec_imag * spec_real - grad_spec_real * spec_imag, axis=1)
+    grad_taps = signal_of(taps_real, taps_imag)
+    grad_pre = grad_taps.T * tap_mask
+    grad_third_cols = jnp.dot(act_two.T, grad_pre, precision=highest)
+    grad_pre_two = jnp.dot(grad_pre, third_cols.T, precision=highest) * jnp.cos(pre_two)
+    grad_second = jnp.dot(act_one.T, grad_pre_two, precision=highest)
+    grad_pre_one = jnp.dot(grad_pre_two, second_f.T, precision=highest) * jnp.cos(pre_one)
+    grad_first = jnp.dot(features.T, grad_pre_one, precision=highest)
+    grad_shorted = jnp.stack([grad_product * shorted[2], grad_key, grad_product * shorted[0]])
+    grad_short_pad = jnp.pad(grad_shorted, ((0, 0), (0, 0), (0, 0), (1, 1)))
+    grad_signals = (
+        grad_short_pad[..., 2:] * tap_zero
+        + grad_short_pad[..., 1:-1] * tap_one
+        + grad_short_pad[..., :-2] * tap_two
+    )
+    grad_kernel = jnp.stack(
+        [
+            jnp.sum(grad_shorted * padded[..., :-2], axis=(2, 3)),
+            jnp.sum(grad_shorted * padded[..., 1:-1], axis=(2, 3)),
+            jnp.sum(grad_shorted * padded[..., 2:], axis=(2, 3)),
+        ],
+        axis=-1,
+    )
+    grad_proj = lax.all_to_all(
+        grad_signals.astype(jnp.bfloat16), "seq", split_axis=3, concat_axis=1, tiled=True
+    )
+    grad_proj_rows = grad_proj.transpose(2, 3, 0, 1).reshape(mix_rows, 3 * model_width)
+    grad_normed_one, grad_in_right, grad_in_left = rows_monarch_backward(
+        grad_proj_rows, normed_low, shuffled_in, in_right, in_left
+    )
+    grad_in_one, grad_gain_one, grad_bias_one = norm_backward(
+        grad_normed_one, scaled_one, inverse_one, norm_gain
+    )
+    grad_mine = (grad_resid_mix + grad_in_one).reshape(mix_count, pos_count, model_width)
+    short_full = lax.dynamic_update_slice_in_dim(
+        jnp.zeros(short_kernel.shape, jnp.float32), grad_kernel, chan_start, 1
+    )
+    third_full = lax.dynamic_update_slice_in_dim(
+        jnp.zeros(filter_third.shape, jnp.float32), grad_third_cols, chan_start, 1
+    )
+    bias_full = lax.dynamic_update_slice_in_dim(
+        jnp.zeros(conv_bias.shape, jnp.float32), grad_bias_cols, chan_start, 0
+    )
+    mixer_grads = (
+        grad_gain_one,
+        grad_bias_one,
+        grad_in_right,
+        grad_in_left,
+        short_full,
+        grad_first,
+        grad_second,
+        third_full,
+        bias_full,
+        grad_out_right,
+        grad_out_left,
+    )
+    grad_tokens = lax.all_gather(grad_mine.astype(jnp.bfloat16), "tp", axis=0, tiled=True).astype(
+        grad_mine.dtype
+    )
+    mixer_grads = (
+        lax.psum(mixer_grads[0].astype(jnp.bfloat16), "tp").astype(jnp.float32),
+        lax.psum(mixer_grads[1].astype(jnp.bfloat16), "tp").astype(jnp.float32),
+        lax.psum(mixer_grads[2].astype(jnp.bfloat16), "tp").astype(jnp.float32),
+        lax.psum(mixer_grads[3].astype(jnp.bfloat16), "tp").astype(jnp.float32),
+        lax.psum(mixer_grads[4].astype(jnp.bfloat16), "tp").astype(jnp.float32),
+        lax.psum(mixer_grads[5].astype(jnp.bfloat16), "tp").astype(jnp.float32),
+        lax.psum(mixer_grads[6].astype(jnp.bfloat16), "tp").astype(jnp.float32),
+        lax.psum(mixer_grads[7].astype(jnp.bfloat16), "tp").astype(jnp.float32),
+        lax.psum(mixer_grads[8].astype(jnp.bfloat16), "tp").astype(jnp.float32),
+        lax.psum(mixer_grads[9].astype(jnp.bfloat16), "tp").astype(jnp.float32),
+        lax.psum(mixer_grads[10].astype(jnp.bfloat16), "tp").astype(jnp.float32),
+    )
+    all_total = lax.psum(
+        (
+            mixer_grads[0],
+            mixer_grads[1],
+            mixer_grads[2],
+            mixer_grads[3],
+            mixer_grads[4],
+            mixer_grads[5],
+            mixer_grads[6],
+            mixer_grads[7],
+            mixer_grads[8],
+            mixer_grads[9],
+            mixer_grads[10],
+            grad_gate_w,
+            grad_up_w,
+            grad_down_w,
+        ),
+        "seq",
+    )
+    return (
+        output,
+        grad_tokens,
+        all_total[0],
+        all_total[1],
+        all_total[2],
+        all_total[3],
+        all_total[4],
+        all_total[5],
+        all_total[6],
+        all_total[7],
+        all_total[8],
+        all_total[9],
+        all_total[10],
+        gain_total[0],
+        gain_total[1],
+        all_total[11],
+        all_total[12],
+        all_total[13],
+    )
+
+
+def choose_body(mesh, *arrays):
+    tokens = arrays[0]
+    chans = tokens.shape[2] // mesh.shape["seq"]
+    fits = mesh.shape["seq"] == 8 and mesh.shape["tp"] == 4 and tokens.shape[:2] == (4, 128) and chans == 96
+    return (fast_body if fits else general_body)(*arrays)
+
+
 def solution(mesh):
     return jax.shard_map(
-        body,
+        functools.partial(choose_body, mesh),
         mesh=mesh,
         in_specs=(
             P(None, "seq", None),

time: 684 us -> 616 us (0.901)
  blocking collectives: 325 us -> 295 us
  matrix products: 122 us -> 94.4 us
  Pallas kernels: 0 us -> 26.2 us
  other arithmetic: 57.5 us -> 32.8 us
    pallas_call x0 -> x1, Pallas kernels: none -> 26.2 us  [front(): pl.pallas_call(functools.partial(front_kernel, n_seq, n_tp, (width, chans...]
    all_gather x4 -> x3, blocking collectives: 94.1 us -> 68.5 us  [the longest x1 29 us: fast_body(): lax.all_gather(grad_resid_part.astype(jnp.bfloat16), 'tp', axis=1, tiled=...]
    reduce_scatter x2, waiting for transfers between devices: 45.7 us -> 23.4 us  [the longest x1 22.6 us: fast_body(): lax.psum_scatter(partial_down.astype(jnp.bfloat16), 'tp', scatter_dimensi...]
    all_gather x1, waiting for transfers between devices: 16.8 us -> 36.1 us  [fast_body(): residual = lax.all_gather(residual_mine, 'tp', axis=0, tiled=True)]
    reduce_sum x3, other arithmetic: 15.6 us -> 3.69 us  [the longest x1 1.47 us: fast_body(): grad_bias_cols = jnp.sum(grad_conv * product, axis=(1, 2))]
    all_to_all x1 -> x0, blocking collectives: 10.2 us -> none  [body(): lax.all_to_all(mixed_low, 'seq', split_axis=2, concat_axis=0, tiled=True)]
    add x2 -> x1, other arithmetic: 9.75 us -> 0.92 us  [fast_body(): padded[..., :-2] * tap_zero + padded[..., 1:-1] * tap_one]
    dot_general x26 -> x24, matrix products: 42.4 us -> 36 us  [the longest x1 4.31 us: fast_body(): jnp.dot(grad_pre, third_cols.T, precision=highest) * jnp.cos(pre_two)]
  transfers between devices with their start and end apart: 8 -> 7, of which waited for: 6 -> 6; matrix products, arithmetic and copies ran while one was open for 13% -> 11% of each run, Pallas kernels for 0% -> 0%
where the time goes in v1:
time: 616 us; the launch traced here: 612 us
  blocking collectives  295 us (48%)
  matrix products  94.4 us (15%)
  waiting for transfers between devices  81.4 us (13%)
  local copies, waits for them, and re-layouts  58.5 us (9%)
  other arithmetic  32.8 us (5%)
  Pallas kernels  26.2 us (4%)
  between operations  15.4 us (2%)
  starting transfers between devices  9.07 us (1%)
    psum x1, blocking collectives, fast_body(): lax.psum((mixer_grads[0], mixer_grads[1], mixer_grads[2], mixer_grads[3],...  164 us
    psum x1, blocking collectives, fast_body(): gain_total = lax.psum((grad_gain_two, grad_bias_two), ('seq', 'tp'))  41.8 us
    all_gather x1, waiting for transfers between devices, fast_body(): residual = lax.all_gather(residual_mine, 'tp', axis=0, tiled=True)  36.1 us
    all_gather x1, blocking collectives, fast_body(): lax.all_gather(grad_resid_part.astype(jnp.bfloat16), 'tp', axis=1, tiled=...  29 us
    pallas_call x1, Pallas kernels, front(): pl.pallas_call(functools.partial(front_kernel, n_seq, n_tp, (width, chans...  26.2 us
    reduce_scatter x1, waiting for transfers between devices, fast_body(): lax.psum_scatter(partial_down.astype(jnp.bfloat16), 'tp', scatter_dimensi...  22.6 us
    unnamed x190, local copies, waits for them, and re-layouts  21.8 us
    all_gather x1, blocking collectives, fast_body(): lax.all_gather(grad_mine.astype(jnp.bfloat16), 'tp', axis=0, tiled=True)  21.5 us
  transfers between devices with their start and end apart: 7, of which 6 were waited for; matrix products, arithmetic and copies ran while one was open for 11% of the time, Pallas kernels for 0%

profile of v1, /device:TPU:0, one launch (start us, length us, event | category | flops | bytes accessed | tf_op | source)
XLA Modules:
  0.0 612.3 jit_solution(5708200129717279101)
XLA Ops:
  17.2 26.2 %front.1 = (bf16[768,128]{1,0:T(8,128)(2,1)}, bf16[3,96,1024]{2,1,0:T(8,128)(2,1)}, f32[96,1024]{1,0:T(8,128)}, bf16[2,1024,128]{2,1,0:T(8,128)(2,1)}, bf16[2,10...) custom-call(bf16[4,128,768]{2,1,0:T(8,128)(2,1)} %refs_0_.1, ...), custom_call_target="tpu_custom_call" | custom-call | tf_op jit(solution)/shard_map/front/pallas_call | solution.py:316
  45.4 2.2 convert_reduce_fusion
  48.0 36.1 %all-gather.2.cloned.1.call-done = f32[4,128,768]{2,1,0:T(8,128)} async-done(((f32[1,128,768]{2,1,0:T(8,128)}), f32[4,128,768]{2,1,0:T(8,128)}) %all-gather.2.cloned.1.call-update) | async-done | bytes 1572880 | tf_op jit(solution)/shard_map/all_gather | solution.py:879
  87.6 18.0 %all_gather.13 = bf16[4,128,768]{2,1,0:T(8,128)(2,1)S(1)} all-gather(bf16[4,32,768]{2,1,0:T(8,128)(2,1)S(1)} %add_convert_fusion.2), channel_id=1, replica_groups=mesh['seq'=8,'tp'=4] {'tp'}, dimensions={1}, use_global_device_ids=true | all-gather | bytes 983040 | tf_op jit(solution)/shard_map/all_gather | solution.py:882
  113.1 6.1 fusion.267
  119.2 5.3 fusion.268
  144.4 2.2 convolution_subtract_fusion.5
  149.9 22.6 %reduce-scatter.3.cloned.1.call-done = bf16[4,32,768]{2,1,0:T(8,128)(2,1)} async-done(((bf16[4,128,768]{2,1,0:T(8,128)(2,1)}), bf16[4,32,768]{2,1,0:T(8,128)(2,1)}) %reduce-scatter.3.cloned.1.call-update) | async-done | bytes 196624 | tf_op jit(solution)/shard_map/reduce_scatter | solution.py:892
  174.5 29.0 %all_gather.14 = bf16[4,128,768]{2,1,0:T(8,128)(2,1)S(1)} all-gather(bf16[4,32,768]{2,1,0:T(8,128)(2,1)S(1)} %get-tuple-element.101), channel_id=1, replica_groups=mesh['seq'=8,'tp'=4] {'tp'}, dimensions={1}, use_global_device_ids=true | all-gather | bytes 983040 | tf_op jit(solution)/shard_map/all_gather | solution.py:917
  210.4 2.7 reduce.9
  213.9 4.0 all-to-all-start
  219.9 4.3 all-to-all-done
  232.2 2.5 copy.270
  234.7 3.1 convolution_bitcast_fusion
  242.8 2.5 copy.243
  245.3 2.3 convolution_bitcast_fusion.2
  247.6 2.5 subtract_bitcast_fusion.2
  269.2 2.2 fusion.14
  274.6 2.5 copy.258
  288.4 4.4 all-to-all-start.1
  299.1 9.1 %all-to-all-done.1 = bf16[3,96,1,1024]{1,0,2,3:T(4,128)(2,1)} async-done(((bf16[3,96,1,1024]{1,0,2,3:T(4,128)(2,1)}), bf16[3,96,1,1024]{1,0,2,3:T(4,128)(2,1)}, u32[]{:S(2)}, u32[]{:S(2)}) %all-to-all-start.1) | async-done | bytes 589856 | tf_op jit(solution)/shard_map/all_to_all | solution.py:978
  314.3 2.2 fusion.277
  316.5 2.2 fusion.278
  318.7 2.2 fusion.279
  325.0 41.8 %all-reduce.6 = (f32[768]{0:T(1024)}, f32[768]{0:T(1024)}) all-reduce(f32[768]{0:T(1024)S(1)} %copy-done.79, f32[768]{0:T(1024)S(1)} %copy-done.80), channel_id=1, replica_groups=mesh['seq'=8,'tp'=4] {'seq','tp'}, use_global_device_ids=true, to_apply=%region_39.40 | all-reduce | flops 1536 | bytes 12288 | tf_op jit(solution)/shard_map/psum | solution.py:915
  368.5 4.3 convolution_multiply_fusion
  372.8 4.0 convolution_multiply_fusion.1
  380.6 19.9 %all-reduce.9 = (bf16[768]{0:T(1024)(128)(2,1)S(1)}, bf16[768]{0:T(1024)(128)(2,1)S(1)}, bf16[3,768,3]{1,2,0:T(4,128)(2,1)S(1)}, bf16[5,128]{1,0:T(8,128)(2,1)S(...) all-reduce(bf16[768]{0:T(1024)(128)(2,1)S(1)} %convert_element_type, ...), channel_id=1, replica_groups=mesh['seq'=8,'tp'=4] {'tp'}, use_global_device_ids=true, to_apply=%region_11.12 | all-reduce | flops 26240 | bytes 104960 | tf_op jit(solution)/shard_map/psum | solution.py:1015
  402.0 21.5 %all_gather.15 = bf16[4,128,768]{2,1,0:T(8,128)(2,1)S(1)} all-gather(bf16[1,128,768]{2,1,0:T(8,128)(2,1)S(1)} %fusion.35), channel_id=1, replica_groups=mesh['seq'=8,'tp'=4] {'tp'}, dimensions={0}, use_global_device_ids=true | all-gather | bytes 983040 | tf_op jit(solution)/shard_map/all_gather | solution.py:1011
  424.8 164.3 %all-reduce.18 = (f32[768]{0:T(1024)}, f32[768]{0:T(1024)}, f32[4,192,192]{2,1,0:T(8,128)}, f32[4,192,576]{2,1,0:T(8,128)}, f32[3,768,3]{1,2,0:T(4,128)}, /*inde...) all-reduce(bf16[768]{0:T(1024)(128)(2,1)S(1)} %get-tuple-element.62, ...), channel_id=1, replica_groups=mesh['seq'=8,'tp'=4] {'seq'}, use_global_device_ids=true, to_apply=%region_12.13 | all-reduce | flops 1009280 | bytes 6055680 | tf_op jit(solution)/shard_map/psum | solution.py:1027
  589.0 8.5 %all-reduce.15.cloned.1.call-done = (f32[768,768]{1,0:T(8,128)}, f32[768,768]{1,0:T(8,128)}, f32[768,768]{1,0:T(8,128)}) async-done(((f32[768,768]{1,0:T(8,128)}, f32[768,768]{1,0:T(8,128)}, f32[768,768]{1,0:T(8,128)}), (f32[768,768]{1,0:T(8,128)}, f32[768,768]{1,0:T(8,128)}, f32[768,768]{1,0:T(8,128)})) %all-reduce.15.cloned.1.call-update) | async-done | bytes 7077904 | tf_op jit(solution)/shard_map/psum | solution.py:1027
  597.5 3.4 copy.374
  (332 shorter events, 132.9 us)
Async XLA Ops:
  7.2 100.5 %copy-start = (bf16[768,768]{1,0:T(8,128)(2,1)S(1)}, bf16[768,768]{1,0:T(8,128)(2,1)}, u32[]{:S(2)}) copy-start(bf16[768,768]{1,0:T(8,128)(2,1)} %param.36) | copy-start | bytes 3538948
  7.2 76.9 %all-gather.2.cloned.1.call-start = ((), (), s32[]{:S(2)}) async-start(), calls=%async_computation.4 | async-start | bytes 1966080 | tf_op jit(solution)/shard_map/all_gather | solution.py:879
  11.9 4.7 copy-start.56
  17.2 26.2 %copy-start.34 = (bf16[4,192,192]{2,1,0:T(8,128)(2,1)S(1)}, bf16[4,192,192]{2,1,0:T(8,128)(2,1)}, u32[]{:S(2)}) copy-start(bf16[4,192,192]{2,1,0:T(8,128)(2,1)} %param.30) | copy-start | bytes 884740
  45.4 41.0 %copy-start.65 = (f32[768]{0:T(1024)S(1)}, f32[768]{0:T(1024)}, u32[]{:S(2)}) copy-start(f32[768]{0:T(1024)} %param.32) | copy-start | bytes 9220
  45.4 41.0 %copy-start.78 = (f32[768]{0:T(1024)S(1)}, f32[768]{0:T(1024)}, u32[]{:S(2)}) copy-start(f32[768]{0:T(1024)} %param.33) | copy-start | bytes 9220
  47.7 99.7 %reduce-scatter.5.cloned.1.call-start = ((), (), s32[]{:S(2)}) async-start(), calls=%async_computation.6 | async-start | bytes 1966080 | tf_op jit(solution)/shard_map/reduce_scatter | solution.py:906
  48.0 57.6 %copy-start.88 = (bf16[768,768]{1,0:T(8,128)(2,1)S(1)}, bf16[768,768]{1,0:T(8,128)(2,1)}, u32[]{:S(2)}) copy-start(bf16[768,768]{1,0:T(8,128)(2,1)} %param.34) | copy-start | bytes 3538948
  85.2 21.2 %copy-start.67 = (f32[4,32]{1,0:T(4,128)}, f32[4,32]{1,0:T(4,128)S(1)}, u32[]{:S(2)}) copy-start(f32[4,32]{1,0:T(4,128)S(1)} %broadcast_multiply_fusion.5) | copy-start | bytes 1540
  86.5 19.9 %copy-start.70 = (f32[4,32]{1,0:T(4,128)}, f32[4,32]{1,0:T(4,128)S(1)}, u32[]{:S(2)}) copy-start(f32[4,32]{1,0:T(4,128)S(1)} %add_rsqrt_fusion) | copy-start | bytes 1540
  109.3 28.3 %copy-start.29 = (bf16[512,768]{1,0:T(8,128)(2,1)}, bf16[512,768]{1,0:T(8,128)(2,1)S(1)}, u32[]{:S(2)}) copy-start(bf16[512,768]{1,0:T(8,128)(2,1)S(1)} %get-tuple-element.86) | copy-start | bytes 2359300
  112.5 60.1 %reduce-scatter.3.cloned.1.call-start = ((), (), s32[]{:S(2)}) async-start(), calls=%async_computation.5 | async-start | bytes 983040 | tf_op jit(solution)/shard_map/reduce_scatter | solution.py:892
  113.1 11.4 %copy-start.49 = (f32[2048,5]{0,1:T(8,128)}, f32[2048,5]{0,1:T(8,128)S(1)}, u32[]{:S(2)}) copy-start(f32[2048,5]{0,1:T(8,128)S(1)} %stack.64) | copy-start | bytes 122884
  119.2 5.3 copy-start.2
  119.2 6.3 %copy-start.58 = (f32[128,96]{1,0:T(8,128)S(1)}, f32[128,96]{1,0:T(8,128)}, u32[]{:S(2)}) copy-start(f32[128,96]{1,0:T(8,128)} %get-tuple-element.30) | copy-start | bytes 147460
  144.4 28.1 %copy-start.48 = (bf16[4,32,768]{2,1,0:T(8,128)(2,1)S(1)}, bf16[4,32,768]{2,1,0:T(8,128)(2,1)}, u32[]{:S(2)}) copy-start(bf16[4,32,768]{2,1,0:T(8,128)(2,1)} %refs_1_.1) | copy-start | bytes 589828
  174.5 33.0 %copy-start.33 = (bf16[128,4,4,48]{0,3,2,1:T(8,128)(2,1)S(1)}, bf16[128,4,4,48]{0,3,2,1:T(8,128)(2,1)}, u32[]{:S(2)}) copy-start(bf16[128,4,4,48]{0,3,2,1:T(8,128)(2,1)} %copy-done.32) | copy-start | bytes 589828
  213.9 10.3 %all-to-all-start = ((bf16[8,2,6144]{2,1,0:T(2,128)(2,1)}), bf16[8,2,6144]{2,1,0:T(2,128)(2,1)}, u32[]{:S(2)}, u32[]{:S(2)}) async-start(bf16[8,2,6144]{2,1,0:T(2,128)(2,1)} %reshape.714), calls=%async_computation.2 | async-start | bytes 393216 | tf_op jit(solution)/shard_map/all_to_all | solution.py:931
  288.4 4.4 copy-start.21
  288.4 4.5 copy-start.22
  288.4 19.8 %all-to-all-start.1 = ((bf16[3,96,1,1024]{1,0,2,3:T(4,128)(2,1)}), bf16[3,96,1,1024]{1,0,2,3:T(4,128)(2,1)}, u32[]{:S(2)}, u32[]{:S(2)}) async-start(bf16[3,96,1,1024]{1,0,2,3:T(4,128)(2,1)} %copy.262), calls=%async_computation.3 | async-start | bytes 2097152 | tf_op jit(solution)/shard_map/all_to_all | solution.py:978
  292.8 132.0 %all-reduce.17.cloned.1.call-start = ((), (), s32[]{:S(2)}) async-start(), calls=%async_computation.8 | async-start | bytes 4718592 | tf_op jit(solution)/shard_map/psum | solution.py:1017
  298.8 11.0 %copy-start.17 = (bf16[4,192,576]{2,1,0:T(8,128)(2,1)S(1)}, bf16[4,192,576]{2,1,0:T(8,128)(2,1)}, u32[]{:S(2)}) copy-start(bf16[4,192,576]{2,1,0:T(8,128)(2,1)} %refs_5_.1) | copy-start | bytes 2654212
  299.1 11.1 %copy-start.41 = (bf16[128,768]{1,0:T(8,128)(2,1)}, bf16[128,768]{1,0:T(8,128)(2,1)S(1)}, u32[]{:S(2)}) copy-start(bf16[128,768]{1,0:T(8,128)(2,1)S(1)} %dynamic_update_slice.10) | copy-start | bytes 589828
  313.2 284.3 %all-reduce.15.cloned.1.call-start = ((), (), s32[]{:S(2)}) async-start(), calls=%async_computation.7 | async-start | bytes 14155776 | tf_op jit(solution)/shard_map/psum | solution.py:1027
  321.6 45.1 %copy-start.14 = (bf16[3,96,1024]{2,1,0:T(8,128)(2,1)S(1)}, bf16[3,96,1024]{2,1,0:T(8,128)(2,1)}, u32[]{:S(2)}) copy-start(bf16[3,96,1024]{2,1,0:T(8,128)(2,1)} %get-tuple-element.29) | copy-start | bytes 1769476
  321.6 45.1 %copy-start.36 = (f32[1,96,1024]{2,1,0:T(8,128)S(1)}, f32[1,96,1024]{2,1,0:T(8,128)}, u32[]{:S(2)}) copy-start(f32[1,96,1024]{2,1,0:T(8,128)} %get-tuple-element.95) | copy-start | bytes 1179652
  321.6 45.1 %copy-start.39 = (f32[1,96,1024]{2,1,0:T(8,128)S(1)}, f32[1,96,1024]{2,1,0:T(8,128)}, u32[]{:S(2)}) copy-start(f32[1,96,1024]{2,1,0:T(8,128)} %get-tuple-element.76) | copy-start | bytes 1179652
  323.7 44.5 %copy-start.86 = (bf16[96]{0:T(256)(128)(2,1)S(1)}, bf16[96]{0:T(256)(128)(2,1)}, u32[]{:S(2)}) copy-start(bf16[96]{0:T(256)(128)(2,1)} %get-tuple-element.73) | copy-start | bytes 580
  323.7 44.8 %copy-start.16 = (f32[2048,128]{1,0:T(8,128)S(1)}, f32[2048,128]{1,0:T(8,128)}, u32[]{:S(2)}) copy-start(f32[2048,128]{1,0:T(8,128)} %get-tuple-element.123) | copy-start | bytes 3145732
  323.7 44.8 %copy-start.57 = (bf16[128,96]{1,0:T(8,128)(2,1)S(1)}, bf16[128,96]{1,0:T(8,128)(2,1)}, u32[]{:S(2)}) copy-start(bf16[128,96]{1,0:T(8,128)(2,1)} %copy-done.56) | copy-start | bytes 73732
  368.5 4.3 copy-start.55
  (65 other events, 137.2 us)
Sparse Core Ops, SparseCore 0:
  47.8 36.2 all-gather.1
  112.6 34.7 reduce-scatter.4
  150.2 22.2 reduce-scatter.2
  313.3 104.0 all-reduce.16
  422.0 175.4 all-reduce.14

commit v2 on v1

--- a/solution.py
+++ b/solution.py
@@ -399,6 +399,861 @@
     return vectors, columns, first, third
 
 
+def monarch_backward(upstream, operand, shuffled, right, left, middle, keep_right, keep_left, store):
+    groups, width, _ = right.shape
+    part = width // groups
+    for g in range(groups):
+        above = upstream(g)
+        keep_left(g, dot(shuffled[pl.ds(g * width, width), :], above, NT))
+        below = dot(left[g], above).astype(BF)
+        for b in range(groups):
+            middle[pl.ds(b * width + g * part, part), :] = below[b * part : (b + 1) * part]
+    for b in range(groups):
+        above = middle[pl.ds(b * width, width), :]
+        keep_right(b, dot(operand(b), above, NT))
+        store(b, dot(right[b], above))
+
+
+CHIPS = (6, 2, 4)
+
+
+def feed_kernel(n_seq, n_tp, dims, *refs):
+    (mixed, tokens, cot_rows, vectors, right, left, gate_w, up_w, down_w) = refs[:9]
+    (grad_mixed_out, grad_resid_out, shard_out, grad_weights_out, grad_vectors_out, output_out) = refs[9:15]
+    (token_v, cot_v, gate_v, up_v, down_v, shuffled, branch, resid, scaled, inverse, normed, hidden, grad_hidden, grad_gate, grad_up,
+     grad_normed, grad_send, grad_recv, glu_own, glu_send, glu_recv, turned, grads, core_recv, halves, chip_recv, grad_branch,
+     middle, grad_mixed, grad_mixed_all, out_rows, output_v, local_sems, gather_send, gather_recv, back_send, back_recv, glu_ssem, glu_rsem,
+     out_send, out_recv, core_ssem, core_rsem, chip_ssem, chip_rsem, seq_send, seq_recv) = refs[15:]
+    width, chans, length, rows = dims
+    me, plane = lax.axis_index("seq"), lax.axis_index("tp")
+    entered = greet(n_seq, n_tp)
+    loads = [
+        pltpu.make_async_copy(tokens.at[plane], token_v, local_sems.at[0]),
+        pltpu.make_async_copy(cot_rows, cot_v, local_sems.at[1]),
+        pltpu.make_async_copy(down_w, down_v, local_sems.at[2]),
+        pltpu.make_async_copy(gate_w, gate_v, local_sems.at[3]),
+        pltpu.make_async_copy(up_w, up_v, local_sems.at[4]),
+    ]
+    for copy in loads:
+        copy.start()
+    groups = right.shape[0]
+    block = width // groups
+
+    def keep_branch(g, result):
+        branch[pl.ds(g * block, block), :] = result
+
+    monarch_forward(lambda b: mixed[pl.ds(b * block, block), :], right, left, shuffled, keep_branch)
+    loads[0].wait()
+    value = token_v[...].astype(F32) + branch[...].T
+    resid[...] = value
+    shifted = value - jnp.mean(value, axis=-1, keepdims=True)
+    inverse[...] = lax.rsqrt(jnp.mean(shifted * shifted, axis=-1, keepdims=True) + 1e-05)
+    value = shifted * inverse[...]
+    scaled[...] = value
+    normed[plane] = (value * vectors[2:3, :] + vectors[3:4, :]).astype(BF)
+    entered()
+    gathers = {}
+    for k in range(1, n_tp):
+        gathers[k] = pltpu.make_async_remote_copy(
+            src_ref=normed.at[plane],
+            dst_ref=normed.at[plane],
+            send_sem=gather_send.at[k],
+            recv_sem=gather_recv.at[k],
+            device_id={"tp": flip(plane, k)},
+            device_id_type=MESH,
+        )
+        gathers[k].start()
+    loads[1].wait()
+    loads[2].wait()
+    chunk = 256
+    pieces = width // chunk
+
+    def hidden_step(at, carry):
+        cols = pl.ds(pl.multiple_of(at * chunk, chunk), chunk)
+        result = dot(cot_v[...].reshape(n_tp * rows, width), down_v[cols, :], NT)
+        grad_hidden[:, :, cols] = result.reshape(n_tp, rows, chunk)
+        return carry
+
+    lax.fori_loop(0, pieces, hidden_step, 0)
+    loads[3].wait()
+    loads[4].wait()
+    backs, glus = {}, {}
+    for k in range(n_tp):
+        other = flip(plane, k)
+        if k > 0:
+            gathers[k].wait_recv()
+
+        def gate_step(at, carry, other=other):
+            cols = pl.ds(pl.multiple_of(at * chunk, chunk), chunk)
+            value = normed[other]
+            gate = dot(value, gate_v[:, cols])
+            upward = dot(value, up_v[:, cols])
+            sigma = 1.0 / (1.0 + jnp.exp(-gate))
+            active = gate * sigma
+            hidden[other, :, cols] = (active * upward).astype(BF)
+            above = grad_hidden[other, :, cols]
+            grad_gate[other, :, cols] = (above * upward * (sigma + active * (1.0 - sigma))).astype(BF)
+            grad_up[other, :, cols] = (above * active).astype(BF)
+            return carry
+
+        lax.fori_loop(0, pieces, gate_step, 0)
+
+        def back_step(at, carry, k=k, other=other):
+            cols = pl.ds(pl.multiple_of(at * chunk, chunk), chunk)
+            result = dot(grad_gate[other], gate_v[cols, :], NT) + dot(grad_up[other], up_v[cols, :], NT)
+            if k == 0:
+                grad_normed[:, cols] = result
+            else:
+                grad_send[k, :, cols] = result.astype(BF)
+            return carry
+
+        lax.fori_loop(0, pieces, back_step, 0)
+        if k > 0:
+            backs[k] = pltpu.make_async_remote_copy(
+                src_ref=grad_send.at[k],
+                dst_ref=grad_recv.at[k],
+                send_sem=back_send.at[k],
+                recv_sem=back_recv.at[k],
+                device_id={"tp": other},
+                device_id_type=MESH,
+            )
+            backs[k].start()
+
+    def turn(source):
+        for s in range(n_tp):
+            turned[:, s * rows : (s + 1) * rows] = source[s].T
+
+    def weight_grad(which, factor):
+        def step(at, carry):
+            here = pl.ds(pl.multiple_of(at * chunk, chunk), chunk)
+            result = dot(turned[here, :], factor[...].reshape(n_tp * rows, width))
+            grads[which, here, :] = result.astype(BF)
+            return carry
+
+        lax.fori_loop(0, pieces, step, 0)
+
+    core = lax.rem(me, 2)
+    half = width // 2
+    core_copies = []
+
+    def core_send(which):
+        copy = pltpu.make_async_remote_copy(
+            src_ref=grads.at[which, pl.ds(pl.multiple_of((1 - core) * half, half), half), :],
+            dst_ref=core_recv.at[which],
+            send_sem=core_ssem.at[which],
+            recv_sem=core_rsem.at[which],
+            device_id={"seq": flip(me, 1)},
+            device_id_type=MESH,
+        )
+        copy.start()
+        core_copies.append(copy)
+
+    turn(normed)
+    weight_grad(0, grad_gate)
+    core_send(0)
+    weight_grad(1, grad_up)
+    core_send(1)
+    turn(hidden)
+    weight_grad(2, cot_v)
+    core_send(2)
+
+    for k in (1, 2, 3, 0):
+        other = flip(plane, k)
+
+        def glu_step(at, carry, k=k, other=other):
+            cols = pl.ds(pl.multiple_of(at * chunk, chunk), chunk)
+            result = dot(hidden[other], down_v[:, cols])
+            if k == 0:
+                glu_own[:, cols] = result
+            else:
+                glu_send[k, :, cols] = result.astype(BF)
+            return carry
+
+        lax.fori_loop(0, pieces, glu_step, 0)
+        if k > 0:
+            glus[k] = pltpu.make_async_remote_copy(
+                src_ref=glu_send.at[k],
+                dst_ref=glu_recv.at[k],
+                send_sem=glu_ssem.at[k],
+                recv_sem=glu_rsem.at[k],
+                device_id={"tp": other},
+                device_id_type=MESH,
+            )
+            glus[k].start()
+
+    quarter = half // (n_seq // 2)
+    chip_copies = []
+    for which in range(3):
+        core_copies[which].wait_recv()
+        own = grads[which, pl.ds(pl.multiple_of(core * half, half), half), :]
+        halves[which] = (own.astype(F32) + core_recv[which].astype(F32)).astype(BF)
+        for k in CHIPS:
+            other = flip(me, k)
+            copy = pltpu.make_async_remote_copy(
+                src_ref=halves.at[which, pl.ds(pl.multiple_of(other // 2 * quarter, 16), quarter), :],
+                dst_ref=chip_recv.at[which, k // 2],
+                send_sem=chip_ssem.at[which, k // 2],
+                recv_sem=chip_rsem.at[which, k // 2],
+                device_id={"seq": other},
+                device_id_type=MESH,
+            )
+            copy.start()
+            chip_copies.append(copy)
+
+    for k in range(1, n_tp):
+        backs[k].wait_recv()
+    total = grad_normed[...]
+    for k in range(1, n_tp):
+        total = total + grad_recv[k].astype(F32)
+    value = scaled[...]
+    grad_vectors_out[0:1, :] = jnp.sum(total * value, axis=0, keepdims=True)
+    grad_vectors_out[1:2, :] = jnp.sum(total, axis=0, keepdims=True)
+    total = total * vectors[2:3, :]
+    first_mean = jnp.mean(total, axis=-1, keepdims=True)
+    second_mean = jnp.mean(total * value, axis=-1, keepdims=True)
+    total = cot_v[plane].astype(F32) + inverse[...] * (total - first_mean - value * second_mean)
+    grad_resid_out[...] = total
+    grad_branch[...] = total.T.astype(BF)
+
+    def keep_right(b, result):
+        grad_weights_out[0, pl.ds(b * block, block), :] = result.astype(BF)
+
+    def keep_left(g, result):
+        grad_weights_out[1, pl.ds(g * block, block), :] = result.astype(BF)
+
+    def keep_mixed(b, result):
+        grad_mixed[pl.ds(b * block, block), :] = result.astype(BF)
+
+    monarch_backward(
+        lambda g: grad_branch[pl.ds(g * block, block), :],
+        lambda b: mixed[pl.ds(b * block, block), :],
+        shuffled, right, left, middle, keep_right, keep_left, keep_mixed,
+    )
+    mine = pl.ds(pl.multiple_of(me * rows, rows), rows)
+    seq_copies = []
+    for k in SEQ_ORDER:
+        other = flip(me, k)
+        copy = pltpu.make_async_remote_copy(
+            src_ref=grad_mixed.at[pl.ds(pl.multiple_of(other * chans, 16), chans), :],
+            dst_ref=grad_mixed_all.at[:, mine],
+            send_sem=seq_send.at[k],
+            recv_sem=seq_recv.at[k],
+            device_id={"seq": other},
+            device_id_type=MESH,
+        )
+        copy.start()
+        seq_copies.append(copy)
+    grad_mixed_all[:, mine] = grad_mixed[pl.ds(pl.multiple_of(me * chans, 16), chans), :]
+
+    for k in range(1, n_tp):
+        glus[k].wait_recv()
+    total = resid[...] + glu_own[...]
+    for k in range(1, n_tp):
+        total = total + glu_recv[k].astype(F32)
+    out_rows[...] = total.astype(BF)
+    part = rows // n_tp
+    out_copies = []
+    for k in range(1, n_tp):
+        other = flip(plane, k)
+        copy = pltpu.make_async_remote_copy(
+            src_ref=out_rows.at[pl.ds(pl.multiple_of(other * part, part), part), :],
+            dst_ref=output_v.at[plane],
+            send_sem=out_send.at[k],
+            recv_sem=out_recv.at[k],
+            device_id={"tp": other},
+            device_id_type=MESH,
+        )
+        copy.start()
+        out_copies.append(copy)
+    output_v[plane] = out_rows[pl.ds(pl.multiple_of(plane * part, part), part), :]
+
+    chip = me // 2
+    for which in range(3):
+        for at in range(3):
+            chip_copies[3 * which + at].wait_recv()
+        total = halves[which, pl.ds(pl.multiple_of(chip * quarter, 16), quarter), :].astype(F32)
+        for k in CHIPS:
+            total = total + chip_recv[which, k // 2].astype(F32)
+        shard_out[which] = total.astype(BF)
+    for copy in seq_copies:
+        copy.wait()
+    grad_mixed_out[...] = grad_mixed_all[...]
+    for copy in out_copies:
+        copy.wait()
+    output_out[...] = output_v[...]
+    for k in range(1, n_tp):
+        gathers[k].wait_send()
+        backs[k].wait_send()
+        glus[k].wait_send()
+    for copy in core_copies + chip_copies:
+        copy.wait_send()
+
+
+def feed(mesh_shape, mixed, tokens, cot_rows, vectors, right, left, gate_w, up_w, down_w):
+    n_seq, n_tp = mesh_shape
+    _, rows, width = tokens.shape
+    chans, length = width // n_seq, rows * n_seq
+    part = rows // n_tp
+    shape = jax.ShapeDtypeStruct
+    dma = pltpu.SemaphoreType.DMA
+    return pl.pallas_call(
+        functools.partial(feed_kernel, n_seq, n_tp, (width, chans, length, rows)),
+        out_shape=(
+            shape((chans, length), BF),
+            shape((rows, width), F32),
+            shape((3, width // n_seq, width), BF),
+            shape((2, width, width // 4), BF),
+            shape((2, width), F32),
+            shape((n_tp, part, width), BF),
+        ),
+        in_specs=[vmem_spec(), any_spec(), any_spec(), vmem_spec(), vmem_spec(), vmem_spec(), any_spec(), any_spec(), any_spec()],
+        out_specs=(vmem_spec(),) * 6,
+        scratch_shapes=[
+            pltpu.VMEM((rows, width), BF),
+            pltpu.VMEM((n_tp, rows, width), BF),
+            pltpu.VMEM((width, width), BF),
+            pltpu.VMEM((width, width), BF),
+            pltpu.VMEM((width, width), BF),
+            pltpu.VMEM((width, rows), BF),
+            pltpu.VMEM((width, rows), F32),
+            pltpu.VMEM((rows, width), F32),
+            pltpu.VMEM((rows, width), F32),
+            pltpu.VMEM((rows, 1), F32),
+            pltpu.VMEM((n_tp, rows, width), BF),
+            pltpu.VMEM((n_tp, rows, width), BF),
+            pltpu.VMEM((n_tp, rows, width), F32),
+            pltpu.VMEM((n_tp, rows, width), BF),
+            pltpu.VMEM((n_tp, rows, width), BF),
+            pltpu.VMEM((rows, width), F32),
+            pltpu.VMEM((n_tp, rows, width), BF),
+            pltpu.VMEM((n_tp, rows, width), BF),
+            pltpu.VMEM((rows, width), F32),
+            pltpu.VMEM((n_tp, rows, width), BF),
+            pltpu.VMEM((n_tp, rows, width), BF),
+            pltpu.VMEM((width, n_tp * rows), BF),
+            pltpu.VMEM((3, width, width), BF),
+            pltpu.VMEM((3, width // 2, width), BF),
+            pltpu.VMEM((3, width // 2, width), BF),
+            pltpu.VMEM((3, n_seq // 2, width // n_seq, width), BF),
+            pltpu.VMEM((width, rows), BF),
+            pltpu.VMEM((width, rows), BF),
+            pltpu.VMEM((width, rows), BF),
+            pltpu.VMEM((chans, length), BF),
+            pltpu.VMEM((rows, width), BF),
+            pltpu.VMEM((n_tp, part, width), BF),
+            dma((5,)),
+            dma((n_tp,)), dma((n_tp,)), dma((n_tp,)), dma((n_tp,)), dma((n_tp,)), dma((n_tp,)), dma((n_tp,)), dma((n_tp,)),
+            dma((3,)), dma((3,)), dma((3, n_seq // 2)), dma((3, n_seq // 2)), dma((n_seq,)), dma((n_seq,)),
+        ],
+        compiler_params=pltpu.CompilerParams(collective_id=1, has_side_effects=True, vmem_limit_bytes=LIMIT),
+        name="feed",
+    )(mixed, tokens, cot_rows, vectors, right, left, gate_w, up_w, down_w)
+
+
+class Reduce:
+    def __init__(self, n_seq, n_tp, own, full, core_in, halves, chip_in, quarter, plane_in, send, recv):
+        self.own, self.full, self.core_in, self.halves = own, full, core_in, halves
+        self.chip_in, self.quarter, self.plane_in = chip_in, quarter, plane_in
+        self.send, self.recv, self.n_tp = send, recv, n_tp
+        rows, width = own.shape
+        self.rows, self.width = rows, width
+        self.per_chip, self.per_plane = rows // (n_seq // 2), rows // (n_seq // 2) // n_tp
+        self.me, self.plane = lax.axis_index("seq"), lax.axis_index("tp")
+        core = lax.rem(self.me, 2)
+        self.mine = pl.ds(pl.multiple_of(core * (width // 2), 128), width // 2)
+        self.theirs = pl.ds(pl.multiple_of((1 - core) * (width // 2), 128), width // 2)
+        self.started = []
+
+    def chip_rows(self, index):
+        return pl.ds(pl.multiple_of(index // 2 * self.per_chip, 16), self.per_chip)
+
+    def copy(self, source, target, at, where):
+        result = pltpu.make_async_remote_copy(
+            src_ref=source, dst_ref=target, send_sem=self.send.at[at], recv_sem=self.recv.at[at],
+            device_id=where, device_id_type=MESH,
+        )
+        result.start()
+        self.started.append(result)
+        return result
+
+    def start_core(self):
+        self.phase = [self.copy(self.own.at[:, self.theirs], self.core_in, 0, {"seq": flip(self.me, 1)})]
+
+    def arrived(self):
+        for copy in self.phase:
+            copy.wait_recv()
+        self.phase = []
+
+    def start_chip(self):
+        self.arrived()
+        self.halves[...] = (self.own[:, self.mine].astype(F32) + self.core_in[...].astype(F32)).astype(BF)
+        for k in CHIPS:
+            other = flip(self.me, k)
+            self.phase.append(
+                self.copy(self.halves.at[self.chip_rows(other), :], self.chip_in.at[k // 2], k // 2, {"seq": other})
+            )
+
+    def start_plane(self):
+        self.arrived()
+        total = self.halves[self.chip_rows(self.me), :].astype(F32)
+        for k in CHIPS:
+            total = total + self.chip_in[k // 2].astype(F32)
+        self.quarter[...] = total.astype(BF)
+        for k in range(1, self.n_tp):
+            other = flip(self.plane, k)
+            here = pl.ds(pl.multiple_of(other * self.per_plane, 16), self.per_plane)
+            self.phase.append(self.copy(self.quarter.at[here, :], self.plane_in.at[k], 3 + k, {"tp": other}))
+
+    def start_plane_back(self):
+        self.arrived()
+        here = pl.ds(pl.multiple_of(self.plane * self.per_plane, 16), self.per_plane)
+        total = self.quarter[here, :].astype(F32)
+        for k in range(1, self.n_tp):
+            total = total + self.plane_in[k].astype(F32)
+        rows = pl.ds(
+            pl.multiple_of(self.me // 2 * self.per_chip + self.plane * self.per_plane, 16), self.per_plane
+        )
+        self.full[rows, self.mine] = total.astype(BF)
+        spot = self.full.at[rows, self.mine]
+        for k in range(1, self.n_tp):
+            self.phase.append(self.copy(spot, spot, 6 + k, {"tp": flip(self.plane, k)}))
+
+    def start_chip_back(self):
+        self.arrived()
+        spot = self.full.at[self.chip_rows(self.me), self.mine]
+        for k in CHIPS:
+            self.phase.append(self.copy(spot, spot, 9 + k // 2, {"seq": flip(self.me, k)}))
+
+    def start_core_back(self):
+        self.arrived()
+        spot = self.full.at[:, self.mine]
+        self.phase.append(self.copy(spot, spot, 13, {"seq": flip(self.me, 1)}))
+
+    def finish(self):
+        self.arrived()
+        for copy in self.started:
+            copy.wait_send()
+
+
+def reduce_scratch(n_seq, n_tp, rows, width):
+    half, chip, plane = width // 2, rows // (n_seq // 2), rows // (n_seq // 2) // n_tp
+    return [
+        pltpu.VMEM((rows, width), BF),
+        pltpu.VMEM((rows, width), BF),
+        pltpu.VMEM((rows, half), BF),
+        pltpu.VMEM((rows, half), BF),
+        pltpu.VMEM((n_seq // 2, chip, half), BF),
+        pltpu.VMEM((chip, half), BF),
+        pltpu.VMEM((n_tp, plane, half), BF),
+        pltpu.SemaphoreType.DMA((14,)),
+        pltpu.SemaphoreType.DMA((14,)),
+    ]
+
+
+def back_kernel(n_seq, n_tp, dims, *refs):
+    (grad_mixed, columns, vectors, right, left, first, second, third, nyquist, shard, grad_weights, grad_vectors,
+     features, tokens, table, signals_in, conv_in, wave_in, taps_in, acts_in, normed_in, shuffled_in, resid_in) = refs[:23]
+    (ffn_out, tokens_out, late_out, early_out, small_out) = refs[23:28]
+    (table_v, signals, conv, wave, taps_v, acts, token_v, normed, shuffled, grad_resid, grad_short, query, value_v, grad_conv,
+     padded, back_wave, cross, sums, grad_signals, grad_proj, middle, grad_rows, grad_tok, grad_second, grad_first, grad_third,
+     local_sems, ffn_ssem, ffn_rsem, seq_send, seq_recv, tp_send, tp_recv) = refs[28:61]
+    width, chans, length, rows = dims
+    late = Reduce(n_seq, n_tp, *refs[61:70])
+    early = Reduce(n_seq, n_tp, *refs[70:79])
+    small = Reduce(n_seq, n_tp, *refs[79:88])
+    me, plane = lax.axis_index("seq"), lax.axis_index("tp")
+    entered = greet(n_seq, n_tp)
+    loads = [
+        pltpu.make_async_copy(source, target, local_sems.at[at])
+        for at, (source, target) in enumerate(
+            (
+                (signals_in, signals), (conv_in, conv), (table, table_v), (wave_in, wave), (taps_in, taps_v), (acts_in, acts),
+                (tokens.at[plane], token_v), (normed_in, normed), (shuffled_in, shuffled), (resid_in, grad_resid),
+            )
+        )
+    ]
+    for copy in loads:
+        copy.start()
+    half, quarter = width // 2, width // n_seq
+    own_rows = pl.ds(pl.multiple_of(lax.rem(me, 2) * half + me // 2 * quarter, 16), quarter)
+    entered()
+    ffn_copies = []
+    for which in range(3):
+        for k in CHIPS:
+            copy = pltpu.make_async_remote_copy(
+                src_ref=shard.at[which],
+                dst_ref=ffn_out.at[which, own_rows, :],
+                send_sem=ffn_ssem.at[which, k // 2],
+                recv_sem=ffn_rsem.at[which, k // 2],
+                device_id={"seq": flip(me, k)},
+                device_id_type=MESH,
+            )
+            copy.start()
+            ffn_copies.append(copy)
+    own_shard = pltpu.make_async_copy(shard, ffn_out.at[:, own_rows, :], local_sems.at[10])
+    own_shard.start()
+    sums[...] = jnp.zeros_like(sums)
+    small.own[...] = jnp.zeros_like(small.own)
+    early.own[...] = jnp.zeros_like(early.own)
+    loads[0].wait()
+    loads[1].wait()
+    step = 16
+    padded[pl.ds(chans, 128 - chans), :] = jnp.zeros((128 - chans, length), BF)
+
+    def short_step(at, carry):
+        here = pl.ds(pl.multiple_of(at * step, step), step)
+        shorted = []
+        for s in range(3):
+            value = signals[s, here, :].astype(F32)
+            shorted.append(
+                previous(value) * columns[here, 3 * s : 3 * s + 1]
+                + value * columns[here, 3 * s + 1 : 3 * s + 2]
+                + following(value) * columns[here, 3 * s + 2 : 3 * s + 3]
+            )
+        query[here, :] = shorted[0]
+        value_v[here, :] = shorted[2]
+        above = grad_mixed[here, :].astype(F32)
+        grad_short[1, here, :] = above * conv[here, :]
+        above = above * shorted[1]
+        grad_conv[here, :] = above
+        padded[here, :] = above.astype(BF)
+        sums[here, 9:10] = jnp.sum(above * shorted[0] * shorted[2], axis=1, keepdims=True)
+        sums[here, 10:11] = jnp.sum(above * sign_lanes(step, length), axis=1, keepdims=True)
+        return carry
+
+    lax.fori_loop(0, chans // step, short_step, 0)
+    for at in (2, 3, 4):
+        loads[at].wait()
+    chunk = 256
+    per = length // chunk
+
+    def wave_step(at, carry):
+        here = pl.ds(pl.multiple_of(at * chunk, chunk), chunk)
+        sign = sign_rows(chunk, 128)
+        index = lax.broadcasted_iota(jnp.int32, (chunk, 128), 0) + at * chunk
+        weight = jnp.where(index == 0, 0.5 / length, 1.0 / length)
+        cos_part = dot(table_v[0, here, :], padded[...], NT)
+        sin_part = dot(table_v[1, here, :], padded[...], NT)
+        tap_cos = taps_v[0, here, :].astype(F32)
+        tap_sin = taps_v[1, here, :].astype(F32)
+        back_wave[0, here, :] = (cos_part * tap_cos + sin_part * tap_sin).astype(BF)
+        back_wave[1, here, :] = (sin_part * tap_cos - cos_part * tap_sin).astype(BF)
+        wave_cos = wave[0, here, :].astype(F32) * weight
+        wave_sin = wave[1, here, :].astype(F32) * weight
+        result = cos_part * wave_cos + sin_part * wave_sin
+        cross[0, here, 0:128] = result.astype(BF)
+        cross[0, here, 128:256] = (result * sign).astype(BF)
+        result = sin_part * wave_cos - cos_part * wave_sin
+        cross[1, here, 0:128] = result.astype(BF)
+        cross[1, here, 128:256] = (result * sign).astype(BF)
+        return carry
+
+    lax.fori_loop(0, per, wave_step, 0)
+
+    def product_step(at, carry):
+        here = pl.ds(pl.multiple_of(at * chunk, chunk), chunk)
+        result = dot(table_v[0, here, :], back_wave[0]) + dot(table_v[1, here, :], back_wave[1])
+        result = (
+            result.T[:chans]
+            + sign_lanes(chans, chunk) * (sums[:chans, 10:11] * nyquist[:, 1:2] * (0.5 / length))
+            + columns[:, 9:10] * grad_conv[:, here]
+        )
+        grad_short[0, :, here] = result * value_v[:, here]
+        grad_short[2, :, here] = result * query[:, here]
+        return carry
+
+    lax.fori_loop(0, per, product_step, 0)
+
+    def signal_step(at, carry):
+        here = pl.ds(pl.multiple_of(at * step, step), step)
+        for s in range(3):
+            above = grad_short[s, here, :]
+            value = signals[s, here, :].astype(F32)
+            before, after = previous(above), following(above)
+            grad_signals[s, here, :] = (
+                after * columns[here, 3 * s : 3 * s + 1]
+                + above * columns[here, 3 * s + 1 : 3 * s + 2]
+                + before * columns[here, 3 * s + 2 : 3 * s + 3]
+            ).astype(BF)
+            sums[here, 3 * s : 3 * s + 1] = jnp.sum(after * value, axis=1, keepdims=True)
+            sums[here, 3 * s + 1 : 3 * s + 2] = jnp.sum(above * value, axis=1, keepdims=True)
+            sums[here, 3 * s + 2 : 3 * s + 3] = jnp.sum(before * value, axis=1, keepdims=True)
+        return carry
+
+    lax.fori_loop(0, chans // step, signal_step, 0)
+    mine = pl.ds(pl.multiple_of(me * rows, rows), rows)
+    seq_copies = []
+    for k in SEQ_ORDER:
+        other = flip(me, k)
+        for s in range(3):
+            copy = pltpu.make_async_remote_copy(
+                src_ref=grad_signals.at[s, :, pl.ds(pl.multiple_of(other * rows, rows), rows)],
+                dst_ref=grad_proj.at[pl.ds(pl.multiple_of(s * width + me * chans, 16), chans), :],
+                send_sem=seq_send.at[k, s],
+                recv_sem=seq_recv.at[k, s],
+                device_id={"seq": other},
+                device_id_type=MESH,
+            )
+            copy.start()
+            seq_copies.append(copy)
+    for s in range(3):
+        grad_proj[pl.ds(pl.multiple_of(s * width + me * chans, 16), chans), :] = grad_signals[s, :, mine]
+
+    loads[5].wait()
+    tap_total = jnp.broadcast_to(sums[:, 10:11], (128, 128)).T[0:1, :]
+    pad_nyquist = jnp.concatenate([nyquist[:, 0:1], jnp.zeros((128 - chans, 1), F32)], axis=0)
+    tap_total = tap_total * jnp.broadcast_to(pad_nyquist, (128, 128)).T[0:1, :] * (0.5 / length)
+    grad_second[...] = jnp.zeros_like(grad_second)
+    grad_first[...] = jnp.zeros_like(grad_first)
+    grad_third[...] = jnp.zeros_like(grad_third)
+
+    def filter_step(at, carry):
+        here = pl.ds(pl.multiple_of(at * chunk, chunk), chunk)
+        result = dot(table_v[0, here, :], cross[0]) + dot(table_v[1, here, :], cross[1])
+        sign = sign_rows(chunk, 128)
+        for part in range(2):
+            above = (result[:, part * 128 : (part + 1) * 128] + sign * tap_total) * (length**-0.5)
+            if part == 1:
+                index = lax.broadcasted_iota(jnp.int32, above.shape, 0) + at * chunk
+                above = jnp.where(index == 0, 0.0, above)
+            above = above.astype(BF)
+            spot = pl.ds(pl.multiple_of(part * length + at * chunk, chunk), chunk)
+            grad_third[...] += dot(above, acts[2, spot, :], TN)
+            below = (dot(above, third[...], NT) * acts[3, spot, :].astype(F32)).astype(BF)
+            grad_second[...] += dot(acts[0, spot, :], below, TN)
+            below = (dot(below, second[...], NT) * acts[1, spot, :].astype(F32)).astype(BF)
+            grad_first[...] += dot(features[spot, :], below, TN)
+        return carry
+
+    lax.fori_loop(0, per, filter_step, 0)
+    early.own[:, 0:384] = jnp.concatenate([grad_weights[0], grad_weights[1]], axis=1)
+    early.own[pl.ds(pl.multiple_of(me * chans, 16), chans), 384:512] = grad_third[:chans, :].astype(BF)
+    small.own[0:128, 0:128] = grad_second[...].astype(BF)
+    small.own[128:136, 0:128] = (grad_first[0:8, :] + grad_first[8:16, :]).astype(BF)
+    small.own[pl.ds(pl.multiple_of(me * 16, 16), 16), 128:256] = sums[...].T[0:16, :].astype(BF)
+    early.start_core()
+    for copy in ffn_copies:
+        copy.wait_recv()
+    own_shard.wait()
+    own_half = pl.ds(pl.multiple_of(lax.rem(me, 2) * half, half), half)
+    ffn_last = []
+    for which in range(3):
+        copy = pltpu.make_async_remote_copy(
+            src_ref=ffn_out.at[which, own_half, :],
+            dst_ref=ffn_out.at[which, own_half, :],
+            send_sem=ffn_ssem.at[which, 0],
+            recv_sem=ffn_rsem.at[which, 0],
+            device_id={"seq": flip(me, 1)},
+            device_id_type=MESH,
+        )
+        copy.start()
+        ffn_last.append(copy)
+    early.start_chip()
+
+    for at in range(6, 10):
+        loads[at].wait()
+    value = token_v[...].astype(F32)
+    shifted = value - jnp.mean(value, axis=-1, keepdims=True)
+    inverse = lax.rsqrt(jnp.mean(shifted * shifted, axis=-1, keepdims=True) + 1e-05)
+    scaled = shifted * inverse
+
+    groups = right.shape[0]
+    block = width // groups
+    fan = left.shape[2]
+    for copy in seq_copies:
+        copy.wait_recv()
+
+    def keep_left(g, result):
+        late.own[pl.ds(g * block, block), 0:512] = result[:, 0:512].astype(BF)
+        middle_left[g] = result[:, 512:576].astype(BF)
+
+    def keep_right(b, result):
+        late.own[pl.ds(b * block, block), 512:768] = jnp.concatenate([middle_left[b], result.astype(BF)], axis=1)
+
+    def keep_rows(b, result):
+        grad_rows[pl.ds(b * block, block), :] = result
+
+    middle_left = {}
+    monarch_backward(
+        lambda g: grad_proj[pl.ds(g * fan, fan), :],
+        lambda b: normed[pl.ds(b * block, block), :],
+        shuffled, right, left, middle, keep_right, keep_left, keep_rows,
+    )
+    late.start_core()
+    early.start_plane()
+    total = grad_rows[...].T
+    norm_grads = [jnp.sum(total * scaled, axis=0, keepdims=True), jnp.sum(total, axis=0, keepdims=True)]
+    total = total * vectors[0:1, :]
+    first_mean = jnp.mean(total, axis=-1, keepdims=True)
+    second_mean = jnp.mean(total * scaled, axis=-1, keepdims=True)
+    total = grad_resid[...] + inverse * (total - first_mean - scaled * second_mean)
+    grad_tok[...] = total.astype(BF)
+    norm_grads += [grad_vectors[0:1, :], grad_vectors[1:2, :]]
+    lines = []
+    for line in norm_grads:
+        for at in range(width // 128):
+            lines.append(line[:, at * 128 : (at + 1) * 128])
+    small.own[128:160, 128:256] = jnp.concatenate(lines + [jnp.zeros((8, 128), F32)], axis=0).astype(BF)
+    small.start_core()
+    tok_copies = []
+    for k in range(1, n_tp):
+        copy = pltpu.make_async_remote_copy(
+            src_ref=grad_tok,
+            dst_ref=tokens_out.at[plane],
+            send_sem=tp_send.at[k],
+            recv_sem=tp_recv.at[k],
+            device_id={"tp": flip(plane, k)},
+            device_id_type=MESH,
+        )
+        copy.start()
+        tok_copies.append(copy)
+    own_tok = pltpu.make_async_copy(grad_tok, tokens_out.at[plane], local_sems.at[11])
+    own_tok.start()
+    late.start_chip()
+    small.start_chip()
+    early.start_plane_back()
+    late.start_plane()
+    small.start_plane()
+    early.start_chip_back()
+    late.start_plane_back()
+    small.start_plane_back()
+    early.start_core_back()
+    late.start_chip_back()
+    small.start_chip_back()
+    late.start_core_back()
+    small.start_core_back()
+    early.finish()
+    early_out[...] = early.full[...]
+    small.finish()
+    small_out[...] = small.full[...]
+    late.finish()
+    late_out[...] = late.full[...]
+    for copy in ffn_copies + seq_copies:
+        copy.wait_send()
+    for copy in ffn_last + tok_copies:
+        copy.wait()
+    own_tok.wait()
+
+
+def back(mesh_shape, *operands):
+    n_seq, n_tp = mesh_shape
+    tokens = operands[13]
+    _, rows, width = tokens.shape
+    chans, length = width // n_seq, rows * n_seq
+    shape = jax.ShapeDtypeStruct
+    dma = pltpu.SemaphoreType.DMA
+    return pl.pallas_call(
+        functools.partial(back_kernel, n_seq, n_tp, (width, chans, length, rows)),
+        out_shape=(
+            shape((3, width, width), BF),
+            shape((n_tp, rows, width), BF),
+            shape((width, width), BF),
+            shape((width, 512), BF),
+            shape((256, 256), BF),
+        ),
+        in_specs=[vmem_spec()] * 13 + [any_spec()] * 10,
+        out_specs=(any_spec(), any_spec(), vmem_spec(), vmem_spec(), vmem_spec()),
+        scratch_shapes=[
+            pltpu.VMEM((2, length, length), BF),
+            pltpu.VMEM((3, chans, length), BF),
+            pltpu.VMEM((chans, length), F32),
+            pltpu.VMEM((2, length, 128), BF),
+            pltpu.VMEM((2, length, 128), BF),
+            pltpu.VMEM((4, 2 * length, 128), BF),
+            pltpu.VMEM((rows, width), BF),
+            pltpu.VMEM((width, rows), BF),
+            pltpu.VMEM((width, rows), BF),
+            pltpu.VMEM((rows, width), F32),
+            pltpu.VMEM((3, chans, length), F32),
+            pltpu.VMEM((chans, length), F32),
+            pltpu.VMEM((chans, length), F32),
+            pltpu.VMEM((chans, length), F32),
+            pltpu.VMEM((128, length), BF),
+            pltpu.VMEM((2, length, 128), BF),
+            pltpu.VMEM((2, length, 256), BF),
+            pltpu.VMEM((128, 128), F32),
+            pltpu.VMEM((3, chans, length), BF),
+            pltpu.VMEM((3 * width, rows), BF),
+            pltpu.VMEM((width, rows), BF),
+            pltpu.VMEM((width, rows), F32),
+            pltpu.VMEM((rows, width), BF),
+            pltpu.VMEM((128, 128), F32),
+            pltpu.VMEM((16, 128), F32),
+            pltpu.VMEM((128, 128), F32),
+            dma((12,)),
+            dma((3, n_seq // 2)), dma((3, n_seq // 2)), dma((n_seq, 3)), dma((n_seq, 3)), dma((n_tp,)), dma((n_tp,)),
+        ]
+        + reduce_scratch(n_seq, n_tp, width, width)
+        + reduce_scratch(n_seq, n_tp, width, 512)
+        + reduce_scratch(n_seq, n_tp, 256, 256),
+        compiler_params=pltpu.CompilerParams(collective_id=2, has_side_effects=True, vmem_limit_bytes=LIMIT),
+        name="back",
+    )(*operands)
+
+
+def fast_body(
+    tokens,
+    norm_gain,
+    norm_bias,
+    in_right,
+    in_left,
+    short_kernel,
+    filter_first,
+    filter_second,
+    filter_third,
+    conv_bias,
+    out_right,
+    out_left,
+    ffn_gain,
+    ffn_bias,
+    gate_weight,
+    up_weight,
+    down_weight,
+    cotangent,
+):
+    n_seq, n_tp = lax.axis_size("seq"), lax.axis_size("tp")
+    _, rows, width = tokens.shape
+    chans, length = width // n_seq, rows * n_seq
+    shape = (n_seq, n_tp)
+    table, features = (jnp.asarray(array) for array in constants(length))
+    vectors, columns, first, third = prepare(
+        tokens, norm_gain, norm_bias, ffn_gain, ffn_bias, short_kernel, filter_first, filter_third, conv_bias
+    )
+    mixed, signals, conv, wave, taps, nyquist, acts, normed, shuffled, cot_rows = front(
+        shape, tokens, cotangent, table, vectors, in_right, in_left, columns, features, first, filter_second, third
+    )
+    grad_mixed, grad_resid, shard, grad_weights, grad_vectors, output = feed(
+        shape, mixed, tokens, cot_rows, vectors, out_right, out_left, gate_weight, up_weight, down_weight
+    )
+    ffn, grad_tokens, late, early, small = back(
+        shape, grad_mixed, columns, vectors, in_right, in_left, first, filter_second, third, nyquist, shard, grad_weights,
+        grad_vectors, features, tokens, table, signals, conv, wave, taps, acts, normed, shuffled, grad_resid,
+    )
+    ffn, late, early, small = (array.astype(F32) for array in (ffn, late, early, small))
+    channel = small[:128, 128:].reshape(n_seq, 16, 128)[:, :10, :chans]
+    lines = small[128:152, 128:].reshape(4, width)
+    return (
+        output,
+        grad_tokens.astype(F32),
+        lines[0],
+        lines[1],
+        late[:, 576:].reshape(in_right.shape),
+        late[:, :576].reshape(in_left.shape),
+        channel[:, :9].reshape(n_seq, 3, 3, chans).transpose(1, 0, 3, 2).reshape(3, width, 3),
+        small[128:133, :128],
+        small[:128, :128],
+        early[:, 384:].T,
+        channel[:, 9].reshape(width),
+        early[:, :192].reshape(out_right.shape),
+        early[:, 192:384].reshape(out_left.shape),
+        lines[2],
+        lines[3],
+        ffn[0],
+        ffn[1],
+        ffn[2],
+    )
+
+
 highest = lax.Precision.HIGHEST
 
 
@@ -809,262 +1664,6 @@
     )
 
 
-def fast_body(
-    tokens,
-    norm_gain,
-    norm_bias,
-    in_right,
-    in_left,
-    short_kernel,
-    filter_first,
-    filter_second,
-    filter_third,
-    conv_bias,
-    out_right,
-    out_left,
-    ffn_gain,
-    ffn_bias,
-    gate_weight,
-    up_weight,
-    down_weight,
-    cotangent,
-):
-    seq_count, pos_count, model_width = tokens.shape
-    row_count = seq_count * pos_count
-    axis_count = lax.axis_size("seq")
-    my_index = lax.axis_index("seq")
-    chan_count = model_width // axis_count
-    seq_length = pos_count * axis_count
-    part_rows = cotangent.shape[1]
-    tp_index = lax.axis_index("tp")
-    tp_count = lax.axis_size("tp")
-    chan_start = my_index * chan_count
-    mix_count = seq_count // tp_count
-    mix_tokens = lax.dynamic_slice_in_dim(tokens, tp_index * mix_count, mix_count, 0)
-    mix_rows = mix_count * pos_count
-    flat = mix_tokens.reshape(mix_rows, model_width).astype(jnp.float32)
-    normed, scaled_one, inverse_one = norm_forward(flat, norm_gain, norm_bias)
-    normed_low = normed.astype(jnp.bfloat16)
-    table, features = constants(seq_length)
-    vectors, columns, first_pair, third_pad = prepare(
-        tokens, norm_gain, norm_bias, ffn_gain, ffn_bias, short_kernel, filter_first, filter_third, conv_bias
-    )
-    (mixed_t, signal_t, conv_t, wave, taps_wave, nyquist, acts, normed_t, shuffled_t, cot_rows) = front(
-        (axis_count, tp_count), tokens, cotangent, jnp.asarray(table), vectors, in_right, in_left, columns,
-        jnp.asarray(features), first_pair, filter_second, third_pad
-    )
-    normed_low = normed_t.T
-    shuffled_in = shuffled_t.T.reshape(mix_rows, 4, -1)
-    channels = signal_t[:, :, None, :]
-    signals = channels.astype(jnp.float32)
-    kernel = lax.dynamic_slice_in_dim(short_kernel, chan_start, chan_count, 1).astype(jnp.float32)
-    tap_zero = kernel[:, :, 0][:, :, None, None]
-    tap_one = kernel[:, :, 1][:, :, None, None]
-    tap_two = kernel[:, :, 2][:, :, None, None]
-    padded = jnp.pad(signals, ((0, 0), (0, 0), (0, 0), (1, 1)))
-    shorted = padded[..., :-2] * tap_zero + padded[..., 1:-1] * tap_one + padded[..., 2:] * tap_two
-    first_f = filter_first.astype(jnp.float32)
-    second_f = filter_second.astype(jnp.float32)
-    third_cols = lax.dynamic_slice_in_dim(filter_third, chan_start, chan_count, 1).astype(
-        jnp.float32
-    )
-    bias_cols = lax.dynamic_slice_in_dim(conv_bias, chan_start, chan_count, 0)[:, None, None]
-    product = shorted[0] * shorted[2]
-    product_pad = jnp.pad(product, ((0, 0), (0, 0), (0, seq_length)))
-    spec_real, spec_imag = spectrum_of(product_pad)
-    convolved = conv_t[:, None, :]
-    mixed_rows = mixed_t.T
-    shuffled_out, branch = rows_monarch_forward(mixed_rows, out_right, out_left)
-    residual_mine = (flat + branch).reshape(mix_count, pos_count, model_width)
-    residual = lax.all_gather(residual_mine, "tp", axis=0, tiled=True)
-    part_resid = lax.dynamic_slice_in_dim(residual, tp_index * part_rows, part_rows, 1)
-    normed_two, scaled_two, inverse_two = norm_forward(part_resid, ffn_gain, ffn_bias)
-    normed_rows = lax.all_gather(normed_two.astype(jnp.bfloat16), "tp", axis=1, tiled=True).reshape(
-        row_count, model_width
-    )
-    gate = jnp.dot(normed_rows, gate_weight, preferred_element_type=jnp.float32)
-    upward = jnp.dot(normed_rows, up_weight, preferred_element_type=jnp.float32)
-    sigma = jax.nn.sigmoid(gate)
-    hidden_low = (gate * sigma * upward).astype(jnp.bfloat16)
-    partial_down = jnp.dot(hidden_low, down_weight, preferred_element_type=jnp.float32).reshape(
-        seq_count, pos_count, model_width
-    )
-    glu_part = lax.psum_scatter(
-        partial_down.astype(jnp.bfloat16), "tp", scatter_dimension=1, tiled=True
-    ).astype(jnp.float32)
-    output = (part_resid + glu_part).astype(jnp.bfloat16)
-    grad_out_rows = cot_rows.reshape(row_count, model_width)
-    grad_hidden = jnp.dot(grad_out_rows, down_weight.T, preferred_element_type=jnp.float32)
-    grad_gate = (grad_hidden * upward * (sigma + gate * sigma * (1.0 - sigma))).astype(jnp.bfloat16)
-    grad_up = (grad_hidden * gate * sigma).astype(jnp.bfloat16)
-    grad_down_w = jnp.dot(hidden_low.T, grad_out_rows, preferred_element_type=jnp.float32)
-    grad_gate_w = jnp.dot(normed_rows.T, grad_gate, preferred_element_type=jnp.float32)
-    grad_up_w = jnp.dot(normed_rows.T, grad_up, preferred_element_type=jnp.float32)
-    grad_normed = jnp.dot(grad_gate, gate_weight.T, preferred_element_type=jnp.float32) + jnp.dot(
-        grad_up, up_weight.T, preferred_element_type=jnp.float32
-    )
-    grad_normed_part = lax.psum_scatter(
-        grad_normed.reshape(seq_count, pos_count, model_width),
-        "tp",
-        scatter_dimension=1,
-        tiled=True,
-    )
-    grad_in_two, grad_gain_two, grad_bias_two = norm_backward(
-        grad_normed_part, scaled_two, inverse_two, ffn_gain
-    )
-    gain_total = lax.psum((grad_gain_two, grad_bias_two), ("seq", "tp"))
-    grad_resid_part = cotangent.astype(jnp.float32) + grad_in_two
-    grad_resid = lax.all_gather(
-        grad_resid_part.astype(jnp.bfloat16), "tp", axis=1, tiled=True
-    ).astype(grad_resid_part.dtype)
-    grad_resid_mix = lax.dynamic_slice_in_dim(
-        grad_resid, tp_index * mix_count, mix_count, 0
-    ).reshape(mix_rows, model_width)
-    grad_mixed_rows, grad_out_right, grad_out_left = rows_monarch_backward(
-        grad_resid_mix.astype(jnp.bfloat16), mixed_rows, shuffled_out, out_right, out_left
-    )
-    grad_mixed_low = (
-        grad_mixed_rows.astype(jnp.bfloat16)
-        .reshape(mix_count, pos_count, model_width)
-        .transpose(2, 0, 1)
-    )
-    grad_mixed = lax.all_to_all(
-        grad_mixed_low, "seq", split_axis=0, concat_axis=2, tiled=True
-    ).astype(jnp.float32)
-    grad_conv = grad_mixed * shorted[1]
-    grad_key = grad_mixed * convolved
-    again = lax.optimization_barrier((first_f, second_f, third_cols))
-    kept = filter_parts(again[0], again[1], again[2], seq_length)
-    filt_real = kept[6][:, None]
-    filt_imag = kept[7][:, None]
-    features, pre_one, act_one, pre_two, act_two, tap_mask = (
-        kept[0],
-        kept[1],
-        kept[2],
-        kept[3],
-        kept[4],
-        kept[5],
-    )
-    grad_pad = jnp.pad(grad_conv, ((0, 0), (0, 0), (0, seq_length)))
-    grad_spec_real, grad_spec_imag = spectrum_of(grad_pad)
-    back_real = grad_spec_real * filt_real + grad_spec_imag * filt_imag
-    back_imag = grad_spec_imag * filt_real - grad_spec_real * filt_imag
-    grad_product = signal_of(back_real, back_imag)[..., :seq_length] + bias_cols * grad_conv
-    grad_bias_cols = jnp.sum(grad_conv * product, axis=(1, 2))
-    taps_real = jnp.sum(grad_spec_real * spec_real + grad_spec_imag * spec_imag, axis=1)
-    taps_imag = jnp.sum(grad_spec_imag * spec_real - grad_spec_real * spec_imag, axis=1)
-    grad_taps = signal_of(taps_real, taps_imag)
-    grad_pre = grad_taps.T * tap_mask
-    grad_third_cols = jnp.dot(act_two.T, grad_pre, precision=highest)
-    grad_pre_two = jnp.dot(grad_pre, third_cols.T, precision=highest) * jnp.cos(pre_two)
-    grad_second = jnp.dot(act_one.T, grad_pre_two, precision=highest)
-    grad_pre_one = jnp.dot(grad_pre_two, second_f.T, precision=highest) * jnp.cos(pre_one)
-    grad_first = jnp.dot(features.T, grad_pre_one, precision=highest)
-    grad_shorted = jnp.stack([grad_product * shorted[2], grad_key, grad_product * shorted[0]])
-    grad_short_pad = jnp.pad(grad_shorted, ((0, 0), (0, 0), (0, 0), (1, 1)))
-    grad_signals = (
-        grad_short_pad[..., 2:] * tap_zero
-        + grad_short_pad[..., 1:-1] * tap_one
-        + grad_short_pad[..., :-2] * tap_two
-    )
-    grad_kernel = jnp.stack(
-        [
-            jnp.sum(grad_shorted * padded[..., :-2], axis=(2, 3)),
-            jnp.sum(grad_shorted * padded[..., 1:-1], axis=(2, 3)),
-            jnp.sum(grad_shorted * padded[..., 2:], axis=(2, 3)),
-        ],
-        axis=-1,
-    )
-    grad_proj = lax.all_to_all(
-        grad_signals.astype(jnp.bfloat16), "seq", split_axis=3, concat_axis=1, tiled=True
-    )
-    grad_proj_rows = grad_proj.transpose(2, 3, 0, 1).reshape(mix_rows, 3 * model_width)
-    grad_normed_one, grad_in_right, grad_in_left = rows_monarch_backward(
-        grad_proj_rows, normed_low, shuffled_in, in_right, in_left
-    )
-    grad_in_one, grad_gain_one, grad_bias_one = norm_backward(
-        grad_normed_one, scaled_one, inverse_one, norm_gain
-    )
-    grad_mine = (grad_resid_mix + grad_in_one).reshape(mix_count, pos_count, model_width)
-    short_full = lax.dynamic_update_slice_in_dim(
-        jnp.zeros(short_kernel.shape, jnp.float32), grad_kernel, chan_start, 1
-    )
-    third_full = lax.dynamic_update_slice_in_dim(
-        jnp.zeros(filter_third.shape, jnp.float32), grad_third_cols, chan_start, 1
-    )
-    bias_full = lax.dynamic_update_slice_in_dim(
-        jnp.zeros(conv_bias.shape, jnp.float32), grad_bias_cols, chan_start, 0
-    )
-    mixer_grads = (
-        grad_gain_one,
-        grad_bias_one,
-        grad_in_right,
-        grad_in_left,
-        short_full,
-        grad_first,
-        grad_second,
-        third_full,
-        bias_full,
-        grad_out_right,
-        grad_out_left,
-    )
-    grad_tokens = lax.all_gather(grad_mine.astype(jnp.bfloat16), "tp", axis=0, tiled=True).astype(
-        grad_mine.dtype
-    )
-    mixer_grads = (
-        lax.psum(mixer_grads[0].astype(jnp.bfloat16), "tp").astype(jnp.float32),
-        lax.psum(mixer_grads[1].astype(jnp.bfloat16), "tp").astype(jnp.float32),
-        lax.psum(mixer_grads[2].astype(jnp.bfloat16), "tp").astype(jnp.float32),
-        lax.psum(mixer_grads[3].astype(jnp.bfloat16), "tp").astype(jnp.float32),
-        lax.psum(mixer_grads[4].astype(jnp.bfloat16), "tp").astype(jnp.float32),
-        lax.psum(mixer_grads[5].astype(jnp.bfloat16), "tp").astype(jnp.float32),
-        lax.psum(mixer_grads[6].astype(jnp.bfloat16), "tp").astype(jnp.float32),
-        lax.psum(mixer_grads[7].astype(jnp.bfloat16), "tp").astype(jnp.float32),
-        lax.psum(mixer_grads[8].astype(jnp.bfloat16), "tp").astype(jnp.float32),
-        lax.psum(mixer_grads[9].astype(jnp.bfloat16), "tp").astype(jnp.float32),
-        lax.psum(mixer_grads[10].astype(jnp.bfloat16), "tp").astype(jnp.float32),
-    )
-    all_total = lax.psum(
-        (
-            mixer_grads[0],
-            mixer_grads[1],
-            mixer_grads[2],
-            mixer_grads[3],
-            mixer_grads[4],
-            mixer_grads[5],
-            mixer_grads[6],
-            mixer_grads[7],
-            mixer_grads[8],
-            mixer_grads[9],
-            mixer_grads[10],
-            grad_gate_w,
-            grad_up_w,
-            grad_down_w,
-        ),
-        "seq",
-    )
-    return (
-        output,
-        grad_tokens,
-        all_total[0],
-        all_total[1],
-        all_total[2],
-        all_total[3],
-        all_total[4],
-        all_total[5],
-        all_total[6],
-        all_total[7],
-        all_total[8],
-        all_total[9],
-        all_total[10],
-        gain_total[0],
-        gain_total[1],
-        all_total[11],
-        all_total[12],
-        all_total[13],
-    )
-
-
 def choose_body(mesh, *arrays):
     tokens = arrays[0]
     chans = tokens.shape[2] // mesh.shape["seq"]

time: 616 us -> 194 us (0.31)
  blocking collectives: 295 us -> 0 us
  Pallas kernels: 26.2 us -> 169 us
  matrix products: 94.4 us -> 0 us
  waiting for transfers between devices: 81.4 us -> 0 us
  local copies, waits for them, and re-layouts: 58.5 us -> 18.2 us
  other arithmetic: 32.8 us -> 5.57 us
  between operations: 15.4 us -> 0.76 us
  starting transfers between devices: 9.07 us -> 0 us
    psum x3 -> x0, blocking collectives: 226 us -> none  [the longest x1 164 us: fast_body(): lax.psum((mixer_grads[0], mixer_grads[1], mixer_grads[2], mixer_grads[3],...]
    pallas_call x0 -> x2, Pallas kernels: none -> 142 us  [the longest x1 77.9 us: back(): pl.pallas_call(functools.partial(back_kernel, n_seq, n_tp, (width, chans,...]
    dot_general x57 -> x0, matrix products: 94.4 us -> none  [the longest x7 10.8 us: complex_step(): jnp.einsum(form, imag_part, sin_table, precision=highest)]
    all_gather x3 -> x0, blocking collectives: 68.5 us -> none  [the longest x1 29 us: fast_body(): lax.all_gather(grad_resid_part.astype(jnp.bfloat16), 'tp', axis=1, tiled=...]
    all_gather x1 -> x0, waiting for transfers between devices: 36.1 us -> none  [fast_body(): residual = lax.all_gather(residual_mine, 'tp', axis=0, tiled=True)]
    reduce_scatter x2 -> x0, waiting for transfers between devices: 23.4 us -> none  [the longest x1 22.6 us: fast_body(): lax.psum_scatter(partial_down.astype(jnp.bfloat16), 'tp', scatter_dimensi...]
    unnamed x190 -> x15, local copies, waits for them, and re-layouts: 21.8 us -> 1.71 us
    all_to_all x2 -> x0, waiting for transfers between devices: 13.4 us -> none  [the longest x1 9.1 us: fast_body(): lax.all_to_all(grad_signals.astype(jnp.bfloat16), 'seq', split_axis=3, co...]
  transfers between devices with their start and end apart: 7 -> 0, of which waited for: 6 -> 0; matrix products, arithmetic and copies ran while one was open for 11% -> 0% of each run, Pallas kernels for 0% -> 0%
where the time goes in v2:
time: 194 us; the launch traced here: 193 us
  Pallas kernels  169 us (87%)
  local copies, waits for them, and re-layouts  18.2 us (9%)
  other arithmetic  5.57 us (3%)
    pallas_call x1, Pallas kernels, back(): pl.pallas_call(functools.partial(back_kernel, n_seq, n_tp, (width, chans,...  77.9 us
    pallas_call x1, Pallas kernels, feed(): pl.pallas_call(functools.partial(feed_kernel, n_seq, n_tp, (width, chans,...  64.6 us
    pallas_call x1, Pallas kernels, front(): pl.pallas_call(functools.partial(front_kernel, n_seq, n_tp, (width, chans...  26.4 us

profile of v2, /device:TPU:0, one launch (start us, length us, event | category | flops | bytes accessed | tf_op | source)
XLA Modules:
  0.0 193.4 jit_solution(10872064322301856183)
XLA Ops:
  0.7 0.8 convert_bitcast_fusion
  1.5 0.8 dynamic-slice_bitcast_fusion
  2.3 0.1 pad.14.clone
  2.3 0.1 maximum_maximum_fusion
  2.4 0.7 copy.46.refs_6_.refs_1_
  3.1 0.1 constant_dynamic-slice_fusion
  3.2 0.6 pad.9.refs_10_.refs_7_
  3.8 0.7 stack.18
  4.5 0.7 stack.19
  5.2 0.7 stack.20
  5.9 0.7 stack.21
  6.6 0.6 stack.23.refs_3_.refs_2_
  7.2 0.7 pad.8
  7.9 0.6 pad_maximum_fusion.refs_8_.refs_5_
  8.5 26.4 %front.1 = (bf16[768,128]{1,0:T(8,128)(2,1)}, bf16[3,96,1024]{2,1,0:T(8,128)(2,1)}, f32[96,1024]{1,0:T(8,128)}, bf16[2,1024,128]{2,1,0:T(8,128)(2,1)}, bf16[2,10...) custom-call(bf16[4,128,768]{2,1,0:T(8,128)(2,1)} %refs_13_.1, ...), custom_call_target="tpu_custom_call" | custom-call | tf_op jit(solution)/shard_map/front/pallas_call | solution.py:316
  34.9 64.6 %feed.1 = (bf16[96,1024]{1,0:T(8,128)(2,1)}, f32[128,768]{1,0:T(8,128)}, bf16[3,96,768]{2,1,0:T(8,128)(2,1)}, bf16[2,768,192]{2,1,0:T(8,128)(2,1)}, f32[2,768]{1,0:T(2,128)}, /*index=5*/bf16[4,32,768]{2,1,0:T(8,128)(2,1)}) custom-call(bf16[768,128]{1,0:T(8,128)(2,1)} %get-tuple-element.39.refs_0_, bf16[4,128,768]{2,1,0:T(8,128)(2,1)} %refs_13_.1, ...), custom_call_target="tpu_custom_call" | custom-call | tf_op jit(solution)/shard_map/feed/pallas_call | solution.py:699
  99.5 77.9 %back.1 = (bf16[3,768,768]{2,1,0:T(8,128)(2,1)}, bf16[4,128,768]{2,1,0:T(8,128)(2,1)}, bf16[768,768]{1,0:T(8,128)(2,1)}, bf16[768,512]{1,0:T(8,128)(2,1)}, bf16[256,256]{1,0:T(8,128)(2,1)}) custom-call(bf16[96,1024]{1,0:T(8,128)(2,1)} %get-tuple-element.42.refs_0_, f32[96,16]{1,0:T(8,128)} %copy.46.refs_6_.refs_1_, f32[8,768]{1,0:T(8,128)} %stack.23.refs_3_.refs_2_, ...), custom_call_target="tpu_custom_call" | custom-call | tf_op jit(solution)/shard_map/back/pallas_call | solution.py:1145
  177.3 2.6 %convert_element_type.24 = f32[3,768,768]{2,1,0:T(8,128)S(1)} convert(bf16[3,768,768]{2,1,0:T(8,128)(2,1)} %get-tuple-element.59) | non-fusion elementwise | flops 1769472 | bytes 10616832 | tf_op jit(solution)/shard_map/convert_element_type | solution.py:1232
  180.0 3.1 %slice_bitcast_fusion = (f32[768,768]{1,0:T(8,128)}, f32[768,768]{1,0:T(8,128)}, f32[768,768]{1,0:T(8,128)}) fusion(f32[3,768,768]{2,1,0:T(8,128)S(1)} %convert_element_type.24), kind=kLoop, calls=%fused_computation | loop fusion | bytes 14155776 | tf_op jit(solution)/shard_map/squeeze | solution.py:1253
  183.1 0.2 convert_element_type.23
  183.3 0.9 copy.49
  184.3 0.1 copy-done.2
  184.3 1.4 slice.83
  185.7 1.3 fusion
  187.1 1.3 convert_element_type.20
  188.3 1.1 slice.82
  189.4 0.6 slice_bitcast_fusion.4
  190.0 0.6 fusion.1
  190.7 0.7 reshape.78
  191.4 0.7 reshape_squeeze.3
  192.1 0.6 slice.86
  192.7 0.7 copy.52
  (18 shorter events, 0.1 us)
Async XLA Ops:
  0.7 2.5 %copy-start = (bf16[128,768]{1,0:T(8,128)(2,1)S(1)}, bf16[128,768]{1,0:T(8,128)(2,1)}, u32[]{:S(2)}) copy-start(bf16[128,768]{1,0:T(8,128)(2,1)} %param.28) | copy-start | bytes 589828
  179.9 3.1 %copy-start.1 = (bf16[768,512]{1,0:T(8,128)(2,1)S(1)}, bf16[768,512]{1,0:T(8,128)(2,1)}, u32[]{:S(2)}) copy-start(bf16[768,512]{1,0:T(8,128)(2,1)} %get-tuple-element.58) | copy-start | bytes 2359300
  183.1 1.3 copy-start.2
  185.7 1.3 copy-start.3
  187.1 2.3 %copy-start.4 = (bf16[256,256]{1,0:T(8,128)(2,1)S(1)}, bf16[256,256]{1,0:T(8,128)(2,1)}, u32[]{:S(2)}) copy-start(bf16[256,256]{1,0:T(8,128)(2,1)} %get-tuple-element.56) | copy-start | bytes 393220
  187.1 5.6 %copy-start.5 = (bf16[4,32,768]{2,1,0:T(8,128)(2,1)S(1)}, bf16[4,32,768]{2,1,0:T(8,128)(2,1)}, u32[]{:S(2)}) copy-start(bf16[4,32,768]{2,1,0:T(8,128)(2,1)} %get-tuple-element.143) | copy-start | bytes 589828

commit v3 on v2

--- a/solution.py
+++ b/solution.py
@@ -107,10 +107,12 @@
 
 
 def front_kernel(n_seq, n_tp, dims, *refs):
-    (tokens, cotangent, table, vectors, right, left, columns, features, first, second, third) = refs[:11]
-    (mixed_out, signals_out, conv_out, wave_out, taps_out, nyquist_out, acts_out, normed_out, shuffled_out, cot_out) = refs[11:21]
+    (tokens, cotangent, table, gain, bias, right, left, short, conv_bias, features, first, second, third) = refs[:13]
+    (mixed_out, signals_out, conv_out, wave_out, taps_out, nyquist_out, acts_out, normed_out, shuffled_out, cot_out,
+     columns_out, third_out) = refs[13:25]
     (token_v, table_v, normed, shuffled, projected, signals, acts, spread, taps_v, padded, product, keyed, wave, spectrum, conv,
-     mixed, mixed_rows, nyquist, totals, local_sems, seq_send, seq_recv, back_send, back_recv, tp_send, tp_recv) = refs[21:]
+     mixed, mixed_rows, nyquist, totals, columns, tall, turned, third_v,
+     local_sems, seq_send, seq_recv, back_send, back_recv, tp_send, tp_recv) = refs[25:]
     width, chans, length, rows = dims
     me, plane = lax.axis_index("seq"), lax.axis_index("tp")
     entered = greet(n_seq, n_tp)
@@ -122,7 +124,7 @@
     value = token_v[...].astype(F32)
     shifted = value - jnp.mean(value, axis=-1, keepdims=True)
     inverse = lax.rsqrt(jnp.mean(shifted * shifted, axis=-1, keepdims=True) + 1e-05)
-    value = shifted * inverse * vectors[0:1, :] + vectors[1:2, :]
+    value = shifted * inverse * gain[...].reshape(1, width) + bias[...].reshape(1, width)
     normed[...] = value.T.astype(BF)
     groups = right.shape[0]
     block = width // groups
@@ -173,6 +175,19 @@
     for copy in out_copies:
         copy.start()
 
+    own = pl.ds(pl.multiple_of(me * chans, 16), chans)
+    lines = [short[s].astype(F32) for s in range(3)]
+    lines += [conv_bias[...].reshape(1, width), jnp.zeros((6, width), F32)]
+    tall[...] = jnp.concatenate(lines, axis=0).T
+    columns[...] = tall[own, :]
+    columns_out[...] = columns[...]
+    turned[...] = third[...].T
+    third_v[pl.ds(0, chans), :] = turned[own, :]
+    third_v[pl.ds(chans, 128 - chans), :] = jnp.zeros((128 - chans, 128), BF)
+    third_out[...] = third_v[...]
+    lead = jnp.concatenate([first[...].astype(F32), jnp.zeros((3, 128), F32)], axis=0)
+    lead = jnp.concatenate([lead, lead], axis=0).astype(BF)
+
     chunk = 256
     per = length // chunk
     totals[...] = jnp.zeros_like(totals)
@@ -181,7 +196,7 @@
         def tap_step(at, carry, half=half):
             row = pl.multiple_of(half * length + at * chunk, chunk)
             here = pl.ds(row, chunk)
-            sine, cosine = sin_cos(dot(features[here, :], first[...]))
+            sine, cosine = sin_cos(dot(features[here, :], lead))
             high = sine.astype(BF)
             acts[0, here, :] = high
             acts[1, here, :] = cosine.astype(BF)
@@ -190,7 +205,7 @@
             high = sine.astype(BF)
             acts[2, here, :] = high
             acts[3, here, :] = cosine.astype(BF)
-            taps = dot(high, third[...]) * (length**-0.5)
+            taps = dot(high, third_v[...], NT) * (length**-0.5)
             if half == 1:
                 index = lax.broadcasted_iota(jnp.int32, taps.shape, 0) + at * chunk
                 taps = jnp.where(index == 0, 0.0, taps)
@@ -308,9 +323,9 @@
         copy.wait()
 
 
-def front(mesh_shape, tokens, cotangent, table, vectors, right, left, columns, features, first, second, third):
+def front(mesh_shape, *operands):
     n_seq, n_tp = mesh_shape
-    _, rows, width = tokens.shape
+    _, rows, width = operands[0].shape
     chans, length = width // n_seq, rows * n_seq
     shape = jax.ShapeDtypeStruct
     return pl.pallas_call(
@@ -326,9 +341,11 @@
             shape((width, rows), BF),
             shape((width, rows), BF),
             shape((n_tp, rows, width), BF),
+            shape((chans, 16), F32),
+            shape((128, 128), BF),
         ),
-        in_specs=[any_spec()] * 3 + [vmem_spec()] * 8,
-        out_specs=(vmem_spec(),) + (any_spec(),) * 9,
+        in_specs=[any_spec()] * 3 + [vmem_spec()] * 10,
+        out_specs=(vmem_spec(),) + (any_spec(),) * 9 + (vmem_spec(),) * 2,
         scratch_shapes=[
             pltpu.VMEM((rows, width), BF),
             pltpu.VMEM((2, length, length), BF),
@@ -349,6 +366,10 @@
             pltpu.VMEM((width, rows), BF),
             pltpu.VMEM((chans, 128), F32),
             pltpu.VMEM((1, 128), F32),
+            pltpu.VMEM((chans, 16), F32),
+            pltpu.VMEM((width, 16), F32),
+            pltpu.VMEM((width, 128), BF),
+            pltpu.VMEM((128, 128), BF),
             pltpu.SemaphoreType.DMA((12,)),
             pltpu.SemaphoreType.DMA((n_seq, 3)),
             pltpu.SemaphoreType.DMA((n_seq, 3)),
@@ -359,7 +380,7 @@
         ],
         compiler_params=pltpu.CompilerParams(collective_id=0, has_side_effects=True, vmem_limit_bytes=LIMIT),
         name="front",
-    )(tokens, cotangent, table, vectors, right, left, columns, features, first, second, third)
+    )(*operands)
 
 
 def split_table(values):
@@ -383,22 +404,6 @@
     return table, np.concatenate(split_table(features), axis=1)
 
 
-def prepare(tokens, norm_gain, norm_bias, ffn_gain, ffn_bias, short_kernel, filter_first, filter_third, conv_bias):
-    me = lax.axis_index("seq")
-    width = tokens.shape[2]
-    chans = width // lax.axis_size("seq")
-    vectors = jnp.stack([norm_gain, norm_bias, ffn_gain, ffn_bias] + [jnp.zeros_like(norm_gain)] * 4)
-    kernel = lax.dynamic_slice_in_dim(short_kernel, me * chans, chans, 1).astype(F32)
-    bias = lax.dynamic_slice_in_dim(conv_bias, me * chans, chans, 0)
-    columns = jnp.concatenate(
-        [kernel.transpose(1, 0, 2).reshape(chans, 9), bias[:, None], jnp.zeros((chans, 6), F32)], axis=1
-    )
-    lead = jnp.pad(filter_first, ((0, 3), (0, 0)))
-    first = jnp.concatenate([lead, lead], axis=0)
-    third = jnp.pad(lax.dynamic_slice_in_dim(filter_third, me * chans, chans, 1), ((0, 0), (0, 128 - chans)))
-    return vectors, columns, first, third
-
-
 def monarch_backward(upstream, operand, shuffled, right, left, middle, keep_right, keep_left, store):
     groups, width, _ = right.shape
     part = width // groups
@@ -418,12 +423,12 @@
 
 
 def feed_kernel(n_seq, n_tp, dims, *refs):
-    (mixed, tokens, cot_rows, vectors, right, left, gate_w, up_w, down_w) = refs[:9]
-    (grad_mixed_out, grad_resid_out, shard_out, grad_weights_out, grad_vectors_out, output_out) = refs[9:15]
+    (mixed, tokens, cot_rows, gain, bias, right, left, gate_w, up_w, down_w) = refs[:10]
+    (grad_mixed_out, grad_resid_out, shard_out, grad_weights_out, grad_vectors_out, output_out) = refs[10:16]
     (token_v, cot_v, gate_v, up_v, down_v, shuffled, branch, resid, scaled, inverse, normed, hidden, grad_hidden, grad_gate, grad_up,
      grad_normed, grad_send, grad_recv, glu_own, glu_send, glu_recv, turned, grads, core_recv, halves, chip_recv, grad_branch,
      middle, grad_mixed, grad_mixed_all, out_rows, output_v, local_sems, gather_send, gather_recv, back_send, back_recv, glu_ssem, glu_rsem,
-     out_send, out_recv, core_ssem, core_rsem, chip_ssem, chip_rsem, seq_send, seq_recv) = refs[15:]
+     out_send, out_recv, core_ssem, core_rsem, chip_ssem, chip_rsem, seq_send, seq_recv) = refs[16:]
     width, chans, length, rows = dims
     me, plane = lax.axis_index("seq"), lax.axis_index("tp")
     entered = greet(n_seq, n_tp)
@@ -450,7 +455,7 @@
     inverse[...] = lax.rsqrt(jnp.mean(shifted * shifted, axis=-1, keepdims=True) + 1e-05)
     value = shifted * inverse[...]
     scaled[...] = value
-    normed[plane] = (value * vectors[2:3, :] + vectors[3:4, :]).astype(BF)
+    normed[plane] = (value * gain[...].reshape(1, width) + bias[...].reshape(1, width)).astype(BF)
     entered()
     gathers = {}
     for k in range(1, n_tp):
@@ -608,7 +613,7 @@
     value = scaled[...]
     grad_vectors_out[0:1, :] = jnp.sum(total * value, axis=0, keepdims=True)
     grad_vectors_out[1:2, :] = jnp.sum(total, axis=0, keepdims=True)
-    total = total * vectors[2:3, :]
+    total = total * gain[...].reshape(1, width)
     first_mean = jnp.mean(total, axis=-1, keepdims=True)
     second_mean = jnp.mean(total * value, axis=-1, keepdims=True)
     total = cot_v[plane].astype(F32) + inverse[...] * (total - first_mean - value * second_mean)
@@ -689,7 +694,7 @@
         copy.wait_send()
 
 
-def feed(mesh_shape, mixed, tokens, cot_rows, vectors, right, left, gate_w, up_w, down_w):
+def feed(mesh_shape, mixed, tokens, cot_rows, gain, bias, right, left, gate_w, up_w, down_w):
     n_seq, n_tp = mesh_shape
     _, rows, width = tokens.shape
     chans, length = width // n_seq, rows * n_seq
@@ -706,7 +711,7 @@
             shape((2, width), F32),
             shape((n_tp, part, width), BF),
         ),
-        in_specs=[vmem_spec(), any_spec(), any_spec(), vmem_spec(), vmem_spec(), vmem_spec(), any_spec(), any_spec(), any_spec()],
+        in_specs=[vmem_spec(), any_spec(), any_spec()] + [vmem_spec()] * 4 + [any_spec()] * 3,
         out_specs=(vmem_spec(),) * 6,
         scratch_shapes=[
             pltpu.VMEM((rows, width), BF),
@@ -747,7 +752,7 @@
         ],
         compiler_params=pltpu.CompilerParams(collective_id=1, has_side_effects=True, vmem_limit_bytes=LIMIT),
         name="feed",
-    )(mixed, tokens, cot_rows, vectors, right, left, gate_w, up_w, down_w)
+    )(mixed, tokens, cot_rows, gain, bias, right, left, gate_w, up_w, down_w)
 
 
 class Reduce:
@@ -851,16 +856,16 @@
 
 
 def back_kernel(n_seq, n_tp, dims, *refs):
-    (grad_mixed, columns, vectors, right, left, first, second, third, nyquist, shard, grad_weights, grad_vectors,
-     features, tokens, table, signals_in, conv_in, wave_in, taps_in, acts_in, normed_in, shuffled_in, resid_in) = refs[:23]
-    (ffn_out, tokens_out, late_out, early_out, small_out) = refs[23:28]
+    (grad_mixed, columns, gain, right, left, second, third, nyquist, shard, grad_weights, grad_vectors,
+     features, tokens, table, signals_in, conv_in, wave_in, taps_in, acts_in, normed_in, shuffled_in, resid_in) = refs[:22]
+    (ffn_out, tokens_out, late_out, early_out, small_out) = refs[22:27]
     (table_v, signals, conv, wave, taps_v, acts, token_v, normed, shuffled, grad_resid, grad_short, query, value_v, grad_conv,
      padded, back_wave, cross, sums, grad_signals, grad_proj, middle, grad_rows, grad_tok, grad_second, grad_first, grad_third,
-     local_sems, ffn_ssem, ffn_rsem, seq_send, seq_recv, tp_send, tp_recv) = refs[28:61]
+     local_sems, ffn_ssem, ffn_rsem, seq_send, seq_recv, tp_send, tp_recv) = refs[27:60]
     width, chans, length, rows = dims
-    late = Reduce(n_seq, n_tp, *refs[61:70])
-    early = Reduce(n_seq, n_tp, *refs[70:79])
-    small = Reduce(n_seq, n_tp, *refs[79:88])
+    late = Reduce(n_seq, n_tp, *refs[60:69])
+    early = Reduce(n_seq, n_tp, *refs[69:78])
+    small = Reduce(n_seq, n_tp, *refs[78:87])
     me, plane = lax.axis_index("seq"), lax.axis_index("tp")
     entered = greet(n_seq, n_tp)
     loads = [
@@ -1019,7 +1024,7 @@
             above = above.astype(BF)
             spot = pl.ds(pl.multiple_of(part * length + at * chunk, chunk), chunk)
             grad_third[...] += dot(above, acts[2, spot, :], TN)
-            below = (dot(above, third[...], NT) * acts[3, spot, :].astype(F32)).astype(BF)
+            below = (dot(above, third[...]) * acts[3, spot, :].astype(F32)).astype(BF)
             grad_second[...] += dot(acts[0, spot, :], below, TN)
             below = (dot(below, second[...], NT) * acts[1, spot, :].astype(F32)).astype(BF)
             grad_first[...] += dot(features[spot, :], below, TN)
@@ -1083,7 +1088,7 @@
     early.start_plane()
     total = grad_rows[...].T
     norm_grads = [jnp.sum(total * scaled, axis=0, keepdims=True), jnp.sum(total, axis=0, keepdims=True)]
-    total = total * vectors[0:1, :]
+    total = total * gain[...].reshape(1, width)
     first_mean = jnp.mean(total, axis=-1, keepdims=True)
     second_mean = jnp.mean(total * scaled, axis=-1, keepdims=True)
     total = grad_resid[...] + inverse * (total - first_mean - scaled * second_mean)
@@ -1137,7 +1142,7 @@
 
 def back(mesh_shape, *operands):
     n_seq, n_tp = mesh_shape
-    tokens = operands[13]
+    tokens = operands[12]
     _, rows, width = tokens.shape
     chans, length = width // n_seq, rows * n_seq
     shape = jax.ShapeDtypeStruct
@@ -1151,7 +1156,7 @@
             shape((width, 512), BF),
             shape((256, 256), BF),
         ),
-        in_specs=[vmem_spec()] * 13 + [any_spec()] * 10,
+        in_specs=[vmem_spec()] * 12 + [any_spec()] * 10,
         out_specs=(any_spec(), any_spec(), vmem_spec(), vmem_spec(), vmem_spec()),
         scratch_shapes=[
             pltpu.VMEM((2, length, length), BF),
@@ -1191,6 +1196,89 @@
     )(*operands)
 
 
+def finish_kernel(width, chans, *refs):
+    (ffn, tokens, late, early, small) = refs[:5]
+    (grad_tokens, norm_gain, norm_bias, in_right, in_left, short, first, second, third, conv_bias, out_right, out_left,
+     ffn_gain, ffn_bias, gate, up, down) = refs[5:22]
+    (ffn_v, ffn_f, token_v, token_f, in_sems, out_sems) = refs[22:]
+    loads = [pltpu.make_async_copy(ffn.at[which], ffn_v.at[which], in_sems.at[which]) for which in range(3)]
+    loads.append(pltpu.make_async_copy(tokens, token_v, in_sems.at[3]))
+    for copy in loads:
+        copy.start()
+    stores = [
+        pltpu.make_async_copy(ffn_f.at[which], target, out_sems.at[which]) for which, target in enumerate((gate, up, down))
+    ]
+    stores.append(pltpu.make_async_copy(token_f, grad_tokens, out_sems.at[3]))
+    chunk = 64
+    for which in range(3):
+        loads[which].wait()
+
+        def step(at, carry, which=which):
+            here = pl.ds(pl.multiple_of(at * chunk, chunk), chunk)
+            ffn_f[which, here, :] = ffn_v[which, here, :].astype(F32)
+            return carry
+
+        lax.fori_loop(0, width // chunk, step, 0)
+        stores[which].start()
+    loads[3].wait()
+
+    def token_step(at, carry):
+        token_f[at] = token_v[at].astype(F32)
+        return carry
+
+    lax.fori_loop(0, token_v.shape[0], token_step, 0)
+    stores[3].start()
+    groups, block, _ = in_right.shape
+    for b in range(groups):
+        here = pl.ds(b * block, block)
+        in_left[b] = late[here, 0 : 3 * block].astype(F32)
+        in_right[b] = late[here, 3 * block : 4 * block].astype(F32)
+        out_right[b] = early[here, 0:block].astype(F32)
+        out_left[b] = early[here, block : 2 * block].astype(F32)
+    third[...] = early[:, 384:512].astype(F32).T
+    values = small[...].astype(F32)
+    second[...] = values[0:128, 0:128]
+    first[...] = values[128:133, 0:128]
+    for at, target in enumerate((norm_gain, norm_bias, ffn_gain, ffn_bias)):
+        row = 128 + at * (width // 128)
+        target[...] = jnp.concatenate([values[row + k : row + k + 1, 128:256] for k in range(width // 128)], axis=1).reshape(width)
+    parts = [values[16 * at : 16 * at + 16, 128 : 128 + chans] for at in range(width // chans)]
+    lines = jnp.concatenate(parts, axis=1)
+    for s in range(3):
+        short[s] = lines[3 * s : 3 * s + 3]
+    conv_bias[...] = lines[9:10].reshape(width)
+    for copy in stores:
+        copy.wait()
+
+
+def finish(chans, ffn, tokens, late, early, small):
+    width = ffn.shape[1]
+    block = width // 4
+    shape = jax.ShapeDtypeStruct
+    vector = shape((width,), F32)
+    square = shape((4, block, block), F32)
+    return pl.pallas_call(
+        functools.partial(finish_kernel, width, chans),
+        out_shape=(
+            shape(tokens.shape, F32), vector, vector, square, shape((4, block, 3 * block), F32), shape((3, 3, width), F32),
+            shape((5, 128), F32), shape((128, 128), F32), shape((128, width), F32), vector, square, square, vector, vector,
+        )
+        + (shape((width, width), F32),) * 3,
+        in_specs=[any_spec()] * 2 + [vmem_spec()] * 3,
+        out_specs=(any_spec(),) + (vmem_spec(),) * 13 + (any_spec(),) * 3,
+        scratch_shapes=[
+            pltpu.VMEM(ffn.shape, BF),
+            pltpu.VMEM(ffn.shape, F32),
+            pltpu.VMEM(tokens.shape, BF),
+            pltpu.VMEM(tokens.shape, F32),
+            pltpu.SemaphoreType.DMA((4,)),
+            pltpu.SemaphoreType.DMA((4,)),
+        ],
+        compiler_params=pltpu.CompilerParams(vmem_limit_bytes=LIMIT),
+        name="finish",
+    )(ffn, tokens, late, early, small)
+
+
 def fast_body(
     tokens,
     norm_gain,
@@ -1216,42 +1304,19 @@
     chans, length = width // n_seq, rows * n_seq
     shape = (n_seq, n_tp)
     table, features = (jnp.asarray(array) for array in constants(length))
-    vectors, columns, first, third = prepare(
-        tokens, norm_gain, norm_bias, ffn_gain, ffn_bias, short_kernel, filter_first, filter_third, conv_bias
-    )
-    mixed, signals, conv, wave, taps, nyquist, acts, normed, shuffled, cot_rows = front(
-        shape, tokens, cotangent, table, vectors, in_right, in_left, columns, features, first, filter_second, third
+    mixed, signals, conv, wave, taps, nyquist, acts, normed, shuffled, cot_rows, columns, third = front(
+        shape, tokens, cotangent, table, norm_gain, norm_bias, in_right, in_left, short_kernel.transpose(0, 2, 1), conv_bias,
+        features, filter_first, filter_second, filter_third,
     )
     grad_mixed, grad_resid, shard, grad_weights, grad_vectors, output = feed(
-        shape, mixed, tokens, cot_rows, vectors, out_right, out_left, gate_weight, up_weight, down_weight
+        shape, mixed, tokens, cot_rows, ffn_gain, ffn_bias, out_right, out_left, gate_weight, up_weight, down_weight
     )
     ffn, grad_tokens, late, early, small = back(
-        shape, grad_mixed, columns, vectors, in_right, in_left, first, filter_second, third, nyquist, shard, grad_weights,
+        shape, grad_mixed, columns, norm_gain, in_right, in_left, filter_second, third, nyquist, shard, grad_weights,
         grad_vectors, features, tokens, table, signals, conv, wave, taps, acts, normed, shuffled, grad_resid,
     )
-    ffn, late, early, small = (array.astype(F32) for array in (ffn, late, early, small))
-    channel = small[:128, 128:].reshape(n_seq, 16, 128)[:, :10, :chans]
-    lines = small[128:152, 128:].reshape(4, width)
-    return (
-        output,
-        grad_tokens.astype(F32),
-        lines[0],
-        lines[1],
-        late[:, 576:].reshape(in_right.shape),
-        late[:, :576].reshape(in_left.shape),
-        channel[:, :9].reshape(n_seq, 3, 3, chans).transpose(1, 0, 3, 2).reshape(3, width, 3),
-        small[128:133, :128],
-        small[:128, :128],
-        early[:, 384:].T,
-        channel[:, 9].reshape(width),
-        early[:, :192].reshape(out_right.shape),
-        early[:, 192:384].reshape(out_left.shape),
-        lines[2],
-        lines[3],
-        ffn[0],
-        ffn[1],
-        ffn[2],
-    )
+    grads = finish(chans, ffn, grad_tokens, late, early, small)
+    return (output,) + grads[:5] + (grads[5].transpose(0, 2, 1),) + grads[6:]
 
 
 highest = lax.Precision.HIGHEST
@@ -1672,7 +1737,7 @@
 
 
 def solution(mesh):
-    return jax.shard_map(
+    mapped = jax.shard_map(
         functools.partial(choose_body, mesh),
         mesh=mesh,
         in_specs=(
@@ -1717,3 +1782,9 @@
         ),
         check_vma=False,
     )
+
+    def program(*arrays):
+        with jax.sharding.use_abstract_mesh(mesh.abstract_mesh):
+            return mapped(*arrays)
+
+    return program

time: 194 us -> 179 us (0.923)
  local copies, waits for them, and re-layouts: 18.2 us -> 0.68 us
  Pallas kernels: 169 us -> 178 us
  other arithmetic: 5.57 us -> 0 us
    pallas_call x0 -> x1, Pallas kernels: none -> 8.74 us  [finish(): pl.pallas_call(functools.partial(finish_kernel, width, chans), out_shape=...]
    slice x6 -> x0, local copies, waits for them, and re-layouts: 5.02 us -> none  [the longest x1 1.4 us: fast_body(): late[:, :576].reshape(in_left.shape)]
    convert_element_type x4 -> x0, other arithmetic: 4.09 us -> none  [the longest x3 2.82 us: fast_body(): array.astype(F32)]
    another operation x7 -> x0, local copies, waits for them, and re-layouts: 4.06 us -> none  [the longest x6 3.4 us: prepare(): jnp.stack([norm_gain, norm_bias, ffn_gain, ffn_bias] + [jnp.zeros_like(no...]
    squeeze x2 -> x0, local copies, waits for them, and re-layouts: 3.72 us -> none  [the longest x1 3.11 us: fast_body(): ffn[2]]
where the time goes in v3:
time: 179 us
  Pallas kernels  178 us (99%)
    pallas_call x1, Pallas kernels, back(): pl.pallas_call(functools.partial(back_kernel, n_seq, n_tp, (width, chans,...  77.9 us
    pallas_call x1, Pallas kernels, feed(): pl.pallas_call(functools.partial(feed_kernel, n_seq, n_tp, (width, chans,...  64.8 us
    pallas_call x1, Pallas kernels, front(): pl.pallas_call(functools.partial(front_kernel, n_seq, n_tp, (width, chans...  26.3 us
    pallas_call x1, Pallas kernels, finish(): pl.pallas_call(functools.partial(finish_kernel, width, chans), out_shape=...  8.74 us

profile of v3, /device:TPU:0, one launch (start us, length us, event | category | flops | bytes accessed | tf_op | source)
XLA Modules:
  0.0 179.1 jit_solution(3593894713113139465)
XLA Ops:
  0.7 26.3 %front.1 = (bf16[768,128]{1,0:T(8,128)(2,1)}, bf16[3,96,1024]{2,1,0:T(8,128)(2,1)}, f32[96,1024]{1,0:T(8,128)}, bf16[2,1024,128]{2,1,0:T(8,128)(2,1)}, bf16[2,10...) custom-call(bf16[4,128,768]{2,1,0:T(8,128)(2,1)} %refs_12_.3, ...), custom_call_target="tpu_custom_call" | custom-call | tf_op jit(solution)/shard_map/front/pallas_call | solution.py:331
  27.0 64.8 %feed.1 = (bf16[96,1024]{1,0:T(8,128)(2,1)}, f32[128,768]{1,0:T(8,128)}, bf16[3,96,768]{2,1,0:T(8,128)(2,1)}, bf16[2,768,192]{2,1,0:T(8,128)(2,1)}, f32[2,768]{1,0:T(2,128)}, /*index=5*/bf16[4,32,768]{2,1,0:T(8,128)(2,1)}) custom-call(bf16[768,128]{1,0:T(8,128)(2,1)} %get-tuple-element.58.refs_0_, bf16[4,128,768]{2,1,0:T(8,128)(2,1)} %refs_12_.3, ...), custom_call_target="tpu_custom_call" | custom-call | tf_op jit(solution)/shard_map/feed/pallas_call | solution.py:704
  91.8 77.9 %back.1 = (bf16[3,768,768]{2,1,0:T(8,128)(2,1)}, bf16[4,128,768]{2,1,0:T(8,128)(2,1)}, bf16[768,768]{1,0:T(8,128)(2,1)}, bf16[768,512]{1,0:T(8,128)(2,1)}, bf16[256,256]{1,0:T(8,128)(2,1)}) custom-call(bf16[96,1024]{1,0:T(8,128)(2,1)} %get-tuple-element.61.refs_0_, f32[96,16]{1,0:T(8,128)} %get-tuple-element.62.refs_1_, f32[768]{0:T(1024)} %refs_2_.2, ...), custom_call_target="tpu_custom_call" | custom-call | tf_op jit(solution)/shard_map/back/pallas_call | solution.py:1150
  169.7 0.0 copy-start
  169.7 8.7 %finish.1 = (f32[4,128,768]{2,1,0:T(8,128)}, f32[768]{0:T(1024)}, f32[768]{0:T(1024)}, f32[4,192,192]{2,1,0:T(8,128)}, f32[4,192,576]{2,1,0:T(8,128)}, /*index=5...) custom-call(bf16[3,768,768]{2,1,0:T(8,128)(2,1)} %get-tuple-element., ...), custom_call_target="tpu_custom_call" | custom-call | tf_op jit(solution)/shard_map/finish/pallas_call | solution.py:1260
  178.4 0.0 copy-done
  178.4 0.7 copy.39
Async XLA Ops:
  169.7 8.8 %copy-start = (bf16[4,32,768]{2,1,0:T(8,128)(2,1)S(1)}, bf16[4,32,768]{2,1,0:T(8,128)(2,1)}, u32[]{:S(2)}) copy-start(bf16[4,32,768]{2,1,0:T(8,128)(2,1)} %get-tuple-element.116) | copy-start | bytes 589828

commit v4 on v3

--- a/solution.py
+++ b/solution.py
@@ -1,5 +1,7 @@
 import functools
 import math
+import types
+import typing
 
 import numpy as np
 import jax
@@ -422,339 +424,6 @@
 CHIPS = (6, 2, 4)
 
 
-def feed_kernel(n_seq, n_tp, dims, *refs):
-    (mixed, tokens, cot_rows, gain, bias, right, left, gate_w, up_w, down_w) = refs[:10]
-    (grad_mixed_out, grad_resid_out, shard_out, grad_weights_out, grad_vectors_out, output_out) = refs[10:16]
-    (token_v, cot_v, gate_v, up_v, down_v, shuffled, branch, resid, scaled, inverse, normed, hidden, grad_hidden, grad_gate, grad_up,
-     grad_normed, grad_send, grad_recv, glu_own, glu_send, glu_recv, turned, grads, core_recv, halves, chip_recv, grad_branch,
-     middle, grad_mixed, grad_mixed_all, out_rows, output_v, local_sems, gather_send, gather_recv, back_send, back_recv, glu_ssem, glu_rsem,
-     out_send, out_recv, core_ssem, core_rsem, chip_ssem, chip_rsem, seq_send, seq_recv) = refs[16:]
-    width, chans, length, rows = dims
-    me, plane = lax.axis_index("seq"), lax.axis_index("tp")
-    entered = greet(n_seq, n_tp)
-    loads = [
-        pltpu.make_async_copy(tokens.at[plane], token_v, local_sems.at[0]),
-        pltpu.make_async_copy(cot_rows, cot_v, local_sems.at[1]),
-        pltpu.make_async_copy(down_w, down_v, local_sems.at[2]),
-        pltpu.make_async_copy(gate_w, gate_v, local_sems.at[3]),
-        pltpu.make_async_copy(up_w, up_v, local_sems.at[4]),
-    ]
-    for copy in loads:
-        copy.start()
-    groups = right.shape[0]
-    block = width // groups
-
-    def keep_branch(g, result):
-        branch[pl.ds(g * block, block), :] = result
-
-    monarch_forward(lambda b: mixed[pl.ds(b * block, block), :], right, left, shuffled, keep_branch)
-    loads[0].wait()
-    value = token_v[...].astype(F32) + branch[...].T
-    resid[...] = value
-    shifted = value - jnp.mean(value, axis=-1, keepdims=True)
-    inverse[...] = lax.rsqrt(jnp.mean(shifted * shifted, axis=-1, keepdims=True) + 1e-05)
-    value = shifted * inverse[...]
-    scaled[...] = value
-    normed[plane] = (value * gain[...].reshape(1, width) + bias[...].reshape(1, width)).astype(BF)
-    entered()
-    gathers = {}
-    for k in range(1, n_tp):
-        gathers[k] = pltpu.make_async_remote_copy(
-            src_ref=normed.at[plane],
-            dst_ref=normed.at[plane],
-            send_sem=gather_send.at[k],
-            recv_sem=gather_recv.at[k],
-            device_id={"tp": flip(plane, k)},
-            device_id_type=MESH,
-        )
-        gathers[k].start()
-    loads[1].wait()
-    loads[2].wait()
-    chunk = 256
-    pieces = width // chunk
-
-    def hidden_step(at, carry):
-        cols = pl.ds(pl.multiple_of(at * chunk, chunk), chunk)
-        result = dot(cot_v[...].reshape(n_tp * rows, width), down_v[cols, :], NT)
-        grad_hidden[:, :, cols] = result.reshape(n_tp, rows, chunk)
-        return carry
-
-    lax.fori_loop(0, pieces, hidden_step, 0)
-    loads[3].wait()
-    loads[4].wait()
-    backs, glus = {}, {}
-    for k in range(n_tp):
-        other = flip(plane, k)
-        if k > 0:
-            gathers[k].wait_recv()
-
-        def gate_step(at, carry, other=other):
-            cols = pl.ds(pl.multiple_of(at * chunk, chunk), chunk)
-            value = normed[other]
-            gate = dot(value, gate_v[:, cols])
-            upward = dot(value, up_v[:, cols])
-            sigma = 1.0 / (1.0 + jnp.exp(-gate))
-            active = gate * sigma
-            hidden[other, :, cols] = (active * upward).astype(BF)
-            above = grad_hidden[other, :, cols]
-            grad_gate[other, :, cols] = (above * upward * (sigma + active * (1.0 - sigma))).astype(BF)
-            grad_up[other, :, cols] = (above * active).astype(BF)
-            return carry
-
-        lax.fori_loop(0, pieces, gate_step, 0)
-
-        def back_step(at, carry, k=k, other=other):
-            cols = pl.ds(pl.multiple_of(at * chunk, chunk), chunk)
-            result = dot(grad_gate[other], gate_v[cols, :], NT) + dot(grad_up[other], up_v[cols, :], NT)
-            if k == 0:
-                grad_normed[:, cols] = result
-            else:
-                grad_send[k, :, cols] = result.astype(BF)
-            return carry
-
-        lax.fori_loop(0, pieces, back_step, 0)
-        if k > 0:
-            backs[k] = pltpu.make_async_remote_copy(
-                src_ref=grad_send.at[k],
-                dst_ref=grad_recv.at[k],
-                send_sem=back_send.at[k],
-                recv_sem=back_recv.at[k],
-                device_id={"tp": other},
-                device_id_type=MESH,
-            )
-            backs[k].start()
-
-    def turn(source):
-        for s in range(n_tp):
-            turned[:, s * rows : (s + 1) * rows] = source[s].T
-
-    def weight_grad(which, factor):
-        def step(at, carry):
-            here = pl.ds(pl.multiple_of(at * chunk, chunk), chunk)
-            result = dot(turned[here, :], factor[...].reshape(n_tp * rows, width))
-            grads[which, here, :] = result.astype(BF)
-            return carry
-
-        lax.fori_loop(0, pieces, step, 0)
-
-    core = lax.rem(me, 2)
-    half = width // 2
-    core_copies = []
-
-    def core_send(which):
-        copy = pltpu.make_async_remote_copy(
-            src_ref=grads.at[which, pl.ds(pl.multiple_of((1 - core) * half, half), half), :],
-            dst_ref=core_recv.at[which],
-            send_sem=core_ssem.at[which],
-            recv_sem=core_rsem.at[which],
-            device_id={"seq": flip(me, 1)},
-            device_id_type=MESH,
-        )
-        copy.start()
-        core_copies.append(copy)
-
-    turn(normed)
-    weight_grad(0, grad_gate)
-    core_send(0)
-    weight_grad(1, grad_up)
-    core_send(1)
-    turn(hidden)
-    weight_grad(2, cot_v)
-    core_send(2)
-
-    for k in (1, 2, 3, 0):
-        other = flip(plane, k)
-
-        def glu_step(at, carry, k=k, other=other):
-            cols = pl.ds(pl.multiple_of(at * chunk, chunk), chunk)
-            result = dot(hidden[other], down_v[:, cols])
-            if k == 0:
-                glu_own[:, cols] = result
-            else:
-                glu_send[k, :, cols] = result.astype(BF)
-            return carry
-
-        lax.fori_loop(0, pieces, glu_step, 0)
-        if k > 0:
-            glus[k] = pltpu.make_async_remote_copy(
-                src_ref=glu_send.at[k],
-                dst_ref=glu_recv.at[k],
-                send_sem=glu_ssem.at[k],
-                recv_sem=glu_rsem.at[k],
-                device_id={"tp": other},
-                device_id_type=MESH,
-            )
-            glus[k].start()
-
-    quarter = half // (n_seq // 2)
-    chip_copies = []
-    for which in range(3):
-        core_copies[which].wait_recv()
-        own = grads[which, pl.ds(pl.multiple_of(core * half, half), half), :]
-        halves[which] = (own.astype(F32) + core_recv[which].astype(F32)).astype(BF)
-        for k in CHIPS:
-            other = flip(me, k)
-            copy = pltpu.make_async_remote_copy(
-                src_ref=halves.at[which, pl.ds(pl.multiple_of(other // 2 * quarter, 16), quarter), :],
-                dst_ref=chip_recv.at[which, k // 2],
-                send_sem=chip_ssem.at[which, k // 2],
-                recv_sem=chip_rsem.at[which, k // 2],
-                device_id={"seq": other},
-                device_id_type=MESH,
-            )
-            copy.start()
-            chip_copies.append(copy)
-
-    for k in range(1, n_tp):
-        backs[k].wait_recv()
-    total = grad_normed[...]
-    for k in range(1, n_tp):
-        total = total + grad_recv[k].astype(F32)
-    value = scaled[...]
-    grad_vectors_out[0:1, :] = jnp.sum(total * value, axis=0, keepdims=True)
-    grad_vectors_out[1:2, :] = jnp.sum(total, axis=0, keepdims=True)
-    total = total * gain[...].reshape(1, width)
-    first_mean = jnp.mean(total, axis=-1, keepdims=True)
-    second_mean = jnp.mean(total * value, axis=-1, keepdims=True)
-    total = cot_v[plane].astype(F32) + inverse[...] * (total - first_mean - value * second_mean)
-    grad_resid_out[...] = total
-    grad_branch[...] = total.T.astype(BF)
-
-    def keep_right(b, result):
-        grad_weights_out[0, pl.ds(b * block, block), :] = result.astype(BF)
-
-    def keep_left(g, result):
-        grad_weights_out[1, pl.ds(g * block, block), :] = result.astype(BF)
-
-    def keep_mixed(b, result):
-        grad_mixed[pl.ds(b * block, block), :] = result.astype(BF)
-
-    monarch_backward(
-        lambda g: grad_branch[pl.ds(g * block, block), :],
-        lambda b: mixed[pl.ds(b * block, block), :],
-        shuffled, right, left, middle, keep_right, keep_left, keep_mixed,
-    )
-    mine = pl.ds(pl.multiple_of(me * rows, rows), rows)
-    seq_copies = []
-    for k in SEQ_ORDER:
-        other = flip(me, k)
-        copy = pltpu.make_async_remote_copy(
-            src_ref=grad_mixed.at[pl.ds(pl.multiple_of(other * chans, 16), chans), :],
-            dst_ref=grad_mixed_all.at[:, mine],
-            send_sem=seq_send.at[k],
-            recv_sem=seq_recv.at[k],
-            device_id={"seq": other},
-            device_id_type=MESH,
-        )
-        copy.start()
-        seq_copies.append(copy)
-    grad_mixed_all[:, mine] = grad_mixed[pl.ds(pl.multiple_of(me * chans, 16), chans), :]
-
-    for k in range(1, n_tp):
-        glus[k].wait_recv()
-    total = resid[...] + glu_own[...]
-    for k in range(1, n_tp):
-        total = total + glu_recv[k].astype(F32)
-    out_rows[...] = total.astype(BF)
-    part = rows // n_tp
-    out_copies = []
-    for k in range(1, n_tp):
-        other = flip(plane, k)
-        copy = pltpu.make_async_remote_copy(
-            src_ref=out_rows.at[pl.ds(pl.multiple_of(other * part, part), part), :],
-            dst_ref=output_v.at[plane],
-            send_sem=out_send.at[k],
-            recv_sem=out_recv.at[k],
-            device_id={"tp": other},
-            device_id_type=MESH,
-        )
-        copy.start()
-        out_copies.append(copy)
-    output_v[plane] = out_rows[pl.ds(pl.multiple_of(plane * part, part), part), :]
-
-    chip = me // 2
-    for which in range(3):
-        for at in range(3):
-            chip_copies[3 * which + at].wait_recv()
-        total = halves[which, pl.ds(pl.multiple_of(chip * quarter, 16), quarter), :].astype(F32)
-        for k in CHIPS:
-            total = total + chip_recv[which, k // 2].astype(F32)
-        shard_out[which] = total.astype(BF)
-    for copy in seq_copies:
-        copy.wait()
-    grad_mixed_out[...] = grad_mixed_all[...]
-    for copy in out_copies:
-        copy.wait()
-    output_out[...] = output_v[...]
-    for k in range(1, n_tp):
-        gathers[k].wait_send()
-        backs[k].wait_send()
-        glus[k].wait_send()
-    for copy in core_copies + chip_copies:
-        copy.wait_send()
-
-
-def feed(mesh_shape, mixed, tokens, cot_rows, gain, bias, right, left, gate_w, up_w, down_w):
-    n_seq, n_tp = mesh_shape
-    _, rows, width = tokens.shape
-    chans, length = width // n_seq, rows * n_seq
-    part = rows // n_tp
-    shape = jax.ShapeDtypeStruct
-    dma = pltpu.SemaphoreType.DMA
-    return pl.pallas_call(
-        functools.partial(feed_kernel, n_seq, n_tp, (width, chans, length, rows)),
-        out_shape=(
-            shape((chans, length), BF),
-            shape((rows, width), F32),
-            shape((3, width // n_seq, width), BF),
-            shape((2, width, width // 4), BF),
-            shape((2, width), F32),
-            shape((n_tp, part, width), BF),
-        ),
-        in_specs=[vmem_spec(), any_spec(), any_spec()] + [vmem_spec()] * 4 + [any_spec()] * 3,
-        out_specs=(vmem_spec(),) * 6,
-        scratch_shapes=[
-            pltpu.VMEM((rows, width), BF),
-            pltpu.VMEM((n_tp, rows, width), BF),
-            pltpu.VMEM((width, width), BF),
-            pltpu.VMEM((width, width), BF),
-            pltpu.VMEM((width, width), BF),
-            pltpu.VMEM((width, rows), BF),
-            pltpu.VMEM((width, rows), F32),
-            pltpu.VMEM((rows, width), F32),
-            pltpu.VMEM((rows, width), F32),
-            pltpu.VMEM((rows, 1), F32),
-            pltpu.VMEM((n_tp, rows, width), BF),
-            pltpu.VMEM((n_tp, rows, width), BF),
-            pltpu.VMEM((n_tp, rows, width), F32),
-            pltpu.VMEM((n_tp, rows, width), BF),
-            pltpu.VMEM((n_tp, rows, width), BF),
-            pltpu.VMEM((rows, width), F32),
-            pltpu.VMEM((n_tp, rows, width), BF),
-            pltpu.VMEM((n_tp, rows, width), BF),
-            pltpu.VMEM((rows, width), F32),
-            pltpu.VMEM((n_tp, rows, width), BF),
-            pltpu.VMEM((n_tp, rows, width), BF),
-            pltpu.VMEM((width, n_tp * rows), BF),
-            pltpu.VMEM((3, width, width), BF),
-            pltpu.VMEM((3, width // 2, width), BF),
-            pltpu.VMEM((3, width // 2, width), BF),
-            pltpu.VMEM((3, n_seq // 2, width // n_seq, width), BF),
-            pltpu.VMEM((width, rows), BF),
-            pltpu.VMEM((width, rows), BF),
-            pltpu.VMEM((width, rows), BF),
-            pltpu.VMEM((chans, length), BF),
-            pltpu.VMEM((rows, width), BF),
-            pltpu.VMEM((n_tp, part, width), BF),
-            dma((5,)),
-            dma((n_tp,)), dma((n_tp,)), dma((n_tp,)), dma((n_tp,)), dma((n_tp,)), dma((n_tp,)), dma((n_tp,)), dma((n_tp,)),
-            dma((3,)), dma((3,)), dma((3, n_seq // 2)), dma((3, n_seq // 2)), dma((n_seq,)), dma((n_seq,)),
-        ],
-        compiler_params=pltpu.CompilerParams(collective_id=1, has_side_effects=True, vmem_limit_bytes=LIMIT),
-        name="feed",
-    )(mixed, tokens, cot_rows, gain, bias, right, left, gate_w, up_w, down_w)
-
-
 class Reduce:
     def __init__(self, n_seq, n_tp, own, full, core_in, halves, chip_in, quarter, plane_in, send, recv):
         self.own, self.full, self.core_in, self.halves = own, full, core_in, halves
@@ -840,131 +509,570 @@
             copy.wait_send()
 
 
-def reduce_scratch(n_seq, n_tp, rows, width):
-    half, chip, plane = width // 2, rows // (n_seq // 2), rows // (n_seq // 2) // n_tp
-    return [
-        pltpu.VMEM((rows, width), BF),
-        pltpu.VMEM((rows, width), BF),
-        pltpu.VMEM((rows, half), BF),
-        pltpu.VMEM((rows, half), BF),
-        pltpu.VMEM((n_seq // 2, chip, half), BF),
-        pltpu.VMEM((chip, half), BF),
-        pltpu.VMEM((n_tp, plane, half), BF),
-        pltpu.SemaphoreType.DMA((14,)),
-        pltpu.SemaphoreType.DMA((14,)),
-    ]
-
-
-def back_kernel(n_seq, n_tp, dims, *refs):
-    (grad_mixed, columns, gain, right, left, second, third, nyquist, shard, grad_weights, grad_vectors,
-     features, tokens, table, signals_in, conv_in, wave_in, taps_in, acts_in, normed_in, shuffled_in, resid_in) = refs[:22]
-    (ffn_out, tokens_out, late_out, early_out, small_out) = refs[22:27]
-    (table_v, signals, conv, wave, taps_v, acts, token_v, normed, shuffled, grad_resid, grad_short, query, value_v, grad_conv,
-     padded, back_wave, cross, sums, grad_signals, grad_proj, middle, grad_rows, grad_tok, grad_second, grad_first, grad_third,
-     local_sems, ffn_ssem, ffn_rsem, seq_send, seq_recv, tp_send, tp_recv) = refs[27:60]
+def neighbour_order(plane, at):
+    upper = plane // 2
+    near = plane + upper * (3 - 2 * plane)
+    result = at * (1 - near) + (0, 0, 2, 3)[at] * near
+    return result + upper * (3 - 2 * result)
+
+
+class Line:
+    def __init__(self, n_tp, slots, send, recv):
+        self.n_tp, self.slots, self.send, self.recv = n_tp, slots, send, recv
+        self.plane = lax.axis_index("tp")
+        self.sent = []
+
+    def copy(self, block, source, way):
+        return pltpu.make_async_remote_copy(
+            src_ref=source, dst_ref=self.slots.at[block], send_sem=self.send.at[way, block], recv_sem=self.recv.at[block],
+            device_id={"tp": self.plane + (1, -1)[way]}, device_id_type=MESH,
+        )
+
+    def start(self, block, source, way, here):
+        @pl.when(here)
+        def _():
+            self.copy(block, source, way).start()
+
+        self.sent.append((block, source, way, here))
+
+    def begin(self, source):
+        self.start(self.plane, source, 0, self.plane < self.n_tp - 1)
+        self.start(self.plane, source, 1, self.plane > 0)
+
+    def take(self, block):
+        pltpu.make_async_remote_copy(
+            src_ref=self.slots.at[block], dst_ref=self.slots.at[block], send_sem=self.send.at[0, block],
+            recv_sem=self.recv.at[block], device_id={"tp": block}, device_id_type=MESH,
+        ).wait_recv()
+        source = self.slots.at[block]
+        self.start(block, source, 0, jnp.logical_and(block < self.plane, self.plane < self.n_tp - 1))
+        self.start(block, source, 1, jnp.logical_and(block > self.plane, self.plane > 0))
+
+    def finish(self):
+        for block, source, way, here in self.sent:
+
+            @pl.when(here)
+            def _(block=block, source=source, way=way):
+                self.copy(block, source, way).wait_send()
+
+
+class Square:
+    def __init__(self, own, full, core_in, half, first_in, second_in, send, recv):
+        self.own, self.full, self.core_in, self.half = own, full, core_in, half
+        self.first_in, self.second_in, self.send, self.recv = first_in, second_in, send, recv
+        me = lax.axis_index("seq")
+        self.me = me
+        rows = own.shape[0]
+        self.rows = rows
+        self.core = lax.rem(me, 2)
+        y, x = me // 4, lax.rem(me // 2, 2)
+        quarter, part = rows // 8, rows // 16
+        base = rows // 4
+        self.ways = ((2, x, y, 0), (4, y, x, base))
+        self.quarter, self.part = quarter, part
+        self.started = []
+        self.phase = []
+
+    def copy(self, source, target, at, k):
+        result = pltpu.make_async_remote_copy(
+            src_ref=source, dst_ref=target, send_sem=self.send.at[at], recv_sem=self.recv.at[at],
+            device_id={"seq": flip(self.me, k)}, device_id_type=MESH,
+        )
+        result.start()
+        self.started.append(result)
+        self.phase.append(result)
+
+    def arrived(self):
+        for copy in self.phase:
+            copy.wait_recv()
+        self.phase = []
+
+    def span(self, start, size):
+        return pl.ds(pl.multiple_of(start, 16), size)
+
+    def start_core(self):
+        half = self.rows // 2
+        self.copy(self.own.at[self.span((1 - self.core) * half, half), :], self.core_in, 0, 1)
+
+    def start_first(self):
+        self.arrived()
+        half = self.rows // 2
+        own = self.own[self.span(self.core * half, half), :]
+        self.half[...] = (own.astype(F32) + self.core_in[...].astype(F32)).astype(BF)
+        for way, (k, near, far, base) in enumerate(self.ways):
+            source = self.half.at[self.span(base + (1 - near) * self.quarter, self.quarter), :]
+            self.copy(source, self.first_in.at[way], 1 + way, k)
+
+    def start_second(self):
+        self.arrived()
+        for way, (k, near, far, base) in enumerate(self.ways):
+            here = self.span(base + near * self.quarter, self.quarter)
+            self.half[here, :] = (self.half[here, :].astype(F32) + self.first_in[way].astype(F32)).astype(BF)
+            source = self.half.at[self.span(base + near * self.quarter + (1 - far) * self.part, self.part), :]
+            self.copy(source, self.second_in.at[way], 3 + way, 6 - k)
+
+    def start_second_back(self):
+        self.arrived()
+        for way, (k, near, far, base) in enumerate(self.ways):
+            place = base + near * self.quarter + far * self.part
+            total = self.half[self.span(place, self.part), :].astype(F32) + self.second_in[way].astype(F32)
+            here = self.span(self.core * (self.rows // 2) + place, self.part)
+            self.full[here, :] = total.astype(BF)
+            spot = self.full.at[here, :]
+            self.copy(spot, spot, 5 + way, 6 - k)
+
+    def start_first_back(self):
+        self.arrived()
+        for way, (k, near, far, base) in enumerate(self.ways):
+            spot = self.full.at[self.span(self.core * (self.rows // 2) + base + near * self.quarter, self.quarter), :]
+            self.copy(spot, spot, 7 + way, k)
+
+    def start_core_back(self):
+        self.arrived()
+        spot = self.full.at[self.span(self.core * (self.rows // 2), self.rows // 2), :]
+        self.copy(spot, spot, 9, 1)
+
+    def finish(self):
+        for copy in self.started:
+            copy.wait_send()
+
+
+class Inputs(typing.NamedTuple):
+    mixed: typing.Any
+    feed_gain: typing.Any
+    feed_bias: typing.Any
+    out_right: typing.Any
+    out_left: typing.Any
+    columns: typing.Any
+    gain: typing.Any
+    in_right: typing.Any
+    in_left: typing.Any
+    second: typing.Any
+    third: typing.Any
+    nyquist: typing.Any
+    features: typing.Any
+    cot_rows: typing.Any
+    tokens: typing.Any
+    gate_w: typing.Any
+    up_w: typing.Any
+    down_w: typing.Any
+    table: typing.Any
+    signals_in: typing.Any
+    conv_in: typing.Any
+    wave_in: typing.Any
+    taps_in: typing.Any
+    acts_in: typing.Any
+    normed_in: typing.Any
+    shuffled_in: typing.Any
+
+
+class Outputs(typing.NamedTuple):
+    output_out: typing.Any
+    ffn_out: typing.Any
+    tokens_out: typing.Any
+    late_out: typing.Any
+    early_out: typing.Any
+    small_out: typing.Any
+
+
+def core_scratch(n_seq, n_tp, width, chans, length, rows):
+    result = dict(
+        token_v=pltpu.VMEM((rows, width), BF),
+        cot_v=pltpu.VMEM((n_tp, rows, width), BF),
+        gate_v=pltpu.VMEM((width, width), BF),
+        up_v=pltpu.VMEM((width, width), BF),
+        down_v=pltpu.VMEM((width, width), BF),
+        out_shuffled=pltpu.VMEM((width, rows), BF),
+        branch=pltpu.VMEM((width, rows), F32),
+        resid=pltpu.VMEM((rows, width), F32),
+        scaled=pltpu.VMEM((rows, width), F32),
+        inverse=pltpu.VMEM((rows, 1), F32),
+        normed=pltpu.VMEM((n_tp, rows, width), BF),
+        hidden=pltpu.VMEM((n_tp, rows, width), BF),
+        grad_hidden=pltpu.VMEM((n_tp, rows, width), F32),
+        grad_gate=pltpu.VMEM((n_tp, rows, width), BF),
+        grad_up=pltpu.VMEM((n_tp, rows, width), BF),
+        grad_normed=pltpu.VMEM((rows, width), F32),
+        grad_send=pltpu.VMEM((n_tp, rows, width), BF),
+        grad_recv=pltpu.VMEM((n_tp, rows, width), BF),
+        glu_own=pltpu.VMEM((rows, width), F32),
+        glu_send=pltpu.VMEM((n_tp, rows, width), BF),
+        glu_recv=pltpu.VMEM((n_tp, rows, width), BF),
+        turned=pltpu.VMEM((width, n_tp*rows), BF),
+        grads=pltpu.VMEM((3, width, width), BF),
+        ffn_v=pltpu.VMEM((3, width, width), BF),
+        core_in=pltpu.VMEM((3, width//2, width), BF),
+        halves=pltpu.VMEM((3, width//2, width), BF),
+        first_in=pltpu.VMEM((3, 2, width//8, width), BF),
+        second_in=pltpu.VMEM((3, 2, width//16, width), BF),
+        grad_branch=pltpu.VMEM((width, rows), BF),
+        middle=pltpu.VMEM((width, rows), BF),
+        grad_mixed_own=pltpu.VMEM((width, rows), BF),
+        grad_mixed=pltpu.VMEM((chans, length), BF),
+        out_rows=pltpu.VMEM((rows, width), BF),
+        output_v=pltpu.VMEM((n_tp, rows//n_tp, width), BF),
+        grad_vectors=pltpu.VMEM((2, width), F32),
+        grad_resid=pltpu.VMEM((rows, width), F32),
+        table_v=pltpu.VMEM((2, length, length), BF),
+        signals=pltpu.VMEM((3, chans, length), BF),
+        conv=pltpu.VMEM((chans, length), F32),
+        wave=pltpu.VMEM((2, length, 128), BF),
+        taps_v=pltpu.VMEM((2, length, 128), BF),
+        acts=pltpu.VMEM((4, 2*length, 128), BF),
+        in_normed=pltpu.VMEM((width, rows), BF),
+        in_shuffled=pltpu.VMEM((width, rows), BF),
+        grad_short=pltpu.VMEM((3, chans, length), F32),
+        query=pltpu.VMEM((chans, length), F32),
+        value_v=pltpu.VMEM((chans, length), F32),
+        grad_conv=pltpu.VMEM((chans, length), F32),
+        padded=pltpu.VMEM((128, length), BF),
+        back_wave=pltpu.VMEM((2, length, 128), BF),
+        cross=pltpu.VMEM((2, length, 256), BF),
+        sums=pltpu.VMEM((128, 128), F32),
+        grad_signals=pltpu.VMEM((3, chans, length), BF),
+        grad_proj=pltpu.VMEM((3*width, rows), BF),
+        grad_rows=pltpu.VMEM((width, rows), F32),
+        grad_tok=pltpu.VMEM((rows, width), BF),
+        grad_second=pltpu.VMEM((128, 128), F32),
+        grad_first=pltpu.VMEM((16, 128), F32),
+        grad_third=pltpu.VMEM((128, 128), F32),
+        local_sems=pltpu.SemaphoreType.DMA((20,)),
+        line_send=pltpu.SemaphoreType.DMA((2,n_tp)),
+        line_recv=pltpu.SemaphoreType.DMA((n_tp,)),
+        tok_send=pltpu.SemaphoreType.DMA((2,n_tp)),
+        tok_recv=pltpu.SemaphoreType.DMA((n_tp,)),
+        back_send=pltpu.SemaphoreType.DMA((n_tp,)),
+        back_recv=pltpu.SemaphoreType.DMA((n_tp,)),
+        glu_ssem=pltpu.SemaphoreType.DMA((n_tp,)),
+        glu_rsem=pltpu.SemaphoreType.DMA((n_tp,)),
+        out_send=pltpu.SemaphoreType.DMA((n_tp,)),
+        out_recv=pltpu.SemaphoreType.DMA((n_tp,)),
+        mixed_send=pltpu.SemaphoreType.DMA((n_seq,)),
+        mixed_recv=pltpu.SemaphoreType.DMA((n_seq,)),
+        seq_send=pltpu.SemaphoreType.DMA((n_seq,3)),
+        seq_recv=pltpu.SemaphoreType.DMA((n_seq,3)),
+        ffn_send=pltpu.SemaphoreType.DMA((3,10)),
+        ffn_recv=pltpu.SemaphoreType.DMA((3,10)),
+        late_own=pltpu.VMEM((width, width), BF),
+        late_full=pltpu.VMEM((width, width), BF),
+        early_own=pltpu.VMEM((width, 512), BF),
+        early_full=pltpu.VMEM((width, 512), BF),
+        small_own=pltpu.VMEM((256, 256), BF),
+        small_full=pltpu.VMEM((256, 256), BF),
+    )
+    groups = []
+    for count, breadth in ((256, width), (256, width), (256, width), (width, 512), (256, 256)):
+        half, chip = breadth // 2, count // (n_seq // 2)
+        groups.append(
+            [
+                pltpu.VMEM((count, half), BF),
+                pltpu.VMEM((count, half), BF),
+                pltpu.VMEM((n_seq // 2, chip, half), BF),
+                pltpu.VMEM((chip, half), BF),
+                pltpu.VMEM((n_tp, chip // n_tp, half), BF),
+                pltpu.SemaphoreType.DMA((14,)),
+                pltpu.SemaphoreType.DMA((14,)),
+            ]
+        )
+    return result, groups
+
+
+def core_kernel(n_seq, n_tp, dims, *refs):
     width, chans, length, rows = dims
-    late = Reduce(n_seq, n_tp, *refs[60:69])
-    early = Reduce(n_seq, n_tp, *refs[69:78])
-    small = Reduce(n_seq, n_tp, *refs[78:87])
+    scratch, groups = core_scratch(n_seq, n_tp, width, chans, length, rows)
+    named = dict(zip(Inputs._fields + Outputs._fields + tuple(scratch), refs))
+    r = types.SimpleNamespace(**named)
+    spare = list(refs[len(named) :])
+    reduce_refs = [[spare.pop(0) for _ in group] for group in groups]
     me, plane = lax.axis_index("seq"), lax.axis_index("tp")
     entered = greet(n_seq, n_tp)
-    loads = [
-        pltpu.make_async_copy(source, target, local_sems.at[at])
-        for at, (source, target) in enumerate(
-            (
-                (signals_in, signals), (conv_in, conv), (table, table_v), (wave_in, wave), (taps_in, taps_v), (acts_in, acts),
-                (tokens.at[plane], token_v), (normed_in, normed), (shuffled_in, shuffled), (resid_in, grad_resid),
-            )
+    sources = dict(
+        token=(r.tokens.at[plane], r.token_v),
+        cot=(r.cot_rows, r.cot_v),
+        down=(r.down_w, r.down_v),
+        gate=(r.gate_w, r.gate_v),
+        up=(r.up_w, r.up_v),
+        signals=(r.signals_in, r.signals),
+        conv=(r.conv_in, r.conv),
+        table=(r.table, r.table_v),
+        wave=(r.wave_in, r.wave),
+        taps=(r.taps_in, r.taps_v),
+        acts=(r.acts_in, r.acts),
+        normed=(r.normed_in, r.in_normed),
+        shuffled=(r.shuffled_in, r.in_shuffled),
+    )
+    copies = {
+        name: pltpu.make_async_copy(*pair, r.local_sems.at[at]) for at, (name, pair) in enumerate(sources.items())
+    }
+    for copy in copies.values():
+        copy.start()
+    loads = types.SimpleNamespace(**copies)
+    _, block, _ = r.out_right.shape
+    chunk = 256
+    pieces = width // chunk
+    per = length // chunk
+    step = 16
+
+    lates = []
+    for at in range(3):
+        here = pl.ds(256 * at, 256)
+        lates.append(Reduce(n_seq, n_tp, r.late_own.at[here, :], r.late_full.at[here, :], *reduce_refs[at]))
+    early = Reduce(n_seq, n_tp, r.early_own, r.early_full, *reduce_refs[3])
+    small = Reduce(n_seq, n_tp, r.small_own, r.small_full, *reduce_refs[4])
+    squares = [
+        Square(
+            r.grads.at[which], r.ffn_v.at[which], r.core_in.at[which], r.halves.at[which], r.first_in.at[which],
+            r.second_in.at[which], r.ffn_send.at[which], r.ffn_recv.at[which],
         )
+        for which in range(3)
     ]
-    for copy in loads:
-        copy.start()
-    half, quarter = width // 2, width // n_seq
-    own_rows = pl.ds(pl.multiple_of(lax.rem(me, 2) * half + me // 2 * quarter, 16), quarter)
+
+    def keep_branch(g, result):
+        r.branch[pl.ds(g * block, block), :] = result
+
+    monarch_forward(lambda b: r.mixed[pl.ds(b * block, block), :], r.out_right, r.out_left, r.out_shuffled, keep_branch)
+    loads.token.wait()
+    tokens = r.token_v[...].astype(F32)
+    value = tokens + r.branch[...].T
+    r.resid[...] = value
+    shifted = value - jnp.mean(value, axis=-1, keepdims=True)
+    r.inverse[...] = lax.rsqrt(jnp.mean(shifted * shifted, axis=-1, keepdims=True) + 1e-05)
+    value = shifted * r.inverse[...]
+    r.scaled[...] = value
+    r.normed[plane] = (value * r.feed_gain[...].reshape(1, width) + r.feed_bias[...].reshape(1, width)).astype(BF)
     entered()
-    ffn_copies = []
-    for which in range(3):
-        for k in CHIPS:
+    line = Line(n_tp, r.normed, r.line_send, r.line_recv)
+    line.begin(r.normed.at[plane])
+    loads.cot.wait()
+    loads.down.wait()
+
+    def hidden_step(at, carry):
+        cols = pl.ds(pl.multiple_of(at * chunk, chunk), chunk)
+        result = dot(r.cot_v[...].reshape(n_tp * rows, width), r.down_v[cols, :], NT)
+        r.grad_hidden[:, :, cols] = result.reshape(n_tp, rows, chunk)
+        return carry
+
+    lax.fori_loop(0, pieces, hidden_step, 0)
+    loads.gate.wait()
+    loads.up.wait()
+    backs = []
+    for k in range(n_tp):
+        other = plane if k == 0 else neighbour_order(plane, k)
+        if k > 0:
+            line.take(other)
+
+        def gate_step(at, carry, other=other):
+            cols = pl.ds(pl.multiple_of(at * chunk, chunk), chunk)
+            value = r.normed[other]
+            gate = dot(value, r.gate_v[:, cols])
+            upward = dot(value, r.up_v[:, cols])
+            sigma = 1.0 / (1.0 + jnp.exp(-gate))
+            active = gate * sigma
+            r.hidden[other, :, cols] = (active * upward).astype(BF)
+            above = r.grad_hidden[other, :, cols]
+            r.grad_gate[other, :, cols] = (above * upward * (sigma + active * (1.0 - sigma))).astype(BF)
+            r.grad_up[other, :, cols] = (above * active).astype(BF)
+            return carry
+
+        lax.fori_loop(0, pieces, gate_step, 0)
+
+        def back_step(at, carry, k=k, other=other):
+            cols = pl.ds(pl.multiple_of(at * chunk, chunk), chunk)
+            result = dot(r.grad_gate[other], r.gate_v[cols, :], NT) + dot(r.grad_up[other], r.up_v[cols, :], NT)
+            if k == 0:
+                r.grad_normed[:, cols] = result
+            else:
+                r.grad_send[other, :, cols] = result.astype(BF)
+            return carry
+
+        lax.fori_loop(0, pieces, back_step, 0)
+        if k > 0:
             copy = pltpu.make_async_remote_copy(
-                src_ref=shard.at[which],
-                dst_ref=ffn_out.at[which, own_rows, :],
-                send_sem=ffn_ssem.at[which, k // 2],
-                recv_sem=ffn_rsem.at[which, k // 2],
-                device_id={"seq": flip(me, k)},
+                src_ref=r.grad_send.at[other],
+                dst_ref=r.grad_recv.at[plane],
+                send_sem=r.back_send.at[other],
+                recv_sem=r.back_recv.at[plane],
+                device_id={"tp": other},
                 device_id_type=MESH,
             )
             copy.start()
-            ffn_copies.append(copy)
-    own_shard = pltpu.make_async_copy(shard, ffn_out.at[:, own_rows, :], local_sems.at[10])
-    own_shard.start()
-    sums[...] = jnp.zeros_like(sums)
-    small.own[...] = jnp.zeros_like(small.own)
-    early.own[...] = jnp.zeros_like(early.own)
-    loads[0].wait()
-    loads[1].wait()
-    step = 16
-    padded[pl.ds(chans, 128 - chans), :] = jnp.zeros((128 - chans, length), BF)
+            backs.append(copy)
+
+    def turn(source):
+        for s in range(n_tp):
+            r.turned[:, s * rows : (s + 1) * rows] = source[s].T
+
+    def weight_grad(which, factor):
+        def grad_step(at, carry):
+            here = pl.ds(pl.multiple_of(at * chunk, chunk), chunk)
+            result = dot(r.turned[here, :], factor[...].reshape(n_tp * rows, width))
+            r.grads[which, here, :] = result.astype(BF)
+            return carry
+
+        lax.fori_loop(0, pieces, grad_step, 0)
+        squares[which].start_core()
+
+    turn(r.normed)
+    weight_grad(0, r.grad_gate)
+    weight_grad(1, r.grad_up)
+    squares[0].start_first()
+    turn(r.hidden)
+    weight_grad(2, r.cot_v)
+    squares[1].start_first()
+    squares[2].start_first()
+
+    def from_planes(recv, slots):
+        total = 0.0
+        for k in range(1, n_tp):
+            other = flip(plane, k)
+            pltpu.make_async_remote_copy(
+                src_ref=slots.at[other], dst_ref=slots.at[other], send_sem=recv.at[other], recv_sem=recv.at[other],
+                device_id={"tp": other}, device_id_type=MESH,
+            ).wait_recv()
+            total = total + slots[other].astype(F32)
+        return total
+
+    total = r.grad_normed[...] + from_planes(r.back_recv, r.grad_recv)
+    value = r.scaled[...]
+    r.grad_vectors[0:1, :] = jnp.sum(total * value, axis=0, keepdims=True)
+    r.grad_vectors[1:2, :] = jnp.sum(total, axis=0, keepdims=True)
+    total = total * r.feed_gain[...].reshape(1, width)
+    first_mean = jnp.mean(total, axis=-1, keepdims=True)
+    second_mean = jnp.mean(total * value, axis=-1, keepdims=True)
+    total = r.cot_v[plane].astype(F32) + r.inverse[...] * (total - first_mean - value * second_mean)
+    r.grad_resid[...] = total
+    r.grad_branch[...] = total.T.astype(BF)
+    out_parts = {}
+
+    def keep_out_left(g, result):
+        out_parts[g] = result.astype(BF)
+
+    def keep_out_right(b, result):
+        both = jnp.concatenate([result.astype(BF), out_parts[b]], axis=1)
+        r.early_own[pl.ds(b * block, block), 0 : 2 * block] = both
+
+    def keep_mixed(b, result):
+        r.grad_mixed_own[pl.ds(b * block, block), :] = result.astype(BF)
+
+    monarch_backward(
+        lambda g: r.grad_branch[pl.ds(g * block, block), :],
+        lambda b: r.mixed[pl.ds(b * block, block), :],
+        r.out_shuffled, r.out_right, r.out_left, r.middle, keep_out_right, keep_out_left, keep_mixed,
+    )
+    mine = pl.ds(pl.multiple_of(me * rows, rows), rows)
+    own_chans = pl.ds(pl.multiple_of(me * chans, 16), chans)
+    mixed_copies = []
+    for k in SEQ_ORDER:
+        other = flip(me, k)
+        copy = pltpu.make_async_remote_copy(
+            src_ref=r.grad_mixed_own.at[pl.ds(pl.multiple_of(other * chans, 16), chans), :],
+            dst_ref=r.grad_mixed.at[:, mine],
+            send_sem=r.mixed_send.at[k],
+            recv_sem=r.mixed_recv.at[k],
+            device_id={"seq": other},
+            device_id_type=MESH,
+        )
+        copy.start()
+        mixed_copies.append(copy)
+    r.grad_mixed[:, mine] = r.grad_mixed_own[own_chans, :]
+    squares[0].start_second()
+
+    glus = []
+    for k in range(n_tp):
+        other = plane if k == 0 else neighbour_order(plane, n_tp - k)
+
+        def glu_step(at, carry, k=k, other=other):
+            cols = pl.ds(pl.multiple_of(at * chunk, chunk), chunk)
+            result = dot(r.hidden[other], r.down_v[:, cols])
+            if k == 0:
+                r.glu_own[:, cols] = result
+            else:
+                r.glu_send[other, :, cols] = result.astype(BF)
+            return carry
+
+        lax.fori_loop(0, pieces, glu_step, 0)
+        if k > 0:
+            copy = pltpu.make_async_remote_copy(
+                src_ref=r.glu_send.at[other],
+                dst_ref=r.glu_recv.at[plane],
+                send_sem=r.glu_ssem.at[other],
+                recv_sem=r.glu_rsem.at[plane],
+                device_id={"tp": other},
+                device_id_type=MESH,
+            )
+            copy.start()
+            glus.append(copy)
+    squares[1].start_second()
+    r.sums[...] = jnp.zeros_like(r.sums)
+    r.small_own[...] = jnp.zeros_like(r.small_own)
+    r.early_own[:, 384:512] = jnp.zeros((width, 128), BF)
+    r.padded[pl.ds(chans, 128 - chans), :] = jnp.zeros((128 - chans, length), BF)
+    loads.signals.wait()
+    loads.conv.wait()
+    for copy in mixed_copies:
+        copy.wait_recv()
 
     def short_step(at, carry):
         here = pl.ds(pl.multiple_of(at * step, step), step)
         shorted = []
         for s in range(3):
-            value = signals[s, here, :].astype(F32)
+            value = r.signals[s, here, :].astype(F32)
             shorted.append(
-                previous(value) * columns[here, 3 * s : 3 * s + 1]
-                + value * columns[here, 3 * s + 1 : 3 * s + 2]
-                + following(value) * columns[here, 3 * s + 2 : 3 * s + 3]
+                previous(value) * r.columns[here, 3 * s : 3 * s + 1]
+                + value * r.columns[here, 3 * s + 1 : 3 * s + 2]
+                + following(value) * r.columns[here, 3 * s + 2 : 3 * s + 3]
             )
-        query[here, :] = shorted[0]
-        value_v[here, :] = shorted[2]
-        above = grad_mixed[here, :].astype(F32)
-        grad_short[1, here, :] = above * conv[here, :]
+        r.query[here, :] = shorted[0]
+        r.value_v[here, :] = shorted[2]
+        above = r.grad_mixed[here, :].astype(F32)
+        r.grad_short[1, here, :] = above * r.conv[here, :]
         above = above * shorted[1]
-        grad_conv[here, :] = above
-        padded[here, :] = above.astype(BF)
-        sums[here, 9:10] = jnp.sum(above * shorted[0] * shorted[2], axis=1, keepdims=True)
-        sums[here, 10:11] = jnp.sum(above * sign_lanes(step, length), axis=1, keepdims=True)
+        r.grad_conv[here, :] = above
+        r.padded[here, :] = above.astype(BF)
+        r.sums[here, 9:10] = jnp.sum(above * shorted[0] * shorted[2], axis=1, keepdims=True)
+        r.sums[here, 10:11] = jnp.sum(above * sign_lanes(step, length), axis=1, keepdims=True)
         return carry
 
     lax.fori_loop(0, chans // step, short_step, 0)
-    for at in (2, 3, 4):
-        loads[at].wait()
-    chunk = 256
-    per = length // chunk
+    for copy in (loads.table, loads.wave, loads.taps):
+        copy.wait()
+    squares[2].start_second()
 
     def wave_step(at, carry):
         here = pl.ds(pl.multiple_of(at * chunk, chunk), chunk)
         sign = sign_rows(chunk, 128)
         index = lax.broadcasted_iota(jnp.int32, (chunk, 128), 0) + at * chunk
         weight = jnp.where(index == 0, 0.5 / length, 1.0 / length)
-        cos_part = dot(table_v[0, here, :], padded[...], NT)
-        sin_part = dot(table_v[1, here, :], padded[...], NT)
-        tap_cos = taps_v[0, here, :].astype(F32)
-        tap_sin = taps_v[1, here, :].astype(F32)
-        back_wave[0, here, :] = (cos_part * tap_cos + sin_part * tap_sin).astype(BF)
-        back_wave[1, here, :] = (sin_part * tap_cos - cos_part * tap_sin).astype(BF)
-        wave_cos = wave[0, here, :].astype(F32) * weight
-        wave_sin = wave[1, here, :].astype(F32) * weight
+        cos_part = dot(r.table_v[0, here, :], r.padded[...], NT)
+        sin_part = dot(r.table_v[1, here, :], r.padded[...], NT)
+        tap_cos = r.taps_v[0, here, :].astype(F32)
+        tap_sin = r.taps_v[1, here, :].astype(F32)
+        r.back_wave[0, here, :] = (cos_part * tap_cos + sin_part * tap_sin).astype(BF)
+        r.back_wave[1, here, :] = (sin_part * tap_cos - cos_part * tap_sin).astype(BF)
+        wave_cos = r.wave[0, here, :].astype(F32) * weight
+        wave_sin = r.wave[1, here, :].astype(F32) * weight
         result = cos_part * wave_cos + sin_part * wave_sin
-        cross[0, here, 0:128] = result.astype(BF)
-        cross[0, here, 128:256] = (result * sign).astype(BF)
+        r.cross[0, here, 0:128] = result.astype(BF)
+        r.cross[0, here, 128:256] = (result * sign).astype(BF)
         result = sin_part * wave_cos - cos_part * wave_sin
-        cross[1, here, 0:128] = result.astype(BF)
-        cross[1, here, 128:256] = (result * sign).astype(BF)
+        r.cross[1, here, 0:128] = result.astype(BF)
+        r.cross[1, here, 128:256] = (result * sign).astype(BF)
         return carry
 
     lax.fori_loop(0, per, wave_step, 0)
+    squares[0].start_second_back()
+    squares[1].start_second_back()
 
     def product_step(at, carry):
         here = pl.ds(pl.multiple_of(at * chunk, chunk), chunk)
-        result = dot(table_v[0, here, :], back_wave[0]) + dot(table_v[1, here, :], back_wave[1])
+        result = dot(r.table_v[0, here, :], r.back_wave[0]) + dot(r.table_v[1, here, :], r.back_wave[1])
         result = (
             result.T[:chans]
-            + sign_lanes(chans, chunk) * (sums[:chans, 10:11] * nyquist[:, 1:2] * (0.5 / length))
-            + columns[:, 9:10] * grad_conv[:, here]
+            + sign_lanes(chans, chunk) * (r.sums[:chans, 10:11] * r.nyquist[:, 1:2] * (0.5 / length))
+            + r.columns[:, 9:10] * r.grad_conv[:, here]
         )
-        grad_short[0, :, here] = result * value_v[:, here]
-        grad_short[2, :, here] = result * query[:, here]
+        r.grad_short[0, :, here] = result * r.value_v[:, here]
+        r.grad_short[2, :, here] = result * r.query[:, here]
         return carry
 
     lax.fori_loop(0, per, product_step, 0)
@@ -972,227 +1080,209 @@
     def signal_step(at, carry):
         here = pl.ds(pl.multiple_of(at * step, step), step)
         for s in range(3):
-            above = grad_short[s, here, :]
-            value = signals[s, here, :].astype(F32)
+            above = r.grad_short[s, here, :]
+            value = r.signals[s, here, :].astype(F32)
             before, after = previous(above), following(above)
-            grad_signals[s, here, :] = (
-                after * columns[here, 3 * s : 3 * s + 1]
-                + above * columns[here, 3 * s + 1 : 3 * s + 2]
-                + before * columns[here, 3 * s + 2 : 3 * s + 3]
+            r.grad_signals[s, here, :] = (
+                after * r.columns[here, 3 * s : 3 * s + 1]
+                + above * r.columns[here, 3 * s + 1 : 3 * s + 2]
+                + before * r.columns[here, 3 * s + 2 : 3 * s + 3]
             ).astype(BF)
-            sums[here, 3 * s : 3 * s + 1] = jnp.sum(after * value, axis=1, keepdims=True)
-            sums[here, 3 * s + 1 : 3 * s + 2] = jnp.sum(above * value, axis=1, keepdims=True)
-            sums[here, 3 * s + 2 : 3 * s + 3] = jnp.sum(before * value, axis=1, keepdims=True)
+            r.sums[here, 3 * s : 3 * s + 1] = jnp.sum(after * value, axis=1, keepdims=True)
+            r.sums[here, 3 * s + 1 : 3 * s + 2] = jnp.sum(above * value, axis=1, keepdims=True)
+            r.sums[here, 3 * s + 2 : 3 * s + 3] = jnp.sum(before * value, axis=1, keepdims=True)
         return carry
 
     lax.fori_loop(0, chans // step, signal_step, 0)
-    mine = pl.ds(pl.multiple_of(me * rows, rows), rows)
     seq_copies = []
     for k in SEQ_ORDER:
         other = flip(me, k)
         for s in range(3):
             copy = pltpu.make_async_remote_copy(
-                src_ref=grad_signals.at[s, :, pl.ds(pl.multiple_of(other * rows, rows), rows)],
-                dst_ref=grad_proj.at[pl.ds(pl.multiple_of(s * width + me * chans, 16), chans), :],
-                send_sem=seq_send.at[k, s],
-                recv_sem=seq_recv.at[k, s],
+                src_ref=r.grad_signals.at[s, :, pl.ds(pl.multiple_of(other * rows, rows), rows)],
+                dst_ref=r.grad_proj.at[pl.ds(pl.multiple_of(s * width + me * chans, 16), chans), :],
+                send_sem=r.seq_send.at[k, s],
+                recv_sem=r.seq_recv.at[k, s],
                 device_id={"seq": other},
                 device_id_type=MESH,
             )
             copy.start()
             seq_copies.append(copy)
     for s in range(3):
-        grad_proj[pl.ds(pl.multiple_of(s * width + me * chans, 16), chans), :] = grad_signals[s, :, mine]
-
-    loads[5].wait()
-    tap_total = jnp.broadcast_to(sums[:, 10:11], (128, 128)).T[0:1, :]
-    pad_nyquist = jnp.concatenate([nyquist[:, 0:1], jnp.zeros((128 - chans, 1), F32)], axis=0)
+        r.grad_proj[pl.ds(pl.multiple_of(s * width + me * chans, 16), chans), :] = r.grad_signals[s, :, mine]
+    squares[2].start_second_back()
+
+    total = r.resid[...] + r.glu_own[...] + from_planes(r.glu_rsem, r.glu_recv)
+    r.out_rows[...] = total.astype(BF)
+    part = rows // n_tp
+    out_copies = []
+    for k in range(1, n_tp):
+        other = flip(plane, k)
+        copy = pltpu.make_async_remote_copy(
+            src_ref=r.out_rows.at[pl.ds(pl.multiple_of(other * part, part), part), :],
+            dst_ref=r.output_v.at[plane],
+            send_sem=r.out_send.at[k],
+            recv_sem=r.out_recv.at[k],
+            device_id={"tp": other},
+            device_id_type=MESH,
+        )
+        copy.start()
+        out_copies.append(copy)
+    r.output_v[plane] = r.out_rows[pl.ds(pl.multiple_of(plane * part, part), part), :]
+
+    loads.acts.wait()
+    tap_total = jnp.broadcast_to(r.sums[:, 10:11], (128, 128)).T[0:1, :]
+    pad_nyquist = jnp.concatenate([r.nyquist[:, 0:1], jnp.zeros((128 - chans, 1), F32)], axis=0)
     tap_total = tap_total * jnp.broadcast_to(pad_nyquist, (128, 128)).T[0:1, :] * (0.5 / length)
-    grad_second[...] = jnp.zeros_like(grad_second)
-    grad_first[...] = jnp.zeros_like(grad_first)
-    grad_third[...] = jnp.zeros_like(grad_third)
+    r.grad_second[...] = jnp.zeros_like(r.grad_second)
+    r.grad_first[...] = jnp.zeros_like(r.grad_first)
+    r.grad_third[...] = jnp.zeros_like(r.grad_third)
 
     def filter_step(at, carry):
         here = pl.ds(pl.multiple_of(at * chunk, chunk), chunk)
-        result = dot(table_v[0, here, :], cross[0]) + dot(table_v[1, here, :], cross[1])
+        result = dot(r.table_v[0, here, :], r.cross[0]) + dot(r.table_v[1, here, :], r.cross[1])
         sign = sign_rows(chunk, 128)
-        for part in range(2):
-            above = (result[:, part * 128 : (part + 1) * 128] + sign * tap_total) * (length**-0.5)
-            if part == 1:
+        for half in range(2):
+            above = (result[:, half * 128 : (half + 1) * 128] + sign * tap_total) * (length**-0.5)
+            if half == 1:
                 index = lax.broadcasted_iota(jnp.int32, above.shape, 0) + at * chunk
                 above = jnp.where(index == 0, 0.0, above)
             above = above.astype(BF)
-            spot = pl.ds(pl.multiple_of(part * length + at * chunk, chunk), chunk)
-            grad_third[...] += dot(above, acts[2, spot, :], TN)
-            below = (dot(above, third[...]) * acts[3, spot, :].astype(F32)).astype(BF)
-            grad_second[...] += dot(acts[0, spot, :], below, TN)
-            below = (dot(below, second[...], NT) * acts[1, spot, :].astype(F32)).astype(BF)
-            grad_first[...] += dot(features[spot, :], below, TN)
+            spot = pl.ds(pl.multiple_of(half * length + at * chunk, chunk), chunk)
+            r.grad_third[...] += dot(above, r.acts[2, spot, :], TN)
+            below = (dot(above, r.third[...]) * r.acts[3, spot, :].astype(F32)).astype(BF)
+            r.grad_second[...] += dot(r.acts[0, spot, :], below, TN)
+            below = (dot(below, r.second[...], NT) * r.acts[1, spot, :].astype(F32)).astype(BF)
+            r.grad_first[...] += dot(r.features[spot, :], below, TN)
         return carry
 
     lax.fori_loop(0, per, filter_step, 0)
-    early.own[:, 0:384] = jnp.concatenate([grad_weights[0], grad_weights[1]], axis=1)
-    early.own[pl.ds(pl.multiple_of(me * chans, 16), chans), 384:512] = grad_third[:chans, :].astype(BF)
-    small.own[0:128, 0:128] = grad_second[...].astype(BF)
-    small.own[128:136, 0:128] = (grad_first[0:8, :] + grad_first[8:16, :]).astype(BF)
-    small.own[pl.ds(pl.multiple_of(me * 16, 16), 16), 128:256] = sums[...].T[0:16, :].astype(BF)
+    r.early_own[own_chans, 384:512] = r.grad_third[:chans, :].astype(BF)
+    r.small_own[0:128, 0:128] = r.grad_second[...].astype(BF)
+    r.small_own[128:136, 0:128] = (r.grad_first[0:8, :] + r.grad_first[8:16, :]).astype(BF)
+    r.small_own[pl.ds(pl.multiple_of(me * 16, 16), 16), 128:256] = r.sums[...].T[0:16, :].astype(BF)
     early.start_core()
-    for copy in ffn_copies:
-        copy.wait_recv()
-    own_shard.wait()
-    own_half = pl.ds(pl.multiple_of(lax.rem(me, 2) * half, half), half)
-    ffn_last = []
-    for which in range(3):
-        copy = pltpu.make_async_remote_copy(
-            src_ref=ffn_out.at[which, own_half, :],
-            dst_ref=ffn_out.at[which, own_half, :],
-            send_sem=ffn_ssem.at[which, 0],
-            recv_sem=ffn_rsem.at[which, 0],
-            device_id={"seq": flip(me, 1)},
-            device_id_type=MESH,
-        )
-        copy.start()
-        ffn_last.append(copy)
-    early.start_chip()
-
-    for at in range(6, 10):
-        loads[at].wait()
-    value = token_v[...].astype(F32)
-    shifted = value - jnp.mean(value, axis=-1, keepdims=True)
+    shifted = tokens - jnp.mean(tokens, axis=-1, keepdims=True)
     inverse = lax.rsqrt(jnp.mean(shifted * shifted, axis=-1, keepdims=True) + 1e-05)
-    scaled = shifted * inverse
-
-    groups = right.shape[0]
-    block = width // groups
-    fan = left.shape[2]
+    r.scaled[...] = shifted * inverse
+    loads.normed.wait()
+    loads.shuffled.wait()
+    fan = r.in_left.shape[2]
     for copy in seq_copies:
         copy.wait_recv()
+    squares[0].start_first_back()
+    squares[1].start_first_back()
+    early.start_chip()
+
+    in_parts = {}
 
     def keep_left(g, result):
-        late.own[pl.ds(g * block, block), 0:512] = result[:, 0:512].astype(BF)
-        middle_left[g] = result[:, 512:576].astype(BF)
+        r.late_own[pl.ds(g * block, block), 0:512] = result[:, 0:512].astype(BF)
+        in_parts[g] = result[:, 512:576].astype(BF)
 
     def keep_right(b, result):
-        late.own[pl.ds(b * block, block), 512:768] = jnp.concatenate([middle_left[b], result.astype(BF)], axis=1)
+        r.late_own[pl.ds(b * block, block), 512:768] = jnp.concatenate([in_parts[b], result.astype(BF)], axis=1)
 
     def keep_rows(b, result):
-        grad_rows[pl.ds(b * block, block), :] = result
-
-    middle_left = {}
+        r.grad_rows[pl.ds(b * block, block), :] = result
+
     monarch_backward(
-        lambda g: grad_proj[pl.ds(g * fan, fan), :],
-        lambda b: normed[pl.ds(b * block, block), :],
-        shuffled, right, left, middle, keep_right, keep_left, keep_rows,
-    )
-    late.start_core()
+        lambda g: r.grad_proj[pl.ds(g * fan, fan), :],
+        lambda b: r.in_normed[pl.ds(b * block, block), :],
+        r.in_shuffled, r.in_right, r.in_left, r.middle, keep_right, keep_left, keep_rows,
+    )
+    for late in lates:
+        late.start_core()
+    squares[2].start_first_back()
     early.start_plane()
-    total = grad_rows[...].T
-    norm_grads = [jnp.sum(total * scaled, axis=0, keepdims=True), jnp.sum(total, axis=0, keepdims=True)]
-    total = total * gain[...].reshape(1, width)
+    for late in lates:
+        late.start_chip()
+    total = r.grad_rows[...].T
+    scaled = r.scaled[...]
+    lines = [jnp.sum(total * scaled, axis=0, keepdims=True), jnp.sum(total, axis=0, keepdims=True)]
+    total = total * r.gain[...].reshape(1, width)
     first_mean = jnp.mean(total, axis=-1, keepdims=True)
     second_mean = jnp.mean(total * scaled, axis=-1, keepdims=True)
-    total = grad_resid[...] + inverse * (total - first_mean - scaled * second_mean)
-    grad_tok[...] = total.astype(BF)
-    norm_grads += [grad_vectors[0:1, :], grad_vectors[1:2, :]]
-    lines = []
-    for line in norm_grads:
-        for at in range(width // 128):
-            lines.append(line[:, at * 128 : (at + 1) * 128])
-    small.own[128:160, 128:256] = jnp.concatenate(lines + [jnp.zeros((8, 128), F32)], axis=0).astype(BF)
+    total = r.grad_resid[...] + inverse * (total - first_mean - scaled * second_mean)
+    r.grad_tok[...] = total.astype(BF)
+    token_line = Line(n_tp, r.tokens_out, r.tok_send, r.tok_recv)
+    token_line.begin(r.grad_tok)
+    own_tok = pltpu.make_async_copy(r.grad_tok, r.tokens_out.at[plane], r.local_sems.at[13])
+    own_tok.start()
+    lines += [r.grad_vectors[0:1, :], r.grad_vectors[1:2, :]]
+    packed = [row[:, at * 128 : (at + 1) * 128] for row in lines for at in range(width // 128)]
+    r.small_own[128:160, 128:256] = jnp.concatenate(packed + [jnp.zeros((8, 128), F32)], axis=0).astype(BF)
     small.start_core()
-    tok_copies = []
-    for k in range(1, n_tp):
-        copy = pltpu.make_async_remote_copy(
-            src_ref=grad_tok,
-            dst_ref=tokens_out.at[plane],
-            send_sem=tp_send.at[k],
-            recv_sem=tp_recv.at[k],
-            device_id={"tp": flip(plane, k)},
-            device_id_type=MESH,
-        )
-        copy.start()
-        tok_copies.append(copy)
-    own_tok = pltpu.make_async_copy(grad_tok, tokens_out.at[plane], local_sems.at[11])
-    own_tok.start()
-    late.start_chip()
+    early.start_plane_back()
     small.start_chip()
-    early.start_plane_back()
-    late.start_plane()
+    token_line.take(neighbour_order(plane, 1))
+    for late in lates:
+        late.start_plane()
     small.start_plane()
     early.start_chip_back()
-    late.start_plane_back()
+    for square in squares:
+        square.start_core_back()
+    token_line.take(neighbour_order(plane, 2))
+    for late in lates:
+        late.start_plane_back()
     small.start_plane_back()
+    for late in lates:
+        late.start_chip_back()
+    small.start_chip_back()
     early.start_core_back()
-    late.start_chip_back()
-    small.start_chip_back()
-    late.start_core_back()
+    token_line.take(neighbour_order(plane, 3))
+    ffn_copies = []
+    for which, square in enumerate(squares):
+        square.arrived()
+        copy = pltpu.make_async_copy(r.ffn_v.at[which], r.ffn_out.at[which], r.local_sems.at[14 + which])
+        copy.start()
+        ffn_copies.append(copy)
+    for late in lates:
+        late.start_core_back()
     small.start_core_back()
     early.finish()
-    early_out[...] = early.full[...]
+    r.early_out[...] = r.early_full[...]
     small.finish()
-    small_out[...] = small.full[...]
-    late.finish()
-    late_out[...] = late.full[...]
-    for copy in ffn_copies + seq_copies:
+    r.small_out[...] = r.small_full[...]
+    for copy in out_copies:
+        copy.wait()
+    r.output_out[...] = r.output_v[...]
+    for late in lates:
+        late.finish()
+    r.late_out[...] = r.late_full[...]
+    for copy in mixed_copies + seq_copies + backs + glus:
         copy.wait_send()
-    for copy in ffn_last + tok_copies:
+    for square in squares:
+        square.finish()
+    line.finish()
+    token_line.finish()
+    own_tok.wait()
+    for copy in ffn_copies:
         copy.wait()
-    own_tok.wait()
-
-
-def back(mesh_shape, *operands):
+
+
+def core(mesh_shape, *operands):
     n_seq, n_tp = mesh_shape
-    tokens = operands[12]
+    tokens = Inputs(*operands).tokens
     _, rows, width = tokens.shape
     chans, length = width // n_seq, rows * n_seq
+    scratch, groups = core_scratch(n_seq, n_tp, width, chans, length, rows)
     shape = jax.ShapeDtypeStruct
-    dma = pltpu.SemaphoreType.DMA
     return pl.pallas_call(
-        functools.partial(back_kernel, n_seq, n_tp, (width, chans, length, rows)),
+        functools.partial(core_kernel, n_seq, n_tp, (width, chans, length, rows)),
         out_shape=(
+            shape((n_tp, rows // n_tp, width), BF),
             shape((3, width, width), BF),
             shape((n_tp, rows, width), BF),
             shape((width, width), BF),
             shape((width, 512), BF),
             shape((256, 256), BF),
         ),
-        in_specs=[vmem_spec()] * 12 + [any_spec()] * 10,
-        out_specs=(any_spec(), any_spec(), vmem_spec(), vmem_spec(), vmem_spec()),
-        scratch_shapes=[
-            pltpu.VMEM((2, length, length), BF),
-            pltpu.VMEM((3, chans, length), BF),
-            pltpu.VMEM((chans, length), F32),
-            pltpu.VMEM((2, length, 128), BF),
-            pltpu.VMEM((2, length, 128), BF),
-            pltpu.VMEM((4, 2 * length, 128), BF),
-            pltpu.VMEM((rows, width), BF),
-            pltpu.VMEM((width, rows), BF),
-            pltpu.VMEM((width, rows), BF),
-            pltpu.VMEM((rows, width), F32),
-            pltpu.VMEM((3, chans, length), F32),
-            pltpu.VMEM((chans, length), F32),
-            pltpu.VMEM((chans, length), F32),
-            pltpu.VMEM((chans, length), F32),
-            pltpu.VMEM((128, length), BF),
-            pltpu.VMEM((2, length, 128), BF),
-            pltpu.VMEM((2, length, 256), BF),
-            pltpu.VMEM((128, 128), F32),
-            pltpu.VMEM((3, chans, length), BF),
-            pltpu.VMEM((3 * width, rows), BF),
-            pltpu.VMEM((width, rows), BF),
-            pltpu.VMEM((width, rows), F32),
-            pltpu.VMEM((rows, width), BF),
-            pltpu.VMEM((128, 128), F32),
-            pltpu.VMEM((16, 128), F32),
-            pltpu.VMEM((128, 128), F32),
-            dma((12,)),
-            dma((3, n_seq // 2)), dma((3, n_seq // 2)), dma((n_seq, 3)), dma((n_seq, 3)), dma((n_tp,)), dma((n_tp,)),
-        ]
-        + reduce_scratch(n_seq, n_tp, width, width)
-        + reduce_scratch(n_seq, n_tp, width, 512)
-        + reduce_scratch(n_seq, n_tp, 256, 256),
-        compiler_params=pltpu.CompilerParams(collective_id=2, has_side_effects=True, vmem_limit_bytes=LIMIT),
-        name="back",
+        in_specs=[vmem_spec()] * 13 + [any_spec()] * (len(Inputs._fields) - 13),
+        out_specs=(vmem_spec(), any_spec(), any_spec(), vmem_spec(), vmem_spec(), vmem_spec()),
+        scratch_shapes=list(scratch.values()) + sum(groups, []),
+        compiler_params=pltpu.CompilerParams(collective_id=1, has_side_effects=True, vmem_limit_bytes=60 * 1024 * 1024),
+        name="core",
     )(*operands)
 
 
@@ -1308,12 +1398,10 @@
         shape, tokens, cotangent, table, norm_gain, norm_bias, in_right, in_left, short_kernel.transpose(0, 2, 1), conv_bias,
         features, filter_first, filter_second, filter_third,
     )
-    grad_mixed, grad_resid, shard, grad_weights, grad_vectors, output = feed(
-        shape, mixed, tokens, cot_rows, ffn_gain, ffn_bias, out_right, out_left, gate_weight, up_weight, down_weight
-    )
-    ffn, grad_tokens, late, early, small = back(
-        shape, grad_mixed, columns, norm_gain, in_right, in_left, filter_second, third, nyquist, shard, grad_weights,
-        grad_vectors, features, tokens, table, signals, conv, wave, taps, acts, normed, shuffled, grad_resid,
+    output, ffn, grad_tokens, late, early, small = core(
+        shape, mixed, ffn_gain, ffn_bias, out_right, out_left, columns, norm_gain, in_right, in_left, filter_second, third,
+        nyquist, features, cot_rows, tokens, gate_weight, up_weight, down_weight, table, signals, conv, wave, taps, acts, normed,
+        shuffled,
     )
     grads = finish(chans, ffn, grad_tokens, late, early, small)
     return (output,) + grads[:5] + (grads[5].transpose(0, 2, 1),) + grads[6:]

time: 179 us -> 149 us (0.83)
  Pallas kernels: 178 us -> 148 us
    pallas_call x2 -> x1, Pallas kernels: 143 us -> 113 us  [core(): pl.pallas_call(functools.partial(core_kernel, n_seq, n_tp, (width, chans,...]
where the time goes in v4:
time: 149 us
  Pallas kernels  148 us (99%)
    pallas_call x1, Pallas kernels, core(): pl.pallas_call(functools.partial(core_kernel, n_seq, n_tp, (width, chans,...  113 us
    pallas_call x1, Pallas kernels, front(): pl.pallas_call(functools.partial(front_kernel, n_seq, n_tp, (width, chans...  26.3 us
    pallas_call x1, Pallas kernels, finish(): pl.pallas_call(functools.partial(finish_kernel, width, chans), out_shape=...  8.74 us

profile of v4, /device:TPU:0, one launch (start us, length us, event | category | flops | bytes accessed | tf_op | source)
XLA Modules:
  0.0 149.2 jit_solution(9193170541369262943)
XLA Ops:
  0.7 26.3 %front.1 = (bf16[768,128]{1,0:T(8,128)(2,1)}, bf16[3,96,1024]{2,1,0:T(8,128)(2,1)}, f32[96,1024]{1,0:T(8,128)}, bf16[2,1024,128]{2,1,0:T(8,128)(2,1)}, bf16[2,10...) custom-call(bf16[4,128,768]{2,1,0:T(8,128)(2,1)} %refs_14_.1, ...), custom_call_target="tpu_custom_call" | custom-call | tf_op jit(solution)/shard_map/front/pallas_call | solution.py:333
  27.0 112.8 %core.1 = (bf16[4,32,768]{2,1,0:T(8,128)(2,1)}, bf16[3,768,768]{2,1,0:T(8,128)(2,1)}, bf16[4,128,768]{2,1,0:T(8,128)(2,1)}, bf16[768,768]{1,0:T(8,128)(2,1)}, bf...) custom-call(bf16[768,128]{1,0:T(8,128)(2,1)} %get-tuple-element.53.refs_0_, f32[768]{0:T(1024)} %refs_1_.3, f32[768]{0:T(1024)} %refs_2_.2, ...), custom_call_target="tpu_custom_call" | custom-call | tf_op jit(solution)/shard_map/core/pallas_call | solution.py:1271
  139.8 0.0 copy-start
  139.8 8.7 %finish.1 = (f32[4,128,768]{2,1,0:T(8,128)}, f32[768]{0:T(1024)}, f32[768]{0:T(1024)}, f32[4,192,192]{2,1,0:T(8,128)}, f32[4,192,576]{2,1,0:T(8,128)}, /*index=5...) custom-call(bf16[3,768,768]{2,1,0:T(8,128)(2,1)} %get-tuple-element., ...), custom_call_target="tpu_custom_call" | custom-call | tf_op jit(solution)/shard_map/finish/pallas_call | solution.py:1350
  148.6 0.0 copy-done
  148.6 0.7 copy.39
Async XLA Ops:
  139.8 8.8 %copy-start = (bf16[4,32,768]{2,1,0:T(8,128)(2,1)S(1)}, bf16[4,32,768]{2,1,0:T(8,128)(2,1)}, u32[]{:S(2)}) copy-start(bf16[4,32,768]{2,1,0:T(8,128)(2,1)} %get-tuple-element.106) | copy-start | bytes 589828

commit v5 on v4

--- a/solution.py
+++ b/solution.py
@@ -108,25 +108,22 @@
 SEQ_ORDER = (6, 7, 2, 3, 4, 5, 1)
 
 
-def front_kernel(n_seq, n_tp, dims, *refs):
-    (tokens, cotangent, table, gain, bias, right, left, short, conv_bias, features, first, second, third) = refs[:13]
-    (mixed_out, signals_out, conv_out, wave_out, taps_out, nyquist_out, acts_out, normed_out, shuffled_out, cot_out,
-     columns_out, third_out) = refs[13:25]
-    (token_v, table_v, normed, shuffled, projected, signals, acts, spread, taps_v, padded, product, keyed, wave, spectrum, conv,
-     mixed, mixed_rows, nyquist, totals, columns, tall, turned, third_v,
-     local_sems, seq_send, seq_recv, back_send, back_recv, tp_send, tp_recv) = refs[25:]
+def front_part(n_seq, n_tp, dims, r, entered, loads):
     width, chans, length, rows = dims
     me, plane = lax.axis_index("seq"), lax.axis_index("tp")
-    entered = greet(n_seq, n_tp)
-    token_load = pltpu.make_async_copy(tokens.at[plane], token_v, local_sems.at[0])
-    token_load.start()
-    table_load = pltpu.make_async_copy(table, table_v, local_sems.at[1])
-    table_load.start()
-    token_load.wait()
+    cotangent, right, left, features = r.cotangent, r.in_right, r.in_left, r.features
+    token_v, table_v, normed, shuffled, signals = r.token_v, r.table_v, r.in_normed, r.in_shuffled, r.signals
+    acts, taps_v, padded, wave, conv, nyquist, columns, third_v = (
+        r.acts, r.taps_v, r.padded, r.wave, r.conv, r.nyquist, r.columns, r.third_v
+    )
+    projected, spread, product, keyed, spectrum, mixed, totals = (
+        r.projected, r.spread, r.product, r.query, r.back_wave, r.front_mixed, r.totals
+    )
+    loads.token.wait()
     value = token_v[...].astype(F32)
     shifted = value - jnp.mean(value, axis=-1, keepdims=True)
     inverse = lax.rsqrt(jnp.mean(shifted * shifted, axis=-1, keepdims=True) + 1e-05)
-    value = shifted * inverse * gain[...].reshape(1, width) + bias[...].reshape(1, width)
+    value = shifted * inverse * r.gain[...].reshape(1, width) + r.bias[...].reshape(1, width)
     normed[...] = value.T.astype(BF)
     groups = right.shape[0]
     block = width // groups
@@ -145,8 +142,8 @@
             copy = pltpu.make_async_remote_copy(
                 src_ref=projected.at[pl.ds(pl.multiple_of(s * width + other * chans, 16), chans), :],
                 dst_ref=signals.at[s, :, mine],
-                send_sem=seq_send.at[k, s],
-                recv_sem=seq_recv.at[k, s],
+                send_sem=r.front_send.at[k, s],
+                recv_sem=r.front_recv.at[k, s],
                 device_id={"seq": other},
                 device_id_type=MESH,
             )
@@ -160,34 +157,26 @@
     for k in range(1, n_tp):
         copy = pltpu.make_async_remote_copy(
             src_ref=cotangent,
-            dst_ref=cot_out.at[:, spot, :],
-            send_sem=tp_send.at[k],
-            recv_sem=tp_recv.at[k],
+            dst_ref=r.cot_v.at[:, spot, :],
+            send_sem=r.cot_send.at[k],
+            recv_sem=r.cot_recv.at[k],
             device_id={"tp": flip(plane, k)},
             device_id_type=MESH,
         )
         copy.start()
         cot_copies.append(copy)
-    own_cot = pltpu.make_async_copy(cotangent, cot_out.at[:, spot, :], local_sems.at[2])
+    own_cot = pltpu.make_async_copy(cotangent, r.cot_v.at[:, spot, :], r.local_sems.at[17])
     own_cot.start()
-    out_copies = [
-        pltpu.make_async_copy(normed, normed_out, local_sems.at[3]),
-        pltpu.make_async_copy(shuffled, shuffled_out, local_sems.at[4]),
-    ]
-    for copy in out_copies:
-        copy.start()
 
     own = pl.ds(pl.multiple_of(me * chans, 16), chans)
-    lines = [short[s].astype(F32) for s in range(3)]
-    lines += [conv_bias[...].reshape(1, width), jnp.zeros((6, width), F32)]
-    tall[...] = jnp.concatenate(lines, axis=0).T
-    columns[...] = tall[own, :]
-    columns_out[...] = columns[...]
-    turned[...] = third[...].T
-    third_v[pl.ds(0, chans), :] = turned[own, :]
+    lines = [r.short[s].astype(F32) for s in range(3)]
+    lines += [r.conv_bias[...].reshape(1, width), jnp.zeros((6, width), F32)]
+    r.tall[...] = jnp.concatenate(lines, axis=0).T
+    columns[...] = r.tall[own, :]
+    r.third_turned[...] = r.third[...].T
+    third_v[pl.ds(0, chans), :] = r.third_turned[own, :]
     third_v[pl.ds(chans, 128 - chans), :] = jnp.zeros((128 - chans, 128), BF)
-    third_out[...] = third_v[...]
-    lead = jnp.concatenate([first[...].astype(F32), jnp.zeros((3, 128), F32)], axis=0)
+    lead = jnp.concatenate([r.first[...].astype(F32), jnp.zeros((3, 128), F32)], axis=0)
     lead = jnp.concatenate([lead, lead], axis=0).astype(BF)
 
     chunk = 256
@@ -203,7 +192,7 @@
             acts[0, here, :] = high
             acts[1, here, :] = cosine.astype(BF)
             low = (sine - high.astype(F32)).astype(BF)
-            sine, cosine = sin_cos(dot(high, second[...]) + dot(low, second[...]))
+            sine, cosine = sin_cos(dot(high, r.second[...]) + dot(low, r.second[...]))
             high = sine.astype(BF)
             acts[2, here, :] = high
             acts[3, here, :] = cosine.astype(BF)
@@ -216,10 +205,7 @@
             return carry
 
         lax.fori_loop(0, per, tap_step, 0)
-    acts_copy = pltpu.make_async_copy(acts, acts_out, local_sems.at[5])
-    acts_copy.start()
-    out_copies.append(acts_copy)
-    table_load.wait()
+    loads.table.wait()
 
     def spectrum_step(at, carry):
         here = pl.ds(pl.multiple_of(at * chunk, chunk), chunk)
@@ -232,16 +218,10 @@
         return carry
 
     lax.fori_loop(0, per, spectrum_step, 0)
-    copy = pltpu.make_async_copy(taps_v, taps_out, local_sems.at[6])
-    copy.start()
-    out_copies.append(copy)
     tap_total = jnp.broadcast_to(totals[...], (128, 128)).T[:chans, 0:1]
 
     for copy in sends:
         copy.wait_recv()
-    copy = pltpu.make_async_copy(signals, signals_out, local_sems.at[7])
-    copy.start()
-    out_copies.append(copy)
 
     step = 16
     padded[pl.ds(chans, 128 - chans), :] = jnp.zeros((128 - chans, length), BF)
@@ -300,89 +280,18 @@
         other = flip(me, k)
         copy = pltpu.make_async_remote_copy(
             src_ref=mixed.at[:, pl.ds(pl.multiple_of(other * rows, rows), rows)],
-            dst_ref=mixed_rows.at[slot, :],
-            send_sem=back_send.at[k],
-            recv_sem=back_recv.at[k],
+            dst_ref=r.mixed.at[slot, :],
+            send_sem=r.mix_send.at[k],
+            recv_sem=r.mix_recv.at[k],
             device_id={"seq": other},
             device_id_type=MESH,
         )
         copy.start()
         backs.append(copy)
-    mixed_rows[slot, :] = mixed[:, mine]
-    for at, pair in enumerate(((wave, wave_out), (conv, conv_out), (nyquist, nyquist_out))):
-        copy = pltpu.make_async_copy(pair[0], pair[1], local_sems.at[8 + at])
-        copy.start()
-        out_copies.append(copy)
-    for copy in sends:
-        copy.wait_send()
-    for copy in cot_copies:
-        copy.wait()
-    own_cot.wait()
+    r.mixed[slot, :] = mixed[:, mine]
     for copy in backs:
-        copy.wait()
-    mixed_out[...] = mixed_rows[...]
-    for copy in out_copies:
-        copy.wait()
-
-
-def front(mesh_shape, *operands):
-    n_seq, n_tp = mesh_shape
-    _, rows, width = operands[0].shape
-    chans, length = width // n_seq, rows * n_seq
-    shape = jax.ShapeDtypeStruct
-    return pl.pallas_call(
-        functools.partial(front_kernel, n_seq, n_tp, (width, chans, length, rows)),
-        out_shape=(
-            shape((width, rows), BF),
-            shape((3, chans, length), BF),
-            shape((chans, length), F32),
-            shape((2, length, 128), BF),
-            shape((2, length, 128), BF),
-            shape((chans, 128), F32),
-            shape((4, 2 * length, 128), BF),
-            shape((width, rows), BF),
-            shape((width, rows), BF),
-            shape((n_tp, rows, width), BF),
-            shape((chans, 16), F32),
-            shape((128, 128), BF),
-        ),
-        in_specs=[any_spec()] * 3 + [vmem_spec()] * 10,
-        out_specs=(vmem_spec(),) + (any_spec(),) * 9 + (vmem_spec(),) * 2,
-        scratch_shapes=[
-            pltpu.VMEM((rows, width), BF),
-            pltpu.VMEM((2, length, length), BF),
-            pltpu.VMEM((width, rows), BF),
-            pltpu.VMEM((width, rows), BF),
-            pltpu.VMEM((3 * width, rows), BF),
-            pltpu.VMEM((3, chans, length), BF),
-            pltpu.VMEM((4, 2 * length, 128), BF),
-            pltpu.VMEM((length, 256), BF),
-            pltpu.VMEM((2, length, 128), BF),
-            pltpu.VMEM((128, length), BF),
-            pltpu.VMEM((chans, length), F32),
-            pltpu.VMEM((chans, length), F32),
-            pltpu.VMEM((2, length, 128), BF),
-            pltpu.VMEM((2, length, 128), BF),
-            pltpu.VMEM((chans, length), F32),
-            pltpu.VMEM((chans, length), BF),
-            pltpu.VMEM((width, rows), BF),
-            pltpu.VMEM((chans, 128), F32),
-            pltpu.VMEM((1, 128), F32),
-            pltpu.VMEM((chans, 16), F32),
-            pltpu.VMEM((width, 16), F32),
-            pltpu.VMEM((width, 128), BF),
-            pltpu.VMEM((128, 128), BF),
-            pltpu.SemaphoreType.DMA((12,)),
-            pltpu.SemaphoreType.DMA((n_seq, 3)),
-            pltpu.SemaphoreType.DMA((n_seq, 3)),
-            pltpu.SemaphoreType.DMA((n_seq,)),
-            pltpu.SemaphoreType.DMA((n_seq,)),
-            pltpu.SemaphoreType.DMA((n_tp,)),
-            pltpu.SemaphoreType.DMA((n_tp,)),
-        ],
-        compiler_params=pltpu.CompilerParams(collective_id=0, has_side_effects=True, vmem_limit_bytes=LIMIT),
-        name="front",
-    )(*operands)
+        copy.wait_recv()
+    return sends + backs, cot_copies, own_cot
 
 
 def split_table(values):
@@ -638,32 +547,26 @@
 
 
 class Inputs(typing.NamedTuple):
-    mixed: typing.Any
     feed_gain: typing.Any
     feed_bias: typing.Any
     out_right: typing.Any
     out_left: typing.Any
-    columns: typing.Any
     gain: typing.Any
+    bias: typing.Any
     in_right: typing.Any
     in_left: typing.Any
+    short: typing.Any
+    conv_bias: typing.Any
+    features: typing.Any
+    first: typing.Any
     second: typing.Any
     third: typing.Any
-    nyquist: typing.Any
-    features: typing.Any
-    cot_rows: typing.Any
     tokens: typing.Any
+    cotangent: typing.Any
+    table: typing.Any
     gate_w: typing.Any
     up_w: typing.Any
     down_w: typing.Any
-    table: typing.Any
-    signals_in: typing.Any
-    conv_in: typing.Any
-    wave_in: typing.Any
-    taps_in: typing.Any
-    acts_in: typing.Any
-    normed_in: typing.Any
-    shuffled_in: typing.Any
 
 
 class Outputs(typing.NamedTuple):
@@ -753,6 +656,23 @@
         seq_recv=pltpu.SemaphoreType.DMA((n_seq,3)),
         ffn_send=pltpu.SemaphoreType.DMA((3,10)),
         ffn_recv=pltpu.SemaphoreType.DMA((3,10)),
+        mixed=pltpu.VMEM((width, rows), BF),
+        front_mixed=pltpu.VMEM((chans, length), BF),
+        nyquist=pltpu.VMEM((chans, 128), F32),
+        columns=pltpu.VMEM((chans, 16), F32),
+        third_v=pltpu.VMEM((128, 128), BF),
+        projected=pltpu.VMEM((3 * width, rows), BF),
+        spread=pltpu.VMEM((length, 256), BF),
+        product=pltpu.VMEM((chans, length), F32),
+        totals=pltpu.VMEM((1, 128), F32),
+        tall=pltpu.VMEM((width, 16), F32),
+        third_turned=pltpu.VMEM((width, 128), BF),
+        front_send=pltpu.SemaphoreType.DMA((n_seq, 3)),
+        front_recv=pltpu.SemaphoreType.DMA((n_seq, 3)),
+        mix_send=pltpu.SemaphoreType.DMA((n_seq,)),
+        mix_recv=pltpu.SemaphoreType.DMA((n_seq,)),
+        cot_send=pltpu.SemaphoreType.DMA((n_tp,)),
+        cot_recv=pltpu.SemaphoreType.DMA((n_tp,)),
         late_own=pltpu.VMEM((width, width), BF),
         late_full=pltpu.VMEM((width, width), BF),
         early_own=pltpu.VMEM((width, 512), BF),
@@ -788,18 +708,10 @@
     entered = greet(n_seq, n_tp)
     sources = dict(
         token=(r.tokens.at[plane], r.token_v),
-        cot=(r.cot_rows, r.cot_v),
         down=(r.down_w, r.down_v),
         gate=(r.gate_w, r.gate_v),
         up=(r.up_w, r.up_v),
-        signals=(r.signals_in, r.signals),
-        conv=(r.conv_in, r.conv),
         table=(r.table, r.table_v),
-        wave=(r.wave_in, r.wave),
-        taps=(r.taps_in, r.taps_v),
-        acts=(r.acts_in, r.acts),
-        normed=(r.normed_in, r.in_normed),
-        shuffled=(r.shuffled_in, r.in_shuffled),
     )
     copies = {
         name: pltpu.make_async_copy(*pair, r.local_sems.at[at]) for at, (name, pair) in enumerate(sources.items())
@@ -807,6 +719,7 @@
     for copy in copies.values():
         copy.start()
     loads = types.SimpleNamespace(**copies)
+    front_sends, cot_copies, own_cot = front_part(n_seq, n_tp, dims, r, entered, loads)
     _, block, _ = r.out_right.shape
     chunk = 256
     pieces = width // chunk
@@ -831,7 +744,6 @@
         r.branch[pl.ds(g * block, block), :] = result
 
     monarch_forward(lambda b: r.mixed[pl.ds(b * block, block), :], r.out_right, r.out_left, r.out_shuffled, keep_branch)
-    loads.token.wait()
     tokens = r.token_v[...].astype(F32)
     value = tokens + r.branch[...].T
     r.resid[...] = value
@@ -840,10 +752,11 @@
     value = shifted * r.inverse[...]
     r.scaled[...] = value
     r.normed[plane] = (value * r.feed_gain[...].reshape(1, width) + r.feed_bias[...].reshape(1, width)).astype(BF)
-    entered()
     line = Line(n_tp, r.normed, r.line_send, r.line_recv)
     line.begin(r.normed.at[plane])
-    loads.cot.wait()
+    for copy in cot_copies:
+        copy.wait_recv()
+    own_cot.wait()
     loads.down.wait()
 
     def hidden_step(at, carry):
@@ -1007,8 +920,6 @@
     r.small_own[...] = jnp.zeros_like(r.small_own)
     r.early_own[:, 384:512] = jnp.zeros((width, 128), BF)
     r.padded[pl.ds(chans, 128 - chans), :] = jnp.zeros((128 - chans, length), BF)
-    loads.signals.wait()
-    loads.conv.wait()
     for copy in mixed_copies:
         copy.wait_recv()
 
@@ -1034,8 +945,6 @@
         return carry
 
     lax.fori_loop(0, chans // step, short_step, 0)
-    for copy in (loads.table, loads.wave, loads.taps):
-        copy.wait()
     squares[2].start_second()
 
     def wave_step(at, carry):
@@ -1130,7 +1039,6 @@
         out_copies.append(copy)
     r.output_v[plane] = r.out_rows[pl.ds(pl.multiple_of(plane * part, part), part), :]
 
-    loads.acts.wait()
     tap_total = jnp.broadcast_to(r.sums[:, 10:11], (128, 128)).T[0:1, :]
     pad_nyquist = jnp.concatenate([r.nyquist[:, 0:1], jnp.zeros((128 - chans, 1), F32)], axis=0)
     tap_total = tap_total * jnp.broadcast_to(pad_nyquist, (128, 128)).T[0:1, :] * (0.5 / length)
@@ -1150,7 +1058,7 @@
             above = above.astype(BF)
             spot = pl.ds(pl.multiple_of(half * length + at * chunk, chunk), chunk)
             r.grad_third[...] += dot(above, r.acts[2, spot, :], TN)
-            below = (dot(above, r.third[...]) * r.acts[3, spot, :].astype(F32)).astype(BF)
+            below = (dot(above, r.third_v[...]) * r.acts[3, spot, :].astype(F32)).astype(BF)
             r.grad_second[...] += dot(r.acts[0, spot, :], below, TN)
             below = (dot(below, r.second[...], NT) * r.acts[1, spot, :].astype(F32)).astype(BF)
             r.grad_first[...] += dot(r.features[spot, :], below, TN)
@@ -1165,8 +1073,6 @@
     shifted = tokens - jnp.mean(tokens, axis=-1, keepdims=True)
     inverse = lax.rsqrt(jnp.mean(shifted * shifted, axis=-1, keepdims=True) + 1e-05)
     r.scaled[...] = shifted * inverse
-    loads.normed.wait()
-    loads.shuffled.wait()
     fan = r.in_left.shape[2]
     for copy in seq_copies:
         copy.wait_recv()
@@ -1186,17 +1092,13 @@
     def keep_rows(b, result):
         r.grad_rows[pl.ds(b * block, block), :] = result
 
-    monarch_backward(
-        lambda g: r.grad_proj[pl.ds(g * fan, fan), :],
-        lambda b: r.in_normed[pl.ds(b * block, block), :],
-        r.in_shuffled, r.in_right, r.in_left, r.middle, keep_right, keep_left, keep_rows,
-    )
-    for late in lates:
-        late.start_core()
-    squares[2].start_first_back()
-    early.start_plane()
-    for late in lates:
-        late.start_chip()
+    part = block // 4
+    for g in range(4):
+        below = dot(r.in_left[g], r.grad_proj[pl.ds(g * fan, fan), :]).astype(BF)
+        for b in range(4):
+            r.middle[pl.ds(b * block + g * part, part), :] = below[b * part : (b + 1) * part]
+    for b in range(4):
+        keep_rows(b, dot(r.in_right[b], r.middle[pl.ds(b * block, block), :]))
     total = r.grad_rows[...].T
     scaled = r.scaled[...]
     lines = [jnp.sum(total * scaled, axis=0, keepdims=True), jnp.sum(total, axis=0, keepdims=True)]
@@ -1209,6 +1111,16 @@
     token_line.begin(r.grad_tok)
     own_tok = pltpu.make_async_copy(r.grad_tok, r.tokens_out.at[plane], r.local_sems.at[13])
     own_tok.start()
+    for g in range(4):
+        keep_left(g, dot(r.in_shuffled[pl.ds(g * block, block), :], r.grad_proj[pl.ds(g * fan, fan), :], NT))
+    for b in range(4):
+        keep_right(b, dot(r.in_normed[pl.ds(b * block, block), :], r.middle[pl.ds(b * block, block), :], NT))
+    for late in lates:
+        late.start_core()
+    squares[2].start_first_back()
+    early.start_plane()
+    for late in lates:
+        late.start_chip()
     lines += [r.grad_vectors[0:1, :], r.grad_vectors[1:2, :]]
     packed = [row[:, at * 128 : (at + 1) * 128] for row in lines for at in range(width // 128)]
     r.small_own[128:160, 128:256] = jnp.concatenate(packed + [jnp.zeros((8, 128), F32)], axis=0).astype(BF)
@@ -1250,7 +1162,7 @@
     for late in lates:
         late.finish()
     r.late_out[...] = r.late_full[...]
-    for copy in mixed_copies + seq_copies + backs + glus:
+    for copy in mixed_copies + seq_copies + backs + glus + front_sends + cot_copies:
         copy.wait_send()
     for square in squares:
         square.finish()
@@ -1278,11 +1190,11 @@
             shape((width, 512), BF),
             shape((256, 256), BF),
         ),
-        in_specs=[vmem_spec()] * 13 + [any_spec()] * (len(Inputs._fields) - 13),
+        in_specs=[vmem_spec()] * 14 + [any_spec()] * (len(Inputs._fields) - 14),
         out_specs=(vmem_spec(), any_spec(), any_spec(), vmem_spec(), vmem_spec(), vmem_spec()),
         scratch_shapes=list(scratch.values()) + sum(groups, []),
-        compiler_params=pltpu.CompilerParams(collective_id=1, has_side_effects=True, vmem_limit_bytes=60 * 1024 * 1024),
-        name="core",
+        compiler_params=pltpu.CompilerParams(collective_id=0, has_side_effects=True, vmem_limit_bytes=60 * 1024 * 1024),
+        name="layer",
     )(*operands)
 
 
@@ -1290,15 +1202,16 @@
     (ffn, tokens, late, early, small) = refs[:5]
     (grad_tokens, norm_gain, norm_bias, in_right, in_left, short, first, second, third, conv_bias, out_right, out_left,
      ffn_gain, ffn_bias, gate, up, down) = refs[5:22]
-    (ffn_v, ffn_f, token_v, token_f, in_sems, out_sems) = refs[22:]
-    loads = [pltpu.make_async_copy(ffn.at[which], ffn_v.at[which], in_sems.at[which]) for which in range(3)]
-    loads.append(pltpu.make_async_copy(tokens, token_v, in_sems.at[3]))
+    (ffn_v, ffn_f, token_v, token_f, late_v, early_v, in_right_f, in_left_f, out_right_f, out_left_f, in_sems, out_sems) = refs[22:]
+    pairs = [(ffn.at[which], ffn_v.at[which]) for which in range(3)] + [(tokens, token_v), (late, late_v), (early, early_v)]
+    loads = [pltpu.make_async_copy(*pair, in_sems.at[at]) for at, pair in enumerate(pairs)]
     for copy in loads:
         copy.start()
-    stores = [
-        pltpu.make_async_copy(ffn_f.at[which], target, out_sems.at[which]) for which, target in enumerate((gate, up, down))
+    pairs = [(ffn_f.at[which], target) for which, target in enumerate((gate, up, down))]
+    pairs += [
+        (token_f, grad_tokens), (in_right_f, in_right), (in_left_f, in_left), (out_right_f, out_right), (out_left_f, out_left)
     ]
-    stores.append(pltpu.make_async_copy(token_f, grad_tokens, out_sems.at[3]))
+    stores = [pltpu.make_async_copy(*pair, out_sems.at[at]) for at, pair in enumerate(pairs)]
     chunk = 64
     for which in range(3):
         loads[which].wait()
@@ -1319,13 +1232,21 @@
     lax.fori_loop(0, token_v.shape[0], token_step, 0)
     stores[3].start()
     groups, block, _ = in_right.shape
+    loads[4].wait()
     for b in range(groups):
         here = pl.ds(b * block, block)
-        in_left[b] = late[here, 0 : 3 * block].astype(F32)
-        in_right[b] = late[here, 3 * block : 4 * block].astype(F32)
-        out_right[b] = early[here, 0:block].astype(F32)
-        out_left[b] = early[here, block : 2 * block].astype(F32)
-    third[...] = early[:, 384:512].astype(F32).T
+        in_left_f[b] = late_v[here, 0 : 3 * block].astype(F32)
+        in_right_f[b] = late_v[here, 3 * block : 4 * block].astype(F32)
+    stores[4].start()
+    stores[5].start()
+    loads[5].wait()
+    for b in range(groups):
+        here = pl.ds(b * block, block)
+        out_right_f[b] = early_v[here, 0:block].astype(F32)
+        out_left_f[b] = early_v[here, block : 2 * block].astype(F32)
+    stores[6].start()
+    stores[7].start()
+    third[...] = early_v[:, 384:512].astype(F32).T
     values = small[...].astype(F32)
     second[...] = values[0:128, 0:128]
     first[...] = values[128:133, 0:128]
@@ -1347,22 +1268,32 @@
     shape = jax.ShapeDtypeStruct
     vector = shape((width,), F32)
     square = shape((4, block, block), F32)
+    wide = shape((4, block, 3 * block), F32)
     return pl.pallas_call(
         functools.partial(finish_kernel, width, chans),
         out_shape=(
-            shape(tokens.shape, F32), vector, vector, square, shape((4, block, 3 * block), F32), shape((3, 3, width), F32),
+            shape(tokens.shape, F32), vector, vector, square, wide, shape((3, 3, width), F32),
             shape((5, 128), F32), shape((128, 128), F32), shape((128, width), F32), vector, square, square, vector, vector,
         )
         + (shape((width, width), F32),) * 3,
-        in_specs=[any_spec()] * 2 + [vmem_spec()] * 3,
-        out_specs=(any_spec(),) + (vmem_spec(),) * 13 + (any_spec(),) * 3,
+        in_specs=[any_spec()] * 4 + [vmem_spec()],
+        out_specs=(any_spec(), vmem_spec(), vmem_spec(), any_spec(), any_spec())
+        + (vmem_spec(),) * 5
+        + (any_spec(), any_spec(), vmem_spec(), vmem_spec())
+        + (any_spec(),) * 3,
         scratch_shapes=[
             pltpu.VMEM(ffn.shape, BF),
             pltpu.VMEM(ffn.shape, F32),
             pltpu.VMEM(tokens.shape, BF),
             pltpu.VMEM(tokens.shape, F32),
-            pltpu.SemaphoreType.DMA((4,)),
-            pltpu.SemaphoreType.DMA((4,)),
+            pltpu.VMEM(late.shape, BF),
+            pltpu.VMEM(early.shape, BF),
+            pltpu.VMEM(square.shape, F32),
+            pltpu.VMEM(wide.shape, F32),
+            pltpu.VMEM(square.shape, F32),
+            pltpu.VMEM(square.shape, F32),
+            pltpu.SemaphoreType.DMA((6,)),
+            pltpu.SemaphoreType.DMA((8,)),
         ],
         compiler_params=pltpu.CompilerParams(vmem_limit_bytes=LIMIT),
         name="finish",
@@ -1394,14 +1325,10 @@
     chans, length = width // n_seq, rows * n_seq
     shape = (n_seq, n_tp)
     table, features = (jnp.asarray(array) for array in constants(length))
-    mixed, signals, conv, wave, taps, nyquist, acts, normed, shuffled, cot_rows, columns, third = front(
-        shape, tokens, cotangent, table, norm_gain, norm_bias, in_right, in_left, short_kernel.transpose(0, 2, 1), conv_bias,
-        features, filter_first, filter_second, filter_third,
-    )
     output, ffn, grad_tokens, late, early, small = core(
-        shape, mixed, ffn_gain, ffn_bias, out_right, out_left, columns, norm_gain, in_right, in_left, filter_second, third,
-        nyquist, features, cot_rows, tokens, gate_weight, up_weight, down_weight, table, signals, conv, wave, taps, acts, normed,
-        shuffled,
+        shape, ffn_gain, ffn_bias, out_right, out_left, norm_gain, norm_bias, in_right, in_left, short_kernel.transpose(0, 2, 1),
+        conv_bias, features, filter_first, filter_second, filter_third, tokens, cotangent, table, gate_weight, up_weight,
+        down_weight,
     )
     grads = finish(chans, ffn, grad_tokens, late, early, small)
     return (output,) + grads[:5] + (grads[5].transpose(0, 2, 1),) + grads[6:]

time: 149 us -> 143 us (0.960)
  Pallas kernels: 148 us -> 142 us
    pallas_call x1 -> x0, Pallas kernels: 26.3 us -> none  [front(): pl.pallas_call(functools.partial(front_kernel, n_seq, n_tp, (width, chans...]
    pallas_call x1, Pallas kernels: 113 us -> 134 us  [core(): pl.pallas_call(functools.partial(core_kernel, n_seq, n_tp, (width, chans,...]
where the time goes in v5:
time: 143 us
  Pallas kernels  142 us (99%)
    pallas_call x1, Pallas kernels, core(): pl.pallas_call(functools.partial(core_kernel, n_seq, n_tp, (width, chans,...  134 us
    pallas_call x1, Pallas kernels, finish(): pl.pallas_call(functools.partial(finish_kernel, width, chans), out_shape=...  8.02 us

profile of v5, /device:TPU:0, one launch (start us, length us, event | category | flops | bytes accessed | tf_op | source)
XLA Modules:
  0.0 143.1 jit_solution(5176083362228460293)
XLA Ops:
  0.7 133.7 %layer.1 = (bf16[4,32,768]{2,1,0:T(8,128)(2,1)}, bf16[3,768,768]{2,1,0:T(8,128)(2,1)}, bf16[4,128,768]{2,1,0:T(8,128)(2,1)}, bf16[768,768]{1,0:T(8,128)(2,1)}, b...) custom-call(f32[768]{0:T(1024)} %refs_0_.1, f32[768]{0:T(1024)} %refs_1_.1, bf16[4,192,192]{2,1,0:T(8,128)(2,1)} %refs_2_.1, ...), custom_call_target="tpu_custom_call" | custom-call | tf_op jit(solution)/shard_map/layer/pallas_call | solution.py:1183
  134.3 0.0 copy-start
  134.3 8.0 %finish.1 = (f32[4,128,768]{2,1,0:T(8,128)}, f32[768]{0:T(1024)}, f32[768]{0:T(1024)}, f32[4,192,192]{2,1,0:T(8,128)}, f32[4,192,576]{2,1,0:T(8,128)}, /*index=5...) custom-call(bf16[3,768,768]{2,1,0:T(8,128)(2,1)} %get-tuple-element., ...), custom_call_target="tpu_custom_call" | custom-call | tf_op jit(solution)/shard_map/finish/pallas_call | solution.py:1272
  142.4 0.0 copy-done
  142.4 0.7 copy.39
Async XLA Ops:
  134.3 8.0 %copy-start = (bf16[4,32,768]{2,1,0:T(8,128)(2,1)S(1)}, bf16[4,32,768]{2,1,0:T(8,128)(2,1)}, u32[]{:S(2)}) copy-start(bf16[4,32,768]{2,1,0:T(8,128)(2,1)} %get-tuple-element.82) | copy-start | bytes 589828

commit v6 on v5

--- a/solution.py
+++ b/solution.py
@@ -425,6 +425,11 @@
     return result + upper * (3 - 2 * result)
 
 
+def work_order(plane):
+    odd = lax.rem(plane, 2)
+    return 1 + odd, lax.rem(plane + 2, 4), 3 - 3 * odd
+
+
 class Line:
     def __init__(self, n_tp, slots, send, recv):
         self.n_tp, self.slots, self.send, self.recv = n_tp, slots, send, recv
@@ -448,14 +453,21 @@
         self.start(self.plane, source, 0, self.plane < self.n_tp - 1)
         self.start(self.plane, source, 1, self.plane > 0)
 
-    def take(self, block):
-        pltpu.make_async_remote_copy(
+    def take(self, block, here=None):
+        arrival = pltpu.make_async_remote_copy(
             src_ref=self.slots.at[block], dst_ref=self.slots.at[block], send_sem=self.send.at[0, block],
             recv_sem=self.recv.at[block], device_id={"tp": block}, device_id_type=MESH,
-        ).wait_recv()
+        )
+        up = jnp.logical_and(block < self.plane, self.plane < self.n_tp - 1)
+        down = jnp.logical_and(block > self.plane, self.plane > 0)
+        if here is None:
+            arrival.wait_recv()
+        else:
+            pl.when(here)(arrival.wait_recv)
+            up, down = jnp.logical_and(up, here), jnp.logical_and(down, here)
         source = self.slots.at[block]
-        self.start(block, source, 0, jnp.logical_and(block < self.plane, self.plane < self.n_tp - 1))
-        self.start(block, source, 1, jnp.logical_and(block > self.plane, self.plane > 0))
+        self.start(block, source, 0, up)
+        self.start(block, source, 1, down)
 
     def finish(self):
         for block, source, way, here in self.sent:
@@ -769,10 +781,32 @@
     loads.gate.wait()
     loads.up.wait()
     backs = []
+    def send_back(other):
+        copy = pltpu.make_async_remote_copy(
+            src_ref=r.grad_send.at[other],
+            dst_ref=r.grad_recv.at[plane],
+            send_sem=r.back_send.at[other],
+            recv_sem=r.back_recv.at[plane],
+            device_id={"tp": other},
+            device_id_type=MESH,
+        )
+        copy.start()
+        backs.append(copy)
+
+    order = work_order(plane)
+    inner = jnp.logical_and(plane > 0, plane < n_tp - 1)
+    outer = jnp.logical_not(inner)
     for k in range(n_tp):
-        other = plane if k == 0 else neighbour_order(plane, k)
-        if k > 0:
-            line.take(other)
+        other = plane if k == 0 else order[k - 1]
+        if k == 1:
+            line.take(order[2], inner)
+            line.take(order[0])
+        if k == 2:
+            line.take(order[1])
+        if k == 3:
+            line.take(order[2], outer)
+        if k > 1:
+            send_back(order[k - 2])
 
         def gate_step(at, carry, other=other):
             cols = pl.ds(pl.multiple_of(at * chunk, chunk), chunk)
@@ -799,17 +833,7 @@
             return carry
 
         lax.fori_loop(0, pieces, back_step, 0)
-        if k > 0:
-            copy = pltpu.make_async_remote_copy(
-                src_ref=r.grad_send.at[other],
-                dst_ref=r.grad_recv.at[plane],
-                send_sem=r.back_send.at[other],
-                recv_sem=r.back_recv.at[plane],
-                device_id={"tp": other},
-                device_id_type=MESH,
-            )
-            copy.start()
-            backs.append(copy)
+    send_back(order[2])
 
     def turn(source):
         for s in range(n_tp):

time: 143 us -> 135 us (0.944)
  Pallas kernels: 142 us -> 133 us
    pallas_call x1, Pallas kernels: 134 us -> 125 us  [core(): pl.pallas_call(functools.partial(core_kernel, n_seq, n_tp, (width, chans,...]
where the time goes in v6:
time: 135 us
  Pallas kernels  133 us (99%)
    pallas_call x1, Pallas kernels, core(): pl.pallas_call(functools.partial(core_kernel, n_seq, n_tp, (width, chans,...  125 us
    pallas_call x1, Pallas kernels, finish(): pl.pallas_call(functools.partial(finish_kernel, width, chans), out_shape=...  8.02 us

profile of v6, /device:TPU:0, one launch (start us, length us, event | category | flops | bytes accessed | tf_op | source)
XLA Modules:
  0.0 134.6 jit_solution(18035703278050318362)
XLA Ops:
  0.7 125.2 %layer.1 = (bf16[4,32,768]{2,1,0:T(8,128)(2,1)}, bf16[3,768,768]{2,1,0:T(8,128)(2,1)}, bf16[4,128,768]{2,1,0:T(8,128)(2,1)}, bf16[768,768]{1,0:T(8,128)(2,1)}, b...) custom-call(f32[768]{0:T(1024)} %refs_0_.1, f32[768]{0:T(1024)} %refs_1_.1, bf16[4,192,192]{2,1,0:T(8,128)(2,1)} %refs_2_.1, ...), custom_call_target="tpu_custom_call" | custom-call | tf_op jit(solution)/shard_map/layer/pallas_call | solution.py:1207
  125.9 0.0 copy-start
  125.9 8.0 %finish.1 = (f32[4,128,768]{2,1,0:T(8,128)}, f32[768]{0:T(1024)}, f32[768]{0:T(1024)}, f32[4,192,192]{2,1,0:T(8,128)}, f32[4,192,576]{2,1,0:T(8,128)}, /*index=5...) custom-call(bf16[3,768,768]{2,1,0:T(8,128)(2,1)} %get-tuple-element., ...), custom_call_target="tpu_custom_call" | custom-call | tf_op jit(solution)/shard_map/finish/pallas_call | solution.py:1296
  133.9 0.0 copy-done
  133.9 0.7 copy.39
Async XLA Ops:
  125.9 8.0 %copy-start = (bf16[4,32,768]{2,1,0:T(8,128)(2,1)S(1)}, bf16[4,32,768]{2,1,0:T(8,128)(2,1)}, u32[]{:S(2)}) copy-start(bf16[4,32,768]{2,1,0:T(8,128)(2,1)} %get-tuple-element.82) | copy-start | bytes 589828

commit v7 on v6

--- a/solution.py
+++ b/solution.py
@@ -1009,6 +1009,7 @@
         return carry
 
     lax.fori_loop(0, per, product_step, 0)
+    squares[2].start_second_back()
 
     def signal_step(at, carry):
         here = pl.ds(pl.multiple_of(at * step, step), step)
@@ -1043,7 +1044,8 @@
             seq_copies.append(copy)
     for s in range(3):
         r.grad_proj[pl.ds(pl.multiple_of(s * width + me * chans, 16), chans), :] = r.grad_signals[s, :, mine]
-    squares[2].start_second_back()
+    squares[0].start_first_back()
+    squares[1].start_first_back()
 
     total = r.resid[...] + r.glu_own[...] + from_planes(r.glu_rsem, r.glu_recv)
     r.out_rows[...] = total.astype(BF)
@@ -1100,8 +1102,6 @@
     fan = r.in_left.shape[2]
     for copy in seq_copies:
         copy.wait_recv()
-    squares[0].start_first_back()
-    squares[1].start_first_back()
     early.start_chip()
 
     in_parts = {}
@@ -1149,16 +1149,17 @@
     packed = [row[:, at * 128 : (at + 1) * 128] for row in lines for at in range(width // 128)]
     r.small_own[128:160, 128:256] = jnp.concatenate(packed + [jnp.zeros((8, 128), F32)], axis=0).astype(BF)
     small.start_core()
+    token_line.take(order[2], inner)
+    token_line.take(order[0])
     early.start_plane_back()
     small.start_chip()
-    token_line.take(neighbour_order(plane, 1))
     for late in lates:
         late.start_plane()
     small.start_plane()
     early.start_chip_back()
     for square in squares:
         square.start_core_back()
-    token_line.take(neighbour_order(plane, 2))
+    token_line.take(order[1])
     for late in lates:
         late.start_plane_back()
     small.start_plane_back()
@@ -1166,7 +1167,7 @@
         late.start_chip_back()
     small.start_chip_back()
     early.start_core_back()
-    token_line.take(neighbour_order(plane, 3))
+    token_line.take(order[2], outer)
     ffn_copies = []
     for which, square in enumerate(squares):
         square.arrived()

time: 135 us -> 130 us (0.963)
  Pallas kernels: 133 us -> 129 us
    pallas_call x1, Pallas kernels: 125 us -> 121 us  [core(): pl.pallas_call(functools.partial(core_kernel, n_seq, n_tp, (width, chans,...]
where the time goes in v7:
time: 130 us
  Pallas kernels  129 us (99%)
    pallas_call x1, Pallas kernels, core(): pl.pallas_call(functools.partial(core_kernel, n_seq, n_tp, (width, chans,...  121 us
    pallas_call x1, Pallas kernels, finish(): pl.pallas_call(functools.partial(finish_kernel, width, chans), out_shape=...  8.02 us

profile of v7, /device:TPU:0, one launch (start us, length us, event | category | flops | bytes accessed | tf_op | source)
XLA Modules:
  0.0 130.3 jit_solution(4095203640001530747)
XLA Ops:
  0.7 120.9 %layer.1 = (bf16[4,32,768]{2,1,0:T(8,128)(2,1)}, bf16[3,768,768]{2,1,0:T(8,128)(2,1)}, bf16[4,128,768]{2,1,0:T(8,128)(2,1)}, bf16[768,768]{1,0:T(8,128)(2,1)}, b...) custom-call(f32[768]{0:T(1024)} %refs_0_.1, f32[768]{0:T(1024)} %refs_1_.1, bf16[4,192,192]{2,1,0:T(8,128)(2,1)} %refs_2_.1, ...), custom_call_target="tpu_custom_call" | custom-call | tf_op jit(solution)/shard_map/layer/pallas_call | solution.py:1208
  121.5 0.0 copy-start
  121.5 8.0 %finish.1 = (f32[4,128,768]{2,1,0:T(8,128)}, f32[768]{0:T(1024)}, f32[768]{0:T(1024)}, f32[4,192,192]{2,1,0:T(8,128)}, f32[4,192,576]{2,1,0:T(8,128)}, /*index=5...) custom-call(bf16[3,768,768]{2,1,0:T(8,128)(2,1)} %get-tuple-element., ...), custom_call_target="tpu_custom_call" | custom-call | tf_op jit(solution)/shard_map/finish/pallas_call | solution.py:1297
  129.6 0.0 copy-done
  129.6 0.7 copy.39
Async XLA Ops:
  121.5 8.0 %copy-start = (bf16[4,32,768]{2,1,0:T(8,128)(2,1)S(1)}, bf16[4,32,768]{2,1,0:T(8,128)(2,1)}, u32[]{:S(2)}) copy-start(bf16[4,32,768]{2,1,0:T(8,128)(2,1)} %get-tuple-element.82) | copy-start | bytes 589828

commit v8 on v7

--- a/solution.py
+++ b/solution.py
@@ -869,6 +869,19 @@
             total = total + slots[other].astype(F32)
         return total
 
+    for k in range(n_tp):
+        other = plane if k == 0 else neighbour_order(plane, n_tp - k)
+
+        def glu_step(at, carry, k=k, other=other):
+            cols = pl.ds(pl.multiple_of(at * chunk, chunk), chunk)
+            result = dot(r.hidden[other], r.down_v[:, cols])
+            if k == 0:
+                r.glu_own[:, cols] = result
+            else:
+                r.glu_send[other, :, cols] = result.astype(BF)
+            return carry
+
+        lax.fori_loop(0, pieces, glu_step, 0)
     total = r.grad_normed[...] + from_planes(r.back_recv, r.grad_recv)
     value = r.scaled[...]
     r.grad_vectors[0:1, :] = jnp.sum(total * value, axis=0, keepdims=True)
@@ -915,30 +928,18 @@
     squares[0].start_second()
 
     glus = []
-    for k in range(n_tp):
-        other = plane if k == 0 else neighbour_order(plane, n_tp - k)
-
-        def glu_step(at, carry, k=k, other=other):
-            cols = pl.ds(pl.multiple_of(at * chunk, chunk), chunk)
-            result = dot(r.hidden[other], r.down_v[:, cols])
-            if k == 0:
-                r.glu_own[:, cols] = result
-            else:
-                r.glu_send[other, :, cols] = result.astype(BF)
-            return carry
-
-        lax.fori_loop(0, pieces, glu_step, 0)
-        if k > 0:
-            copy = pltpu.make_async_remote_copy(
-                src_ref=r.glu_send.at[other],
-                dst_ref=r.glu_recv.at[plane],
-                send_sem=r.glu_ssem.at[other],
-                recv_sem=r.glu_rsem.at[plane],
-                device_id={"tp": other},
-                device_id_type=MESH,
-            )
-            copy.start()
-            glus.append(copy)
+    for k in range(1, n_tp):
+        other = neighbour_order(plane, n_tp - k)
+        copy = pltpu.make_async_remote_copy(
+            src_ref=r.glu_send.at[other],
+            dst_ref=r.glu_recv.at[plane],
+            send_sem=r.glu_ssem.at[other],
+            recv_sem=r.glu_rsem.at[plane],
+            device_id={"tp": other},
+            device_id_type=MESH,
+        )
+        copy.start()
+        glus.append(copy)
     squares[1].start_second()
     r.sums[...] = jnp.zeros_like(r.sums)
     r.small_own[...] = jnp.zeros_like(r.small_own)

time: 130 us -> 130 us (level)
  no operation moved by 1% of the time
where the time goes in v8:
time: 130 us
  Pallas kernels  129 us (99%)
    pallas_call x1, Pallas kernels, core(): pl.pallas_call(functools.partial(core_kernel, n_seq, n_tp, (width, chans,...  121 us
    pallas_call x1, Pallas kernels, finish(): pl.pallas_call(functools.partial(finish_kernel, width, chans), out_shape=...  8.02 us

profile of v8, /device:TPU:0, one launch (start us, length us, event | category | flops | bytes accessed | tf_op | source)
XLA Modules:
  0.0 130.2 jit_solution(7124746538771375826)
XLA Ops:
  0.7 120.8 %layer.1 = (bf16[4,32,768]{2,1,0:T(8,128)(2,1)}, bf16[3,768,768]{2,1,0:T(8,128)(2,1)}, bf16[4,128,768]{2,1,0:T(8,128)(2,1)}, bf16[768,768]{1,0:T(8,128)(2,1)}, b...) custom-call(f32[768]{0:T(1024)} %refs_0_.1, f32[768]{0:T(1024)} %refs_1_.1, bf16[4,192,192]{2,1,0:T(8,128)(2,1)} %refs_2_.1, ...), custom_call_target="tpu_custom_call" | custom-call | tf_op jit(solution)/shard_map/layer/pallas_call | solution.py:1209
  121.5 0.0 copy-start
  121.5 8.0 %finish.1 = (f32[4,128,768]{2,1,0:T(8,128)}, f32[768]{0:T(1024)}, f32[768]{0:T(1024)}, f32[4,192,192]{2,1,0:T(8,128)}, f32[4,192,576]{2,1,0:T(8,128)}, /*index=5...) custom-call(bf16[3,768,768]{2,1,0:T(8,128)(2,1)} %get-tuple-element., ...), custom_call_target="tpu_custom_call" | custom-call | tf_op jit(solution)/shard_map/finish/pallas_call | solution.py:1298
  129.5 0.0 copy-done
  129.5 0.7 copy.39
Async XLA Ops:
  121.5 8.0 %copy-start = (bf16[4,32,768]{2,1,0:T(8,128)(2,1)S(1)}, bf16[4,32,768]{2,1,0:T(8,128)(2,1)}, u32[]{:S(2)}) copy-start(bf16[4,32,768]{2,1,0:T(8,128)(2,1)} %get-tuple-element.82) | copy-start | bytes 589828
